TPU v7x, 32 devices: a whole 2x2x4 slice. The times are simulated.
32 devices in a mesh: gx: 16 (over z, y, core), gy: 2 (over x).
Axes of the slice: x: 2, y: 2, z: 4, core: 2. Of those that a mesh axis runs over, the one named last changes fastest.
Arguments:
- fwd_pops: bfloat16 [3, 19, 64, 16, 128], P(None, None, 'gx', 'gy'), may hold values from -4 to 4
- fwd_scale: float32 [3, 64, 16, 128], P(None, 'gx', 'gy'), may hold values from 0.01 to 0.1
- seed_adjoint: float32 [19, 64, 16, 128], P(None, 'gx', 'gy'), may hold values from -16 to 16
- turbine_map: int32 [64, 16, 128], P('gx', 'gy'), may hold values from -1 to 9, as said below
- thrust: float32 [10], replicated, may hold values from 0.4 to 0.88
Outputs:
- adjoint_out: float32 [19, 64, 16, 128], P(None, 'gx', 'gy')
- thrust_grad: float32 [10], replicated
Inputs may be any that keep to these rules, and one draw needn't show every extreme that they name: `turbine_map`: every turbine's disk is the set of cells in one streamwise plane within 4 cells (Euclidean, spanwise distance wrapping) of its centre; disks never intersect and every turbine covers cells.
All inputs are finite; a program needn't handle non-finite values.
Results may differ from a plain program's by a relative error of at most 0.0003.
Values sent between devices are 32-bit elements; how exact they have to be, the bound alone decides.
No kernel may reach another device: no remote copies, remote signals or barrier semaphores. Data moves between devices by JAX's collectives and lax.ppermute only.
A program may use at most 64 MiB of HBM per device.

v0:
```python
import jax
import jax.numpy as jnp
from jax import lax
from jax.sharding import PartitionSpec as P

VELOCITIES = (
    (0, 0, 0),
    (1, 0, 0),
    (-1, 0, 0),
    (0, 1, 0),
    (0, -1, 0),
    (0, 0, 1),
    (0, 0, -1),
    (1, 1, 0),
    (-1, -1, 0),
    (1, -1, 0),
    (-1, 1, 0),
    (1, 0, 1),
    (-1, 0, -1),
    (1, 0, -1),
    (-1, 0, 1),
    (0, 1, 1),
    (0, -1, -1),
    (0, 1, -1),
    (0, -1, 1),
)
OPPOSITE = (0, 2, 1, 4, 3, 6, 5, 8, 7, 10, 9, 12, 11, 14, 13, 16, 15, 18, 17)
WEIGHTS = tuple([1.0 / 3.0] + [1.0 / 18.0] * 6 + [1.0 / 36.0] * 12)
MEAN_FLOW = 0.1
TAU_BASE = 0.51
SMAG_COEF = 18.0 * 1.4142135623730951 * 0.17 * 0.17
QUAD_FLOOR = 0.0001
PAIRS = ((0, 0, 1.0), (1, 1, 1.0), (2, 2, 1.0), (0, 1, 2.0), (0, 2, 2.0), (1, 2, 2.0))


def extended(block, sides, width):
    for axis, dim in sides:
        count = lax.axis_size(axis)
        forward = [(i, i + 1) for i in range(count - 1)]
        forward.append((count - 1, 0))
        backward = [(target, source) for source, target in forward]
        low = lax.ppermute(
            lax.slice_in_dim(block, block.shape[dim] - width, None, axis=dim), axis, forward
        )
        high = lax.ppermute(lax.slice_in_dim(block, 0, width, axis=dim), axis, backward)
        block = jnp.concatenate([low, block, high], axis=dim)
    return block


def base_values():
    values = []
    for member in range(19):
        along = float(VELOCITIES[member][0])
        values.append(
            WEIGHTS[member]
            * (
                1.0
                + 3.0 * MEAN_FLOW * along
                + 4.5 * MEAN_FLOW * MEAN_FLOW * along * along
                - 1.5 * MEAN_FLOW * MEAN_FLOW
            )
        )
    return values


def decode(stored, scaling):
    base = jnp.asarray(base_values(), dtype=jnp.float32)
    return base[:, None, None, None] * (1.0 + scaling[None] * stored.astype(jnp.float32))


def collide(populations, thrust_cell):
    density = populations[0]
    for member in range(1, 19):
        density = density + populations[member]
    velocity = []
    for axis_id in range(3):
        moment = jnp.zeros_like(density)
        for member in range(19):
            component = VELOCITIES[member][axis_id]
            if component != 0:
                moment = moment + float(component) * populations[member]
        velocity.append(moment / density)
    speed_sq = velocity[0] * velocity[0] + velocity[1] * velocity[1] + velocity[2] * velocity[2]
    nonequil = []
    for member in range(19):
        proj = (
            float(VELOCITIES[member][0]) * velocity[0]
            + float(VELOCITIES[member][1]) * velocity[1]
            + float(VELOCITIES[member][2]) * velocity[2]
        )
        equilib = (
            WEIGHTS[member] * density * (1.0 + 3.0 * proj + 4.5 * proj * proj - 1.5 * speed_sq)
        )
        nonequil.append(populations[member] - equilib)
    stress_sum = jnp.zeros_like(density)
    for first, second, factor in PAIRS:
        stress = jnp.zeros_like(density)
        for member in range(19):
            product = VELOCITIES[member][first] * VELOCITIES[member][second]
            if product != 0:
                stress = stress + float(product) * nonequil[member]
        stress_sum = stress_sum + factor * stress * stress
    magnitude = jnp.sqrt(stress_sum + QUAD_FLOOR)
    relaxation = 0.5 * (TAU_BASE + jnp.sqrt(TAU_BASE * TAU_BASE + SMAG_COEF * magnitude / density))
    thrust_force = -0.5 * thrust_cell * velocity[0] * jnp.abs(velocity[0])
    result = []
    for member in range(19):
        result.append(
            populations[member]
            - nonequil[member] / relaxation
            + 3.0 * WEIGHTS[member] * float(VELOCITIES[member][0]) * thrust_force
        )
    return jnp.stack(result)


def local_thrust(values):
    return 4.0 * values / jnp.square(1.0 + jnp.sqrt(1.0 - values))


def finish_vertical(shifted, adjoint):
    result = []
    for member in range(19):
        vertical = VELOCITIES[member][2]
        mirror = adjoint[OPPOSITE[member]]
        if vertical == 1:
            result.append(jnp.concatenate([shifted[member][..., 1:], mirror[..., -1:]], axis=-1))
        elif vertical == -1:
            result.append(jnp.concatenate([mirror[..., :1], shifted[member][..., :-1]], axis=-1))
        else:
            result.append(shifted[member])
    return jnp.stack(result)


def pull_whole(adjoint):
    width_x = adjoint.shape[1]
    width_y = adjoint.shape[2]
    padded = extended(adjoint, (("gx", 1), ("gy", 2)), 1)
    shifted = []
    for member in range(19):
        start_x = 1 + VELOCITIES[member][0]
        start_y = 1 + VELOCITIES[member][1]
        shifted.append(padded[member, start_x : start_x + width_x, start_y : start_y + width_y])
    return shifted


def shards(fwd_pops, fwd_scale, seed_adjoint, turbine_map, thrust):
    steps_count = fwd_pops.shape[0]
    turbines = thrust.shape[0]
    inside = turbine_map >= 0
    ids = jnp.maximum(turbine_map, 0)
    thrust_cell = jnp.where(inside, jnp.take(local_thrust(thrust), ids), 0.0)
    selector = (
        turbine_map.reshape(-1)[None, :] == jnp.arange(turbines, dtype=jnp.int32)[:, None]
    ).astype(jnp.float32)
    adjoint = seed_adjoint
    summed = jnp.zeros((turbines,), jnp.float32)
    for instant in range(steps_count - 1, -1, -1):
        shifted = pull_whole(adjoint)
        incoming = finish_vertical(shifted, adjoint)
        populations = decode(fwd_pops[instant], fwd_scale[instant])
        _, pullback = jax.vjp(collide, populations, thrust_cell)
        adjoint, cell_grad = pullback(incoming)
        partial_value = jnp.dot(selector, cell_grad.reshape(-1), precision=lax.Precision.HIGHEST)
        summed = summed + lax.psum(partial_value, ("gx", "gy"))
    _, slope = jax.vjp(local_thrust, thrust)
    thrust_grad = slope(summed)[0]
    return (adjoint, thrust_grad)


def solution(mesh):
    placed = (
        P(None, None, "gx", "gy", None),
        P(None, "gx", "gy", None),
        P(None, "gx", "gy", None),
        P("gx", "gy", None),
        P(),
    )
    return jax.shard_map(
        shards,
        mesh=mesh,
        in_specs=placed,
        out_specs=(P(None, "gx", "gy", None), P()),
        check_vma=False,
    )
```

profile of v0, /device:TPU:0, one launch (start us, length us, event | category | flops | bytes accessed | tf_op | source)
XLA Modules:
  0.0 113.3 jit_solution(9196952424378563904)
XLA Ops:
  0.6 1.0 fusion.1098
  1.6 0.5 collective-permute-start
  2.1 5.1 %collective-permute-start.1 = (f32[19,1,8,128]{3,2,1,0:T(8,128)S(1)}, f32[19,1,8,128]{3,2,1,0:T(8,128)S(1)}, u32[]{:S(2)}, u32[]{:S(2)}) collective-permute-start(f32[19,1,8,128]{3,2,1,0:T(8,128)S(1)} %get-tuple-element.325), channel_id=1, source_target_pairs={{2,0},{4,2},{6,4},{8,6},{10,8},{12,10},{14,12},{16,14},{18,16},{20... | collective-permute-start | bytes 233480 | tf_op jit(solution)/shard_map/ppermute | solution.py:45
  7.2 0.1 slice_bitcast_fusion.77
  7.4 0.6 copy-done.2
  8.0 0.1 copy-done.3
  8.4 0.7 copy-done.5
  9.1 0.1 fusion.7
  9.2 0.5 copy-done.6
  9.7 24.7 %gather_fusion = f32[4096]{0:T(1024)S(1)} fusion(f32[10]{0:T(128)S(1)} %multiply_divide_fusion, s32[4096]{0:T(1024)S(1)} %bitcast_clamp_fusion), kind=kCustom, calls=%fused_computation | custom fusion | bytes 49152 | tf_op jit(solution)/shard_map/jit(_take)/gather | solution.py:151
  34.7 1.9 %collective-permute-start.3 = (f32[19,6,1,128]{3,2,1,0:T(1,128)S(1)}, f32[19,6,1,128]{3,2,1,0:T(1,128)S(1)}, u32[]{:S(2)}, u32[]{:S(2)}) collective-permute-start(f32[19,6,1,128]{3,2,1,0:T(1,128)S(1)} %get-tuple-element.261), channel_id=1, source_target_pairs={{1,0},{0,1},{3,2},{2,3},{5,4},{4,5},{7,6},{6,7},{9,8},{8,9},{11,10... | collective-permute-start | bytes 175112 | tf_op jit(solution)/shard_map/ppermute | solution.py:45
  36.6 0.2 collective-permute-start.2
  36.9 2.0 %collective-permute-done.3 = f32[19,6,1,128]{3,2,1,0:T(1,128)S(1)} collective-permute-done((f32[19,6,1,128]{3,2,1,0:T(1,128)S(1)}, f32[19,6,1,128]{3,2,1,0:T(1,128)S(1)}, u32[]{:S(2)}, u32[]{:S(2)}) %collective-permute-start.3) | collective-permute-done | bytes 58400 | tf_op jit(solution)/shard_map/ppermute | solution.py:45
  38.9 1.9 %collective-permute-done.2 = f32[19,6,1,128]{3,2,1,0:T(1,128)S(1)} collective-permute-done((f32[19,6,1,128]{3,2,1,0:T(1,128)S(1)}, f32[19,6,1,128]{3,2,1,0:T(1,128)S(1)}, u32[]{:S(2)}, u32[]{:S(2)}) %collective-permute-start.2) | collective-permute-done | bytes 58400 | tf_op jit(solution)/shard_map/ppermute | solution.py:42
  40.8 0.1 slice_bitcast_fusion.90
  41.0 0.1 fusion.755
  41.1 0.3 fusion.127
  41.5 0.4 broadcast_multiply_fusion.11
  42.0 0.3 divide_multiply_fusion.4
  42.3 0.3 multiply_bitcast_fusion.2
  42.6 0.5 fusion.670
  43.1 0.2 broadcast_multiply_fusion.10
  43.3 0.6 copy-done.4
  44.0 0.1 pad_add_fusion.2
  44.2 4.4 %collective-permute-start.5 = (f32[19,1,8,128]{3,2,1,0:T(8,128)S(1)}, f32[19,1,8,128]{3,2,1,0:T(8,128)S(1)}, u32[]{:S(2)}, u32[]{:S(2)}) collective-permute-start(f32[19,1,8,128]{3,2,1,0:T(8,128)S(1)} %get-tuple-element.310), channel_id=1, source_target_pairs={{2,0},{4,2},{6,4},{8,6},{10,8},{12,10},{14,12},{16,14},{18,16},{20... | collective-permute-start | bytes 233480 | tf_op jit(solution)/shard_map/ppermute | solution.py:45
  48.6 0.3 convolution_bitcast_fusion.2
  48.9 1.8 %collective-permute-done.4 = f32[19,1,8,128]{3,2,1,0:T(8,128)S(1)} collective-permute-done((f32[19,1,8,128]{3,2,1,0:T(8,128)S(1)}, f32[19,1,8,128]{3,2,1,0:T(8,128)S(1)}, u32[]{:S(2)}, u32[]{:S(2)}) %collective-permute-start.4) | collective-permute-done | bytes 77856 | tf_op jit(solution)/shard_map/ppermute | solution.py:42
  50.7 0.1 slice_bitcast_fusion.58
  50.9 0.1 pad_maximum_fusion.3
  51.0 0.7 collective-permute-start.7
  51.6 1.4 %collective-permute-start.6 = (f32[19,6,1,128]{3,2,1,0:T(1,128)S(1)}, f32[19,6,1,128]{3,2,1,0:T(1,128)S(1)}, u32[]{:S(2)}, u32[]{:S(2)}) collective-permute-start(f32[19,6,1,128]{3,2,1,0:T(1,128)S(1)} %get-tuple-element.258), channel_id=1, source_target_pairs={{0,1},{1,0},{2,3},{3,2},{4,5},{5,4},{6,7},{7,6},{8,9},{9,8},{10,11... | collective-permute-start | bytes 175112 | tf_op jit(solution)/shard_map/ppermute | solution.py:42
  53.3 0.1 slice_bitcast_fusion.67
  53.5 1.7 %collective-permute-done.7 = f32[19,6,1,128]{3,2,1,0:T(1,128)S(1)} collective-permute-done((f32[19,6,1,128]{3,2,1,0:T(1,128)S(1)}, f32[19,6,1,128]{3,2,1,0:T(1,128)S(1)}, u32[]{:S(2)}, u32[]{:S(2)}) %collective-permute-start.7) | collective-permute-done | bytes 58400 | tf_op jit(solution)/shard_map/ppermute | solution.py:45
  55.2 0.6 collective-permute-done.6
  55.9 0.1 slice_bitcast_fusion.70
  56.0 0.1 fusion.737
  56.1 0.3 add_add_fusion.54
  56.5 0.1 fusion.345
  56.6 0.3 broadcast_multiply_fusion.13
  56.9 0.3 divide_multiply_fusion.2
  57.3 0.3 multiply_bitcast_fusion.1
  57.6 0.5 fusion.682
  58.1 0.2 broadcast_multiply_fusion.12
  58.3 0.5 pad_add_fusion.1
  58.9 4.4 %collective-permute-start.9 = (f32[19,1,8,128]{3,2,1,0:T(8,128)S(1)}, f32[19,1,8,128]{3,2,1,0:T(8,128)S(1)}, u32[]{:S(2)}, u32[]{:S(2)}) collective-permute-start(f32[19,1,8,128]{3,2,1,0:T(8,128)S(1)} %get-tuple-element.296), channel_id=1, source_target_pairs={{2,0},{4,2},{6,4},{8,6},{10,8},{12,10},{14,12},{16,14},{18,16},{20... | collective-permute-start | bytes 233480 | tf_op jit(solution)/shard_map/ppermute | solution.py:45
  63.3 0.3 fusion.1
  63.6 1.8 %collective-permute-done.8 = f32[19,1,8,128]{3,2,1,0:T(8,128)S(1)} collective-permute-done((f32[19,1,8,128]{3,2,1,0:T(8,128)S(1)}, f32[19,1,8,128]{3,2,1,0:T(8,128)S(1)}, u32[]{:S(2)}, u32[]{:S(2)}) %collective-permute-start.8) | collective-permute-done | bytes 77856 | tf_op jit(solution)/shard_map/ppermute | solution.py:42
  65.6 0.1 pad_maximum_fusion
  65.7 1.5 %collective-permute-start.11 = (f32[19,6,1,128]{3,2,1,0:T(1,128)S(1)}, f32[19,6,1,128]{3,2,1,0:T(1,128)S(1)}, u32[]{:S(2)}, u32[]{:S(2)}) collective-permute-start(f32[19,6,1,128]{3,2,1,0:T(1,128)S(1)} %get-tuple-element.253), channel_id=1, source_target_pairs={{1,0},{0,1},{3,2},{2,3},{5,4},{4,5},{7,6},{6,7},{9,8},{8,9},{11,10... | collective-permute-start | bytes 175112 | tf_op jit(solution)/shard_map/ppermute | solution.py:45
  67.1 0.6 collective-permute-start.10
  68.2 1.7 %collective-permute-done.11 = f32[19,6,1,128]{3,2,1,0:T(1,128)S(1)} collective-permute-done((f32[19,6,1,128]{3,2,1,0:T(1,128)S(1)}, f32[19,6,1,128]{3,2,1,0:T(1,128)S(1)}, u32[]{:S(2)}, u32[]{:S(2)}) %collective-permute-start.11) | collective-permute-done | bytes 58400 | tf_op jit(solution)/shard_map/ppermute | solution.py:45
  69.9 1.4 %collective-permute-done.10 = f32[19,6,1,128]{3,2,1,0:T(1,128)S(1)} collective-permute-done((f32[19,6,1,128]{3,2,1,0:T(1,128)S(1)}, f32[19,6,1,128]{3,2,1,0:T(1,128)S(1)}, u32[]{:S(2)}, u32[]{:S(2)}) %collective-permute-start.10) | collective-permute-done | bytes 58400 | tf_op jit(solution)/shard_map/ppermute | solution.py:42
  71.5 0.1 fusion.719
  71.6 0.3 fusion
  71.9 37.3 %psum.25 = f32[10]{0:T(128)S(1)} all-reduce(f32[10]{0:T(128)S(1)} %fusion), channel_id=1, replica_groups=mesh['gx'=16,'gy'=2] {'gx','gy'}, use_global_device_ids=true, to_apply=%region_0.1 | all-reduce | flops 10 | bytes 80 | tf_op jit(solution)/shard_map/psum | solution.py:164
  109.2 0.5 multiply_add_fusion.114
  109.7 0.3 add_add_fusion.26
  110.1 0.1 fusion.562
  110.2 0.3 broadcast_multiply_fusion.9
  110.5 0.3 divide_multiply_fusion
  110.9 0.3 multiply_bitcast_fusion
  111.1 0.5 fusion.694
  111.7 0.2 broadcast_multiply_fusion.14
  111.9 1.4 %pad_add_fusion = f32[19,4,8,128]{3,2,1,0:T(8,128)} fusion(f32[1,4,8,128]{3,2,1,0:T(8,128)S(1)} %fusion.694, f32[1,4,8,128]{3,2,1,0:T(8,128)S(1)} %bitcast.3262, f32[1,4,8,128]{3,2,1,0:T(8,128)S(1)} %get-tuple-element.93, f32[1,4,8,128]{3,2,1,0:T(8,128)S(1)} %get-tuple-element.92, f32[1,4,8,128]{3,2,1,0:T(8,128)S(1)} %get-tuple-element.91, ...), kind=kLoop, calls=%fused_computation.15 | loop fusion | flops 20312064 | bytes 2785299 | tf_op jit(solution)/shard_map/transpose(jvp())/add_any | solution.py:72
  (82 shorter events, 2.5 us)
Async XLA Ops:
  0.6 6.6 %copy-start = (f32[19,4,8,128]{3,2,1,0:T(8,128)S(1)}, f32[19,4,8,128]{3,2,1,0:T(8,128)}, u32[]{:S(2)}) copy-start(f32[19,4,8,128]{3,2,1,0:T(8,128)} %param.10) | copy-start | bytes 933892
  1.6 32.8 %collective-permute-start = (f32[19,1,8,128]{3,2,1,0:T(8,128)S(1)}, f32[19,1,8,128]{3,2,1,0:T(8,128)S(1)}, u32[]{:S(2)}, u32[]{:S(2)}) collective-permute-start(f32[19,1,8,128]{3,2,1,0:T(8,128)S(1)} %get-tuple-element.324), channel_id=1, source_target_pairs={{0,2},{2,4},{4,6},{6,8},{8,10},{10,12},{12,14},{14,16},{16,18},{18... | collective-permute-start | bytes 233480 | tf_op jit(solution)/shard_map/ppermute | solution.py:42
  2.1 6.3 %copy-start.1 = (bf16[3,19,4,8,128]{4,3,2,1,0:T(8,128)(2,1)S(1)}, bf16[3,19,4,8,128]{4,3,2,1,0:T(8,128)(2,1)}, u32[]{:S(2)}) copy-start(bf16[3,19,4,8,128]{4,3,2,1,0:T(8,128)(2,1)} %param.8) | copy-start | bytes 1400836
  2.1 32.4 %collective-permute-start.1 = (f32[19,1,8,128]{3,2,1,0:T(8,128)S(1)}, f32[19,1,8,128]{3,2,1,0:T(8,128)S(1)}, u32[]{:S(2)}, u32[]{:S(2)}) collective-permute-start(f32[19,1,8,128]{3,2,1,0:T(8,128)S(1)} %get-tuple-element.325), channel_id=1, source_target_pairs={{2,0},{4,2},{6,4},{8,6},{10,8},{12,10},{14,12},{16,14},{18,16},{20... | collective-permute-start | bytes 233480 | tf_op jit(solution)/shard_map/ppermute | solution.py:45
  7.3 0.7 copy-start.2
  7.3 0.8 copy-start.3
  8.4 0.7 copy-start.5
  9.1 0.7 copy-start.6
  34.7 4.3 %collective-permute-start.3 = (f32[19,6,1,128]{3,2,1,0:T(1,128)S(1)}, f32[19,6,1,128]{3,2,1,0:T(1,128)S(1)}, u32[]{:S(2)}, u32[]{:S(2)}) collective-permute-start(f32[19,6,1,128]{3,2,1,0:T(1,128)S(1)} %get-tuple-element.261), channel_id=1, source_target_pairs={{1,0},{0,1},{3,2},{2,3},{5,4},{4,5},{7,6},{6,7},{9,8},{8,9},{11,10... | collective-permute-start | bytes 175112 | tf_op jit(solution)/shard_map/ppermute | solution.py:45
  36.6 4.2 %collective-permute-start.2 = (f32[19,6,1,128]{3,2,1,0:T(1,128)S(1)}, f32[19,6,1,128]{3,2,1,0:T(1,128)S(1)}, u32[]{:S(2)}, u32[]{:S(2)}) collective-permute-start(f32[19,6,1,128]{3,2,1,0:T(1,128)S(1)} %get-tuple-element.262), channel_id=1, source_target_pairs={{0,1},{1,0},{2,3},{3,2},{4,5},{5,4},{6,7},{7,6},{8,9},{9,8},{10,11... | collective-permute-start | bytes 175112 | tf_op jit(solution)/shard_map/ppermute | solution.py:42
  43.3 0.7 copy-start.4
  44.1 6.6 %collective-permute-start.4 = (f32[19,1,8,128]{3,2,1,0:T(8,128)S(1)}, f32[19,1,8,128]{3,2,1,0:T(8,128)S(1)}, u32[]{:S(2)}, u32[]{:S(2)}) collective-permute-start(f32[19,1,8,128]{3,2,1,0:T(8,128)S(1)} %get-tuple-element.309), channel_id=1, source_target_pairs={{0,2},{2,4},{4,6},{6,8},{8,10},{10,12},{12,14},{14,16},{16,18},{18... | collective-permute-start | bytes 233480 | tf_op jit(solution)/shard_map/ppermute | solution.py:42
  44.2 6.5 %collective-permute-start.5 = (f32[19,1,8,128]{3,2,1,0:T(8,128)S(1)}, f32[19,1,8,128]{3,2,1,0:T(8,128)S(1)}, u32[]{:S(2)}, u32[]{:S(2)}) collective-permute-start(f32[19,1,8,128]{3,2,1,0:T(8,128)S(1)} %get-tuple-element.310), channel_id=1, source_target_pairs={{2,0},{4,2},{6,4},{8,6},{10,8},{12,10},{14,12},{16,14},{18,16},{20... | collective-permute-start | bytes 233480 | tf_op jit(solution)/shard_map/ppermute | solution.py:45
  51.0 4.3 %collective-permute-start.7 = (f32[19,6,1,128]{3,2,1,0:T(1,128)S(1)}, f32[19,6,1,128]{3,2,1,0:T(1,128)S(1)}, u32[]{:S(2)}, u32[]{:S(2)}) collective-permute-start(f32[19,6,1,128]{3,2,1,0:T(1,128)S(1)} %get-tuple-element.257), channel_id=1, source_target_pairs={{1,0},{0,1},{3,2},{2,3},{5,4},{4,5},{7,6},{6,7},{9,8},{8,9},{11,10... | collective-permute-start | bytes 175112 | tf_op jit(solution)/shard_map/ppermute | solution.py:45
  51.6 4.2 %collective-permute-start.6 = (f32[19,6,1,128]{3,2,1,0:T(1,128)S(1)}, f32[19,6,1,128]{3,2,1,0:T(1,128)S(1)}, u32[]{:S(2)}, u32[]{:S(2)}) collective-permute-start(f32[19,6,1,128]{3,2,1,0:T(1,128)S(1)} %get-tuple-element.258), channel_id=1, source_target_pairs={{0,1},{1,0},{2,3},{3,2},{4,5},{5,4},{6,7},{7,6},{8,9},{9,8},{10,11... | collective-permute-start | bytes 175112 | tf_op jit(solution)/shard_map/ppermute | solution.py:42
  58.8 6.6 %collective-permute-start.8 = (f32[19,1,8,128]{3,2,1,0:T(8,128)S(1)}, f32[19,1,8,128]{3,2,1,0:T(8,128)S(1)}, u32[]{:S(2)}, u32[]{:S(2)}) collective-permute-start(f32[19,1,8,128]{3,2,1,0:T(8,128)S(1)} %get-tuple-element.295), channel_id=1, source_target_pairs={{0,2},{2,4},{4,6},{6,8},{8,10},{10,12},{12,14},{14,16},{16,18},{18... | collective-permute-start | bytes 233480 | tf_op jit(solution)/shard_map/ppermute | solution.py:42
  58.9 6.5 %collective-permute-start.9 = (f32[19,1,8,128]{3,2,1,0:T(8,128)S(1)}, f32[19,1,8,128]{3,2,1,0:T(8,128)S(1)}, u32[]{:S(2)}, u32[]{:S(2)}) collective-permute-start(f32[19,1,8,128]{3,2,1,0:T(8,128)S(1)} %get-tuple-element.296), channel_id=1, source_target_pairs={{2,0},{4,2},{6,4},{8,6},{10,8},{12,10},{14,12},{16,14},{18,16},{20... | collective-permute-start | bytes 233480 | tf_op jit(solution)/shard_map/ppermute | solution.py:45
  65.7 4.3 %collective-permute-start.11 = (f32[19,6,1,128]{3,2,1,0:T(1,128)S(1)}, f32[19,6,1,128]{3,2,1,0:T(1,128)S(1)}, u32[]{:S(2)}, u32[]{:S(2)}) collective-permute-start(f32[19,6,1,128]{3,2,1,0:T(1,128)S(1)} %get-tuple-element.253), channel_id=1, source_target_pairs={{1,0},{0,1},{3,2},{2,3},{5,4},{4,5},{7,6},{6,7},{9,8},{8,9},{11,10... | collective-permute-start | bytes 175112 | tf_op jit(solution)/shard_map/ppermute | solution.py:45
  67.1 4.2 %collective-permute-start.10 = (f32[19,6,1,128]{3,2,1,0:T(1,128)S(1)}, f32[19,6,1,128]{3,2,1,0:T(1,128)S(1)}, u32[]{:S(2)}, u32[]{:S(2)}) collective-permute-start(f32[19,6,1,128]{3,2,1,0:T(1,128)S(1)} %get-tuple-element.254), channel_id=1, source_target_pairs={{0,1},{1,0},{2,3},{3,2},{4,5},{5,4},{6,7},{7,6},{8,9},{9,8},{10,11... | collective-permute-start | bytes 175112 | tf_op jit(solution)/shard_map/ppermute | solution.py:42
where the time goes:
time: 114 us; the launch traced here: 113 us
  blocking collectives  37.3 us (33%)
  local copies, waits for them, and re-layouts  30.7 us (27%)
  starting transfers between devices  20.8 us (18%)
  waiting for transfers between devices  12.9 us (11%)
  other arithmetic  9.76 us (9%)
    psum x1, blocking collectives, shards(): summed = summed + lax.psum(partial_value, ('gx', 'gy'))  37.3 us
    gather x1, local copies, waits for them, and re-layouts, shards(): thrust_cell = jnp.where(inside, jnp.take(local_thrust(thrust), ids), 0.0)  24.7 us
    ppermute x6, starting transfers between devices, extended(): lax.ppermute(lax.slice_in_dim(block, 0, width, axis=dim), axis, backward)  18 us
    ppermute x6, waiting for transfers between devices, extended(): lax.ppermute(lax.slice_in_dim(block, block.shape[dim] - width, None, axis...  7.52 us
    ppermute x6, waiting for transfers between devices, extended(): lax.ppermute(lax.slice_in_dim(block, 0, width, axis=dim), axis, backward)  5.4 us
    ppermute x6, starting transfers between devices, extended(): lax.ppermute(lax.slice_in_dim(block, block.shape[dim] - width, None, axis...  2.81 us
    unnamed x16, local copies, waits for them, and re-layouts  2.63 us
  transfers between devices with their start and end apart: 12, of which 8 were waited for; matrix products, arithmetic and copies ran while one was open for 24% of the time, Pallas kernels for 0%

commit v1 on v0

v1 whole, which is shorter than its diff:
```python
import jax
import jax.numpy as jnp
from jax import lax
from jax.experimental import pallas as pl
from jax.experimental.pallas import tpu as pltpu
from jax.sharding import PartitionSpec as P

VELOCITIES = (
    (0, 0, 0),
    (1, 0, 0),
    (-1, 0, 0),
    (0, 1, 0),
    (0, -1, 0),
    (0, 0, 1),
    (0, 0, -1),
    (1, 1, 0),
    (-1, -1, 0),
    (1, -1, 0),
    (-1, 1, 0),
    (1, 0, 1),
    (-1, 0, -1),
    (1, 0, -1),
    (-1, 0, 1),
    (0, 1, 1),
    (0, -1, -1),
    (0, 1, -1),
    (0, -1, 1),
)
OPPOSITE = (0, 2, 1, 4, 3, 6, 5, 8, 7, 10, 9, 12, 11, 14, 13, 16, 15, 18, 17)
WEIGHTS = tuple([1.0 / 3.0] + [1.0 / 18.0] * 6 + [1.0 / 36.0] * 12)
MEAN_FLOW = 0.1
TAU_BASE = 0.51
SMAG_COEF = 18.0 * 1.4142135623730951 * 0.17 * 0.17
QUAD_FLOOR = 0.0001

X_UP = (1, 7, 9, 11, 13)
X_DOWN = (2, 8, 10, 12, 14)
Y_UP = (3, 7, 10, 15, 17)
Y_DOWN = (4, 8, 9, 16, 18)

KEEP, MASS, FLUX, UX, UY, UZ, Q1 = 19, 20, 21, 22, 23, 24, 25
RATE, BULK, PX, PY, PZ, DRAG, DRAG_U, GAIN = 34, 35, 36, 37, 38, 39, 40, 41
COEFS = 42

VMEM = pltpu.VMEM


def base_values():
    values = []
    for member in range(19):
        along = float(VELOCITIES[member][0])
        values.append(
            WEIGHTS[member]
            * (
                1.0
                + 3.0 * MEAN_FLOW * along
                + 4.5 * MEAN_FLOW * MEAN_FLOW * along * along
                - 1.5 * MEAN_FLOW * MEAN_FLOW
            )
        )
    return values


def plane_coefs(pops, thrust_cell, slope_cell):
    rho = pops[0]
    for member in range(1, 19):
        rho = rho + pops[member]
    inv_rho = 1.0 / rho
    vel = []
    for axis_id in range(3):
        moment = None
        for member in range(19):
            component = VELOCITIES[member][axis_id]
            if component == 1:
                moment = pops[member] if moment is None else moment + pops[member]
            elif component == -1:
                moment = moment - pops[member]
        vel.append(moment * inv_rho)
    ux, uy, uz = vel
    speed_sq = ux * ux + uy * uy + uz * uz
    rest = 1.0 - 1.5 * speed_sq
    part = []
    for member in range(19):
        if member == 0:
            part.append(pops[0] - (WEIGHTS[0] * rho) * rest)
            continue
        proj = None
        for axis_id in range(3):
            component = VELOCITIES[member][axis_id]
            if component == 1:
                proj = vel[axis_id] if proj is None else proj + vel[axis_id]
            elif component == -1:
                proj = -vel[axis_id] if proj is None else proj - vel[axis_id]
        part.append(pops[member] - (WEIGHTS[member] * rho) * (rest + 3.0 * proj + 4.5 * proj * proj))

    def pair(member):
        return part[member] + part[member + 1]

    in_xy, in_xz, in_yz = pair(7) + pair(9), pair(11) + pair(13), pair(15) + pair(17)
    pxx, pyy, pzz = pair(1) + in_xy + in_xz, pair(3) + in_xy + in_yz, pair(5) + in_xz + in_yz
    pxy, pxz, pyz = pair(7) - pair(9), pair(11) - pair(13), pair(15) - pair(17)
    square = (
        pxx * pxx + pyy * pyy + pzz * pzz + 2.0 * (pxy * pxy + pxz * pxz + pyz * pyz) + QUAD_FLOOR
    )
    size = jnp.sqrt(square)
    root = jnp.sqrt(TAU_BASE * TAU_BASE + SMAG_COEF * size * inv_rho)
    omega = 1.0 / (0.5 * (TAU_BASE + root))
    pux = pxx * ux + pxy * uy + pxz * uz
    puy = pxy * ux + pyy * uy + pyz * uz
    puz = pxz * ux + pyz * uy + pzz * uz
    flux = omega * (3.0 / 36.0)
    drag = (3.0 / 36.0) * thrust_cell * jnp.abs(ux) * inv_rho
    result = list(part)
    result.append(1.0 - omega)
    result.append((omega * (1.0 / 36.0)) * (1.0 + 1.5 * speed_sq))
    result.append(flux)
    result.extend(vel)
    result.extend((pxx, pyy, pzz))
    result.extend((pxx + pyy + 2.0 * pxy, pxx + pyy - 2.0 * pxy))
    result.extend((pxx + pzz + 2.0 * pxz, pxx + pzz - 2.0 * pxz))
    result.extend((pyy + pzz + 2.0 * pyz, pyy + pzz - 2.0 * pyz))
    result.append((0.25 * SMAG_COEF) * omega * omega * inv_rho / (root * size))
    result.append(
        (pux * ux + puy * uy + puz * uz) - (pxx + pyy + pzz) * (1.0 / 3.0) - square * inv_rho
    )
    result.extend((-2.0 * pux, -2.0 * puy, -2.0 * puz))
    result.append(drag)
    result.append(drag * ux)
    result.append((-1.5 / 36.0) * ux * jnp.abs(ux) * slope_cell)
    return result


def plane_adjoint(mu, coef):
    total, diff = {}, {}
    for member in range(1, 19, 2):
        total[member] = mu[member] + mu[member + 1]
        diff[member] = mu[member] - mu[member + 1]
    two_x, two_y, two_z = 2.0 * total[1], 2.0 * total[3], 2.0 * total[5]
    in_xy, in_xz, in_yz = total[7] + total[9], total[11] + total[13], total[15] + total[17]
    mxx, myy, mzz = two_x + in_xy + in_xz, two_y + in_xy + in_yz, two_z + in_xz + in_yz
    mxy, mxz, myz = total[7] - total[9], total[11] - total[13], total[15] - total[17]
    m0 = 12.0 * mu[0] + (two_x + two_y + two_z) + (in_xy + in_xz + in_yz)
    mx = 2.0 * diff[1] + (diff[7] + diff[9]) + (diff[11] + diff[13])
    my = 2.0 * diff[3] + (diff[7] - diff[9]) + (diff[15] + diff[17])
    mz = 2.0 * diff[5] + (diff[11] - diff[13]) + (diff[15] - diff[17])
    ux, uy, uz = coef(UX), coef(UY), coef(UZ)
    vx = mxx * ux + mxy * uy + mxz * uz
    vy = mxy * ux + myy * uy + myz * uz
    vz = mxz * ux + myz * uy + mzz * uz
    along = [mu[member] * coef(member) for member in range(19)]
    while len(along) > 1:
        along = [
            along[k] + along[k + 1] if k + 1 < len(along) else along[k]
            for k in range(0, len(along), 2)
        ]
    gamma = along[0] * coef(RATE)
    flux = coef(FLUX)
    alpha = (
        coef(MASS) * m0
        - 1.5 * flux * (vx * ux + vy * uy + vz * uz)
        + gamma * coef(BULK)
        + mx * coef(DRAG_U)
    )
    beta_x = flux * (mx + 3.0 * vx - ux * m0) + gamma * coef(PX) - mx * coef(DRAG)
    beta_y = flux * (my + 3.0 * vy - uy * m0) + gamma * coef(PY)
    beta_z = flux * (mz + 3.0 * vz - uz * m0) + gamma * coef(PZ)
    keep = coef(KEEP)
    odd = {
        1: beta_x,
        3: beta_y,
        5: beta_z,
        7: beta_x + beta_y,
        9: beta_x - beta_y,
        11: beta_x + beta_z,
        13: beta_x - beta_z,
        15: beta_y + beta_z,
        17: beta_y - beta_z,
    }
    result = [keep * mu[0] + alpha]
    for member in range(1, 19, 2):
        even = alpha + gamma * coef(Q1 + member // 2)
        result.append(keep * mu[member] + (even + odd[member]))
        result.append(keep * mu[member + 1] + (even - odd[member]))
    return result, mx


def coef_kernel(thrust_ref, map_ref, scale_ref, pops_ref, *out_refs):
    steps, width = pops_ref.shape[0], pops_ref.shape[2]
    base = base_values()
    for plane in range(width):
        ids = map_ref[plane]
        ratio = jnp.zeros(ids.shape, jnp.float32)
        for turbine in range(thrust_ref.shape[0]):
            ratio = jnp.where(ids == turbine, thrust_ref[turbine], ratio)
        root = jnp.sqrt(1.0 - ratio)
        square = (1.0 + root) * (1.0 + root)
        inside = ids >= 0
        thrust_cell = jnp.where(inside, 4.0 * ratio / square, 0.0)
        slope_cell = jnp.where(inside, 4.0 / (root * square), 0.0)
        for instant in range(steps):
            scale = scale_ref[instant, plane]
            pops = [
                base[member] * (1.0 + scale * pops_ref[instant, member, plane].astype(jnp.float32))
                for member in range(19)
            ]
            for index, value in enumerate(plane_coefs(pops, thrust_cell, slope_cell)):
                out_refs[instant][index, plane] = value


def write_rows(lam_ref, gain_ref, map_ref, rows_ref):
    width, span = lam_ref.shape[1], lam_ref.shape[2]
    for side, (members, row) in enumerate(((Y_UP, 0), (Y_DOWN, span - 1))):
        for index, member in enumerate(members):
            rows_ref[side, index * width : (index + 1) * width, :] = lam_ref[member, :, row, :]
        if gain_ref is not None:
            start = 5 * width
            rows_ref[side, start : start + width, :] = gain_ref[GAIN, :, row, :]
            rows_ref[side, start + width : start + 2 * width, :] = map_ref[:, row, :].astype(
                jnp.float32
            )


def rows_kernel(lam_ref, rows_ref):
    write_rows(lam_ref, None, None, rows_ref)


def span_shift(value, move, row):
    span = value.shape[0]
    place = lax.broadcasted_iota(jnp.int32, value.shape, 0)
    if move == 1:
        return jnp.where(place == span - 1, row, pltpu.roll(value, span - 1, 0))
    return jnp.where(place == 0, row, pltpu.roll(value, 1, 0))


def moved(lam_ref, rows_ref, member, plane):
    move = VELOCITIES[member][1]
    value = lam_ref[member, plane]
    if move == 0:
        return value
    width = lam_ref.shape[1]
    side, members = (0, Y_UP) if move == 1 else (1, Y_DOWN)
    place = members.index(member) * width + plane
    return span_shift(value, move, rows_ref[side, place : place + 1, :])


def faces_kernel(has_gain, *refs):
    if has_gain:
        lam_ref, rows_ref, coef_ref, map_ref, low_ref, high_ref = refs
    else:
        lam_ref, rows_ref, low_ref, high_ref = refs
    width = lam_ref.shape[1]
    for members, plane, out_ref in ((X_UP, 0, low_ref), (X_DOWN, width - 1, high_ref)):
        for index, member in enumerate(members):
            out_ref[index] = moved(lam_ref, rows_ref, member, plane)
        if has_gain:
            out_ref[5] = coef_ref[GAIN, plane]
            out_ref[6] = map_ref[plane].astype(jnp.float32)
            out_ref[7] = jnp.zeros(out_ref.shape[1:], jnp.float32)
            for side in range(2):
                for field in range(2):
                    place = (5 + field) * width + plane
                    out_ref[7, 2 * field + side : 2 * field + side + 1, :] = rows_ref[
                        side, place : place + 1, :
                    ]


def step_kernel(kind, turbines, *refs):
    lam_ref, rows_ref, above_ref, below_ref, coef_ref = refs[:5]
    width, span, height = lam_ref.shape[1:]
    if kind == 0:
        next_ref, map_ref, out_ref, next_rows_ref, cell_ref = refs[5:]
    elif kind == 1:
        next_ref, map_ref, cell_ref, out_ref, next_rows_ref, sums_ref, pad_ref = refs[5:]
    else:
        (out_ref,) = refs[5:]
    lane = lax.broadcasted_iota(jnp.int32, (span, height), 1)
    first, last = lane == 0, lane == height - 1
    totals = []
    for plane in range(width):
        mu = []
        for member in range(19):
            move_x, _, move_z = VELOCITIES[member]
            source = plane + move_x
            if source < 0:
                value = below_ref[X_DOWN.index(member)]
            elif source >= width:
                value = above_ref[X_UP.index(member)]
            else:
                value = moved(lam_ref, rows_ref, member, source)
            if move_z == 1:
                value = jnp.where(
                    last, lam_ref[OPPOSITE[member], plane], pltpu.roll(value, height - 1, 1)
                )
            elif move_z == -1:
                value = jnp.where(first, lam_ref[OPPOSITE[member], plane], pltpu.roll(value, 1, 1))
            mu.append(value)
        lam, mx = plane_adjoint(mu, lambda index: coef_ref[index, plane])
        for member in range(19):
            out_ref[member, plane] = lam[member]
        if kind == 0:
            cell_ref[plane] = mx * coef_ref[GAIN, plane]
        elif kind == 1:
            totals.append(cell_ref[plane] + mx * coef_ref[GAIN, plane])
    if kind < 2:
        write_rows(
            out_ref, next_ref if kind == 0 else None, map_ref if kind == 0 else None, next_rows_ref
        )
    if kind == 1:
        sum_turbines(
            turbines,
            out_ref,
            next_ref,
            map_ref,
            rows_ref,
            above_ref,
            below_ref,
            totals,
            sums_ref,
            pad_ref,
            first,
            last,
        )


def sum_turbines(
    turbines,
    lam_ref,
    coef_ref,
    map_ref,
    rows_ref,
    above_ref,
    below_ref,
    totals,
    sums_ref,
    pad_ref,
    first,
    last,
):
    width, span, height = lam_ref.shape[1:]

    def roll_z(value, move):
        if move == 1:
            return jnp.where(last, 0.0, pltpu.roll(value, height - 1, 1))
        return jnp.where(first, 0.0, pltpu.roll(value, 1, 1))

    nothing = jnp.zeros((1, height), jnp.float32)
    up, down = [], []
    for plane in range(width):
        up.append(
            2.0 * lam_ref[1, plane]
            + span_shift(lam_ref[7, plane], 1, nothing)
            + span_shift(lam_ref[9, plane], -1, nothing)
            + roll_z(lam_ref[11, plane], 1)
            + roll_z(lam_ref[13, plane], -1)
        )
        down.append(
            2.0 * lam_ref[2, plane]
            + span_shift(lam_ref[8, plane], -1, nothing)
            + span_shift(lam_ref[10, plane], 1, nothing)
            + roll_z(lam_ref[12, plane], -1)
            + roll_z(lam_ref[14, plane], 1)
        )
    tiles = []
    for plane in range(-1, width + 1):
        value = None
        if plane + 1 < width:
            value = up[plane + 1]
        if plane >= 1:
            value = -down[plane - 1] if value is None else value - down[plane - 1]
        if plane < 0:
            tiles.append((below_ref[5] * value, below_ref[6]))
        elif plane >= width:
            tiles.append((above_ref[5] * value, above_ref[6]))
        else:
            value = value + jnp.where(last, lam_ref[12, plane] - lam_ref[13, plane], 0.0)
            value = value + jnp.where(first, lam_ref[14, plane] - lam_ref[11, plane], 0.0)
            tiles.append(
                (
                    totals[plane] + coef_ref[GAIN, plane] * value,
                    map_ref[plane].astype(jnp.float32),
                )
            )
    for side, (upward, downward, row) in enumerate(((9, 8, span - 1), (7, 10, 0))):
        pad_ref[0] = jnp.zeros(pad_ref.shape[1:], jnp.float32)
        pad_ref[1] = jnp.zeros(pad_ref.shape[1:], jnp.float32)
        pad_ref[2] = jnp.zeros(pad_ref.shape[1:], jnp.float32)
        pad_ref[3] = jnp.full(pad_ref.shape[1:], -1.0, jnp.float32)
        pad_ref[0, 0:width, :] = lam_ref[upward, :, row, :]
        pad_ref[1, 2 : width + 2, :] = lam_ref[downward, :, row, :]
        for field in range(2):
            place = (5 + field) * width
            pad_ref[2 + field, 1 : width + 1, :] = rows_ref[side, place : place + width, :]
            pick = 2 * field + side
            pad_ref[2 + field, 0:1, :] = below_ref[7, pick : pick + 1, :]
            pad_ref[2 + field, width + 1 : width + 2, :] = above_ref[7, pick : pick + 1, :]
        tiles.append(((pad_ref[0] - pad_ref[1]) * pad_ref[2], pad_ref[3]))
    sums_ref[...] = jnp.zeros(sums_ref.shape, jnp.float32)
    for turbine in range(turbines):
        row = None
        for value, ids in tiles:
            kept = jnp.sum(jnp.where(ids == float(turbine), value, 0.0), axis=0, keepdims=True)
            row = kept if row is None else row + kept
        sums_ref[turbine : turbine + 1, :] = row


def call(kernel, outs, *args, scratch=(), smem_first=False, micros=1):
    specs = [pl.BlockSpec(memory_space=VMEM)] * len(args)
    if smem_first:
        specs[0] = pl.BlockSpec(memory_space=pltpu.SMEM)
    return pl.pallas_call(
        kernel,
        out_shape=tuple(jax.ShapeDtypeStruct(shape, jnp.float32) for shape in outs),
        in_specs=specs,
        out_specs=tuple(pl.BlockSpec(memory_space=VMEM) for _ in outs),
        scratch_shapes=list(scratch),
        cost_estimate=pl.CostEstimate(
            flops=int(1e6 * micros), bytes_accessed=int(2e6 * micros), transcendentals=0
        ),
        compiler_params=pltpu.CompilerParams(vmem_limit_bytes=32 * 1024 * 1024),
    )(*args)


def ring(axis, step):
    count = lax.axis_size(axis)
    return [(i, (i + step) % count) for i in range(count)]


def swap_rows(rows):
    if lax.axis_size("gy") == 2:
        return lax.ppermute(rows, "gy", ring("gy", 1))
    return jnp.stack(
        [
            lax.ppermute(rows[0], "gy", ring("gy", -1)),
            lax.ppermute(rows[1], "gy", ring("gy", 1)),
        ]
    )


def swap_faces(low, high):
    above = lax.ppermute(low, "gx", ring("gx", -1))
    below = lax.ppermute(high, "gx", ring("gx", 1))
    return above, below


def total(value):
    for axis, stages in (("gx", (1, 1, 2, 2, 2)), ("gy", (1, 1, 1, 1))):
        count = lax.axis_size(axis)
        if count & (count - 1):
            value = lax.psum(value, axis)
            continue
        start = 1
        for bits in stages:
            stop = min(start << bits, count)
            if start >= stop:
                break
            parts = [value]
            for flip in range(start, stop, start):
                parts.append(lax.ppermute(value, axis, [(i, i ^ flip) for i in range(count)]))
            value = sum(parts[1:], parts[0])
            start = stop
        assert start >= count
    return value


def shards(fwd_pops, fwd_scale, seed_adjoint, turbine_map, thrust):
    steps, _, width, span, height = fwd_pops.shape
    turbines = thrust.shape[0]
    whole = (19, width, span, height)
    coefs = call(
        coef_kernel,
        [(COEFS, width, span, height)] * steps,
        thrust,
        turbine_map,
        fwd_scale,
        fwd_pops,
        smem_first=True,
        micros=1.5,
    )
    lam = seed_adjoint
    (rows,) = call(rows_kernel, [(2, 5 * width, height)], lam, micros=0.2)
    cells = None
    sums = None
    for instant in range(steps - 1, -1, -1):
        got_rows = swap_rows(rows)
        has_gain = instant == 1
        static = (coefs[0], turbine_map) if has_gain else ()
        face = ((8 if has_gain else 5), span, height)
        low, high = call(
            lambda *refs, has_gain=has_gain: faces_kernel(has_gain, *refs),
            [face, face],
            lam,
            got_rows,
            *static,
            micros=0.2,
        )
        above, below = swap_faces(low, high)
        common = (lam, got_rows, above, below, coefs[instant])
        if instant == 2:
            lam, rows, cells = call(
                lambda *refs: step_kernel(0, turbines, *refs),
                [whole, (2, 7 * width, height), (width, span, height)],
                *common,
                coefs[0],
                turbine_map,
                micros=0.5,
            )
        elif instant == 1:
            lam, rows, sums = call(
                lambda *refs: step_kernel(1, turbines, *refs),
                [whole, (2, 5 * width, height), (-(-turbines // 8) * 8, height)],
                *common,
                coefs[0],
                turbine_map,
                cells,
                scratch=[pltpu.VMEM((4, -(-(width + 2) // 8) * 8, height), jnp.float32)],
                micros=0.7,
            )
        else:
            (lam,) = call(
                lambda *refs: step_kernel(2, turbines, *refs), [whole], *common, micros=0.5
            )
    thrust_grad = jnp.sum(total(sums), axis=1)[:turbines]
    return (lam, thrust_grad)


def solution(mesh):
    placed = (
        P(None, None, "gx", "gy", None),
        P(None, "gx", "gy", None),
        P(None, "gx", "gy", None),
        P("gx", "gy", None),
        P(),
    )
    return jax.shard_map(
        shards,
        mesh=mesh,
        in_specs=placed,
        out_specs=(P(None, "gx", "gy", None), P()),
        check_vma=False,
    )
```

time: 114 us -> 46.7 us (0.41)
  blocking collectives: 37.3 us -> 0 us
  local copies, waits for them, and re-layouts: 30.7 us -> 0.99 us
  waiting for transfers between devices: 12.9 us -> 24.9 us
  other arithmetic: 9.76 us -> 0.64 us
  starting transfers between devices: 20.8 us -> 16.5 us
  Pallas kernels: 0 us -> 2.81 us
    psum x1 -> x0, blocking collectives: 37.3 us -> none  [shards(): summed = summed + lax.psum(partial_value, ('gx', 'gy'))]
    gather x1 -> x0, local copies, waits for them, and re-layouts: 24.7 us -> none  [shards(): thrust_cell = jnp.where(inside, jnp.take(local_thrust(thrust), ids), 0.0)]
    ppermute x12 -> x15, waiting for transfers between devices: 12.9 us -> 24.9 us  [the longest x3 12.8 us: swap_faces(): below = lax.ppermute(high, 'gx', ring('gx', 1))]
    ppermute x12 -> x15, starting transfers between devices: 20.8 us -> 16.5 us  [the longest x3 6.05 us: swap_rows(): return lax.ppermute(rows, 'gy', ring('gy', 1))]
    add_any x12 -> x0, other arithmetic: 3.88 us -> none  [the longest x3 2.05 us: collide(): density = populations[0]]
    mul x13 -> x0, other arithmetic: 3.16 us -> none  [the longest x6 1.61 us: collide(): moment = moment + float(component) * populations[member]]
    pallas_call x0 -> x8, Pallas kernels: none -> 2.81 us  [call(): pl.pallas_call(kernel, out_shape=tuple((jax.ShapeDtypeStruct(shape, jnp.f...]
    broadcast_in_dim x6 -> x0, other arithmetic: 2.45 us -> none  [the longest x3 1.59 us: collide(): density = density + populations[member]]
  transfers between devices with their start and end apart: 12 -> 15, of which waited for: 8 -> 12; matrix products, arithmetic and copies ran while one was open for 24% -> 1% of each run, Pallas kernels for 0% -> 3%
where the time goes in v1:
time: 46.7 us; the launch traced here: 46.6 us
  waiting for transfers between devices  24.9 us (53%)
  starting transfers between devices  16.5 us (35%)
  Pallas kernels  2.81 us (6%)
  local copies, waits for them, and re-layouts  0.99 us (2%)
  between operations  0.75 us (2%)
  other arithmetic  0.64 us (1%)
    ppermute x3, waiting for transfers between devices, swap_faces(): below = lax.ppermute(high, 'gx', ring('gx', 1))  12.8 us
    ppermute x3, starting transfers between devices, swap_rows(): return lax.ppermute(rows, 'gy', ring('gy', 1))  6.05 us
    ppermute x6, starting transfers between devices, total(): lax.ppermute(value, axis, [(i, i ^ flip) for i in range(count)])  5.95 us
    ppermute x6, waiting for transfers between devices, total(): lax.ppermute(value, axis, [(i, i ^ flip) for i in range(count)])  5.88 us
    ppermute x3, waiting for transfers between devices, swap_rows(): return lax.ppermute(rows, 'gy', ring('gy', 1))  4.93 us
    ppermute x3, starting transfers between devices, swap_faces(): above = lax.ppermute(low, 'gx', ring('gx', -1))  3.49 us
    pallas_call x8, Pallas kernels, call(): pl.pallas_call(kernel, out_shape=tuple((jax.ShapeDtypeStruct(shape, jnp.f...  2.81 us
    ppermute x3, waiting for transfers between devices, swap_faces(): above = lax.ppermute(low, 'gx', ring('gx', -1))  1.28 us
  transfers between devices with their start and end apart: 15, of which 12 were waited for; matrix products, arithmetic and copies ran while one was open for 1% of the time, Pallas kernels for 3%

profile of v1, /device:TPU:0, one launch (start us, length us, event | category | flops | bytes accessed | tf_op | source)
XLA Modules:
  0.0 46.6 jit_solution(8722503274084170306)
XLA Ops:
  0.6 0.0 copy-start
  0.6 1.0 %copy-done = f32[19,4,8,128]{3,2,1,0:T(8,128)S(1)} copy-done((f32[19,4,8,128]{3,2,1,0:T(8,128)S(1)}, f32[19,4,8,128]{3,2,1,0:T(8,128)}, u32[]{:S(2)}) %copy-start) | copy-done | bytes 311320
  1.6 0.0 copy-start.2
  1.6 0.0 copy-start.3
  1.6 0.0 copy-start.4
  1.6 3.0 %collective-permute-start = (f32[2,20,128]{2,1,0:T(8,128)S(1)}, f32[2,20,128]{2,1,0:T(8,128)S(1)}, u32[]{:S(2)}, u32[]{:S(2)}) collective-permute-start(f32[2,20,128]{2,1,0:T(8,128)S(1)} %shard_map.68), channel_id=1, source_target_pairs={{0,1},{1,0},{2,3},{3,2},{4,5},{5,4},{6,7},{7,6},{8,9},{9,8},{10,11... | collective-permute-start | bytes 61448 | tf_op jit(solution)/shard_map/ppermute | solution.py:430
  4.6 1.8 %collective-permute-done.refs_1_ = f32[2,20,128]{2,1,0:T(8,128)S(1)} collective-permute-done((f32[2,20,128]{2,1,0:T(8,128)S(1)}, f32[2,20,128]{2,1,0:T(8,128)S(1)}, u32[]{:S(2)}, u32[]{:S(2)}) %collective-permute-start) | collective-permute-done | bytes 20512 | tf_op jit(solution)/shard_map/ppermute | solution.py:430
  6.5 0.0 copy-start.5
  6.5 0.0 copy-start.1
  6.5 3.4 %collective-permute-start.1 = (f32[5,8,128]{2,1,0:T(8,128)S(1)}, f32[5,8,128]{2,1,0:T(8,128)S(1)}, u32[]{:S(2)}, u32[]{:S(2)}) collective-permute-start(f32[5,8,128]{2,1,0:T(8,128)S(1)} %get-tuple-element.17), channel_id=1, source_target_pairs={{0,30},{2,0},{4,2},{6,4},{8,6},{10,8},{12,10},{14,12},{16,14},{18,... | collective-permute-start | bytes 61448 | tf_op jit(solution)/shard_map/ppermute | solution.py:440
  9.9 0.0 collective-permute-start.2
  9.9 0.0 copy-done.2
  9.9 0.0 copy-done.3
  9.9 0.0 copy-done.4
  9.9 0.0 copy-done.5
  9.9 1.3 %shard_map.70 = (f32[42,4,8,128]{3,2,1,0:T(8,128)S(1)}, f32[42,4,8,128]{3,2,1,0:T(8,128)S(1)}, f32[42,4,8,128]{3,2,1,0:T(8,128)S(1)}) custom-call(f32[10]{0:T(128)S(1)} %copy-done.5, s32[4,8,128]{2,1,0:T(8,128)S(1)} %copy-done.3, f32[3,4,8,128]{3,2,1,0:T(8,128)S(1)} %copy-done.4, bf16[3,19,4,8,128]{4,3,2,1,0:T(8,128)(2,1)S(1)} %copy-done.2), custom_call_target="tpu_custom_call" | custom-call | flops 1500000 | bytes 3000000 | tf_op jit(solution)/shard_map/pallas_call | solution.py:410
  11.2 0.2 collective-permute-done.1.refs_2_
  11.4 4.4 %collective-permute-done.2.refs_3_ = f32[5,8,128]{2,1,0:T(8,128)S(1)} collective-permute-done((f32[5,8,128]{2,1,0:T(8,128)S(1)}, f32[5,8,128]{2,1,0:T(8,128)S(1)}, u32[]{:S(2)}, u32[]{:S(2)}) %collective-permute-start.2) | collective-permute-done | bytes 20512 | tf_op jit(solution)/shard_map/ppermute | solution.py:441
  15.8 0.0 copy-done.1
  15.8 0.2 shard_map.71
  16.1 1.6 %collective-permute-start.3 = (f32[2,28,128]{2,1,0:T(8,128)S(1)}, f32[2,28,128]{2,1,0:T(8,128)S(1)}, u32[]{:S(2)}, u32[]{:S(2)}) collective-permute-start(f32[2,28,128]{2,1,0:T(8,128)S(1)} %get-tuple-element.22), channel_id=1, source_target_pairs={{0,1},{1,0},{2,3},{3,2},{4,5},{5,4},{6,7},{7,6},{8,9},{9,8},{10,11... | collective-permute-start | bytes 86024 | tf_op jit(solution)/shard_map/ppermute | solution.py:430
  17.6 2.4 %collective-permute-done.3.refs_1_ = f32[2,28,128]{2,1,0:T(8,128)S(1)} collective-permute-done((f32[2,28,128]{2,1,0:T(8,128)S(1)}, f32[2,28,128]{2,1,0:T(8,128)S(1)}, u32[]{:S(2)}, u32[]{:S(2)}) %collective-permute-start.3) | collective-permute-done | bytes 28704 | tf_op jit(solution)/shard_map/ppermute | solution.py:430
  20.0 0.1 collective-permute-start.4
  20.1 0.5 %collective-permute-start.5 = (f32[8,8,128]{2,1,0:T(8,128)S(1)}, f32[8,8,128]{2,1,0:T(8,128)S(1)}, u32[]{:S(2)}, u32[]{:S(2)}) collective-permute-start(f32[8,8,128]{2,1,0:T(8,128)S(1)} %get-tuple-element.24), channel_id=1, source_target_pairs={{0,2},{2,4},{4,6},{6,8},{8,10},{10,12},{12,14},{14,16},{16,18},{18... | collective-permute-start | bytes 98312 | tf_op jit(solution)/shard_map/ppermute | solution.py:441
  20.6 1.1 %collective-permute-done.4.refs_2_ = f32[8,8,128]{2,1,0:T(8,128)S(1)} collective-permute-done((f32[8,8,128]{2,1,0:T(8,128)S(1)}, f32[8,8,128]{2,1,0:T(8,128)S(1)}, u32[]{:S(2)}, u32[]{:S(2)}) %collective-permute-start.4) | collective-permute-done | bytes 32800 | tf_op jit(solution)/shard_map/ppermute | solution.py:440
  21.7 4.5 %collective-permute-done.5.refs_3_ = f32[8,8,128]{2,1,0:T(8,128)S(1)} collective-permute-done((f32[8,8,128]{2,1,0:T(8,128)S(1)}, f32[8,8,128]{2,1,0:T(8,128)S(1)}, u32[]{:S(2)}, u32[]{:S(2)}) %collective-permute-start.5) | collective-permute-done | bytes 32800 | tf_op jit(solution)/shard_map/ppermute | solution.py:441
  26.2 0.4 shard_map.73
  26.6 0.1 collective-permute-start.9
  26.6 1.2 %collective-permute-done.9 = f32[16,128]{1,0:T(8,128)S(1)} collective-permute-done((f32[16,128]{1,0:T(8,128)S(1)}, f32[16,128]{1,0:T(8,128)S(1)}, u32[]{:S(2)}, u32[]{:S(2)}) %collective-permute-start.9) | collective-permute-done | bytes 8224 | tf_op jit(solution)/shard_map/ppermute | solution.py:458
  27.8 0.0 collective-permute-start.10
  27.8 3.6 %collective-permute-done.10 = f32[16,128]{1,0:T(8,128)S(1)} collective-permute-done((f32[16,128]{1,0:T(8,128)S(1)}, f32[16,128]{1,0:T(8,128)S(1)}, u32[]{:S(2)}, u32[]{:S(2)}) %collective-permute-start.10) | collective-permute-done | bytes 8224 | tf_op jit(solution)/shard_map/ppermute | solution.py:458
  31.5 0.0 collective-permute-start.13
  31.5 0.0 collective-permute-start.12
  31.5 4.4 %collective-permute-start.11 = (f32[16,128]{1,0:T(8,128)S(1)}, f32[16,128]{1,0:T(8,128)S(1)}, u32[]{:S(2)}, u32[]{:S(2)}) collective-permute-start(f32[16,128]{1,0:T(8,128)S(1)} %add.19), channel_id=1, source_target_pairs={{0,8},{2,10},{4,12},{6,14},{8,0},{10,2},{12,4},{14,6},{16,24},{18,... | collective-permute-start | bytes 24584 | tf_op jit(solution)/shard_map/ppermute | solution.py:458
  35.8 1.5 %collective-permute-start.6 = (f32[2,20,128]{2,1,0:T(8,128)S(1)}, f32[2,20,128]{2,1,0:T(8,128)S(1)}, u32[]{:S(2)}, u32[]{:S(2)}) collective-permute-start(f32[2,20,128]{2,1,0:T(8,128)S(1)} %get-tuple-element.28), channel_id=1, source_target_pairs={{0,1},{1,0},{2,3},{3,2},{4,5},{5,4},{6,7},{7,6},{8,9},{9,8},{10,11... | collective-permute-start | bytes 61448 | tf_op jit(solution)/shard_map/ppermute | solution.py:430
  37.3 0.0 collective-permute-done.13
  37.3 0.0 collective-permute-done.12
  37.3 0.1 collective-permute-done.11
  37.5 1.5 %collective-permute-start.14 = (f32[16,128]{1,0:T(8,128)S(1)}, f32[16,128]{1,0:T(8,128)S(1)}, u32[]{:S(2)}, u32[]{:S(2)}) collective-permute-start(f32[16,128]{1,0:T(8,128)S(1)} %add_add_fusion), channel_id=1, source_target_pairs={{0,1},{1,0},{2,3},{3,2},{4,5},{5,4},{6,7},{7,6},{8,9},{9,8},{10,11... | collective-permute-start | bytes 24584 | tf_op jit(solution)/shard_map/ppermute | solution.py:458
  39.0 0.7 %collective-permute-done.6.refs_1_ = f32[2,20,128]{2,1,0:T(8,128)S(1)} collective-permute-done((f32[2,20,128]{2,1,0:T(8,128)S(1)}, f32[2,20,128]{2,1,0:T(8,128)S(1)}, u32[]{:S(2)}, u32[]{:S(2)}) %collective-permute-start.6) | collective-permute-done | bytes 20512 | tf_op jit(solution)/shard_map/ppermute | solution.py:430
  39.7 0.0 collective-permute-start.7
  39.7 0.5 %collective-permute-start.8 = (f32[5,8,128]{2,1,0:T(8,128)S(1)}, f32[5,8,128]{2,1,0:T(8,128)S(1)}, u32[]{:S(2)}, u32[]{:S(2)}) collective-permute-start(f32[5,8,128]{2,1,0:T(8,128)S(1)} %get-tuple-element.30), channel_id=1, source_target_pairs={{0,2},{2,4},{4,6},{6,8},{8,10},{10,12},{12,14},{14,16},{16,18},{18... | collective-permute-start | bytes 61448 | tf_op jit(solution)/shard_map/ppermute | solution.py:441
  40.2 0.9 %collective-permute-done.14 = f32[16,128]{1,0:T(8,128)S(1)} collective-permute-done((f32[16,128]{1,0:T(8,128)S(1)}, f32[16,128]{1,0:T(8,128)S(1)}, u32[]{:S(2)}, u32[]{:S(2)}) %collective-permute-start.14) | collective-permute-done | bytes 8224 | tf_op jit(solution)/shard_map/ppermute | solution.py:458
  41.1 0.6 %add_reduce_fusion = f32[16]{0:T(128)} fusion(f32[16,128]{1,0:T(8,128)S(1)} %add_add_fusion, f32[16,128]{1,0:T(8,128)S(1)} %collective-permute-done.14), kind=kLoop, calls=%fused_computation | loop fusion | flops 4080 | bytes 16448 | tf_op jit(solution)/shard_map/reduce_sum | solution.py:522
  41.8 0.0 collective-permute-done.7.refs_2_
  41.8 3.9 %collective-permute-done.8.refs_3_ = f32[5,8,128]{2,1,0:T(8,128)S(1)} collective-permute-done((f32[5,8,128]{2,1,0:T(8,128)S(1)}, f32[5,8,128]{2,1,0:T(8,128)S(1)}, u32[]{:S(2)}, u32[]{:S(2)}) %collective-permute-start.8) | collective-permute-done | bytes 20512 | tf_op jit(solution)/shard_map/ppermute | solution.py:441
  45.6 0.9 %shard_map.75 = f32[19,4,8,128]{3,2,1,0:T(8,128)} custom-call(f32[19,4,8,128]{3,2,1,0:T(8,128)S(1)} %get-tuple-element.27.refs_0_, f32[2,20,128]{2,1,0:T(8,128)S(1)} %collective-permute-done.6.refs_1_, f32[5,8,128]{2,1,0:T(8,128)S(1)} %collective-permute-done.7.refs_2_, f32[5,8,128]{2,1,0:T(8,128)S(1)} %collective-permute-done.8.refs_3_, ...), custom_call_target="tpu_custom_call" | custom-call | flops 500000 | bytes 1000000 | tf_op jit(solution)/shard_map/pallas_call | solution.py:410
  (7 shorter events, 0.0 us)
Async XLA Ops:
  0.6 1.0 %copy-start = (f32[19,4,8,128]{3,2,1,0:T(8,128)S(1)}, f32[19,4,8,128]{3,2,1,0:T(8,128)}, u32[]{:S(2)}) copy-start(f32[19,4,8,128]{3,2,1,0:T(8,128)} %refs_0_.3) | copy-start | bytes 933892
  1.6 8.3 %copy-start.2 = (bf16[3,19,4,8,128]{4,3,2,1,0:T(8,128)(2,1)S(1)}, bf16[3,19,4,8,128]{4,3,2,1,0:T(8,128)(2,1)}, u32[]{:S(2)}) copy-start(bf16[3,19,4,8,128]{4,3,2,1,0:T(8,128)(2,1)} %pops_ref.1) | copy-start | bytes 1400836
  1.6 8.3 %copy-start.3 = (s32[4,8,128]{2,1,0:T(8,128)S(1)}, s32[4,8,128]{2,1,0:T(8,128)}, u32[]{:S(2)}) copy-start(s32[4,8,128]{2,1,0:T(8,128)} %refs_6_.3) | copy-start | bytes 49156
  1.6 8.3 %copy-start.4 = (f32[3,4,8,128]{3,2,1,0:T(8,128)S(1)}, f32[3,4,8,128]{3,2,1,0:T(8,128)}, u32[]{:S(2)}) copy-start(f32[3,4,8,128]{3,2,1,0:T(8,128)} %scale_ref.1) | copy-start | bytes 147460
  1.6 4.8 %collective-permute-start = (f32[2,20,128]{2,1,0:T(8,128)S(1)}, f32[2,20,128]{2,1,0:T(8,128)S(1)}, u32[]{:S(2)}, u32[]{:S(2)}) collective-permute-start(f32[2,20,128]{2,1,0:T(8,128)S(1)} %shard_map.68), channel_id=1, source_target_pairs={{0,1},{1,0},{2,3},{3,2},{4,5},{5,4},{6,7},{7,6},{8,9},{9,8},{10,11... | collective-permute-start | bytes 61448 | tf_op jit(solution)/shard_map/ppermute | solution.py:430
  6.5 3.5 %copy-start.5 = (f32[10]{0:T(128)S(1)}, f32[10]{0:T(128)}, u32[]{:S(2)}) copy-start(f32[10]{0:T(128)} %thrust_ref.1) | copy-start | bytes 124
  6.5 9.3 %copy-start.1 = (f32[19,4,8,128]{3,2,1,0:T(8,128)S(1)}, f32[19,4,8,128]{3,2,1,0:T(8,128)}, u32[]{:S(2)}) copy-start(f32[19,4,8,128]{3,2,1,0:T(8,128)} %refs_0_.3) | copy-start | bytes 933892
  6.5 4.9 %collective-permute-start.1 = (f32[5,8,128]{2,1,0:T(8,128)S(1)}, f32[5,8,128]{2,1,0:T(8,128)S(1)}, u32[]{:S(2)}, u32[]{:S(2)}) collective-permute-start(f32[5,8,128]{2,1,0:T(8,128)S(1)} %get-tuple-element.17), channel_id=1, source_target_pairs={{0,30},{2,0},{4,2},{6,4},{8,6},{10,8},{12,10},{14,12},{16,14},{18,... | collective-permute-start | bytes 61448 | tf_op jit(solution)/shard_map/ppermute | solution.py:440
  9.9 5.9 %collective-permute-start.2 = (f32[5,8,128]{2,1,0:T(8,128)S(1)}, f32[5,8,128]{2,1,0:T(8,128)S(1)}, u32[]{:S(2)}, u32[]{:S(2)}) collective-permute-start(f32[5,8,128]{2,1,0:T(8,128)S(1)} %get-tuple-element.18), channel_id=1, source_target_pairs={{0,2},{2,4},{4,6},{6,8},{8,10},{10,12},{12,14},{14,16},{16,18},{18... | collective-permute-start | bytes 61448 | tf_op jit(solution)/shard_map/ppermute | solution.py:441
  16.1 4.0 %collective-permute-start.3 = (f32[2,28,128]{2,1,0:T(8,128)S(1)}, f32[2,28,128]{2,1,0:T(8,128)S(1)}, u32[]{:S(2)}, u32[]{:S(2)}) collective-permute-start(f32[2,28,128]{2,1,0:T(8,128)S(1)} %get-tuple-element.22), channel_id=1, source_target_pairs={{0,1},{1,0},{2,3},{3,2},{4,5},{5,4},{6,7},{7,6},{8,9},{9,8},{10,11... | collective-permute-start | bytes 86024 | tf_op jit(solution)/shard_map/ppermute | solution.py:430
  20.0 1.7 %collective-permute-start.4 = (f32[8,8,128]{2,1,0:T(8,128)S(1)}, f32[8,8,128]{2,1,0:T(8,128)S(1)}, u32[]{:S(2)}, u32[]{:S(2)}) collective-permute-start(f32[8,8,128]{2,1,0:T(8,128)S(1)} %get-tuple-element.23), channel_id=1, source_target_pairs={{0,30},{2,0},{4,2},{6,4},{8,6},{10,8},{12,10},{14,12},{16,14},{18,... | collective-permute-start | bytes 98312 | tf_op jit(solution)/shard_map/ppermute | solution.py:440
  20.1 6.1 %collective-permute-start.5 = (f32[8,8,128]{2,1,0:T(8,128)S(1)}, f32[8,8,128]{2,1,0:T(8,128)S(1)}, u32[]{:S(2)}, u32[]{:S(2)}) collective-permute-start(f32[8,8,128]{2,1,0:T(8,128)S(1)} %get-tuple-element.24), channel_id=1, source_target_pairs={{0,2},{2,4},{4,6},{6,8},{8,10},{10,12},{12,14},{14,16},{16,18},{18... | collective-permute-start | bytes 98312 | tf_op jit(solution)/shard_map/ppermute | solution.py:441
  26.6 1.2 %collective-permute-start.9 = (f32[16,128]{1,0:T(8,128)S(1)}, f32[16,128]{1,0:T(8,128)S(1)}, u32[]{:S(2)}, u32[]{:S(2)}) collective-permute-start(f32[16,128]{1,0:T(8,128)S(1)} %get-tuple-element.31), channel_id=1, source_target_pairs={{0,2},{2,0},{4,6},{6,4},{8,10},{10,8},{12,14},{14,12},{16,18},{18,... | collective-permute-start | bytes 24584 | tf_op jit(solution)/shard_map/ppermute | solution.py:458
  27.8 3.7 %collective-permute-start.10 = (f32[16,128]{1,0:T(8,128)S(1)}, f32[16,128]{1,0:T(8,128)S(1)}, u32[]{:S(2)}, u32[]{:S(2)}) collective-permute-start(f32[16,128]{1,0:T(8,128)S(1)} %add.18), channel_id=1, source_target_pairs={{0,4},{2,6},{4,0},{6,2},{8,12},{10,14},{12,8},{14,10},{16,20},{18,... | collective-permute-start | bytes 24584 | tf_op jit(solution)/shard_map/ppermute | solution.py:458
  31.5 5.9 %collective-permute-start.13 = (f32[16,128]{1,0:T(8,128)S(1)}, f32[16,128]{1,0:T(8,128)S(1)}, u32[]{:S(2)}, u32[]{:S(2)}) collective-permute-start(f32[16,128]{1,0:T(8,128)S(1)} %add.19), channel_id=1, source_target_pairs={{0,24},{2,26},{4,28},{6,30},{8,16},{10,18},{12,20},{14,22},{16,8},... | collective-permute-start | bytes 24584 | tf_op jit(solution)/shard_map/ppermute | solution.py:458
  31.5 5.9 %collective-permute-start.12 = (f32[16,128]{1,0:T(8,128)S(1)}, f32[16,128]{1,0:T(8,128)S(1)}, u32[]{:S(2)}, u32[]{:S(2)}) collective-permute-start(f32[16,128]{1,0:T(8,128)S(1)} %add.19), channel_id=1, source_target_pairs={{0,16},{2,18},{4,20},{6,22},{8,24},{10,26},{12,28},{14,30},{16,0},... | collective-permute-start | bytes 24584 | tf_op jit(solution)/shard_map/ppermute | solution.py:458
  31.5 6.0 %collective-permute-start.11 = (f32[16,128]{1,0:T(8,128)S(1)}, f32[16,128]{1,0:T(8,128)S(1)}, u32[]{:S(2)}, u32[]{:S(2)}) collective-permute-start(f32[16,128]{1,0:T(8,128)S(1)} %add.19), channel_id=1, source_target_pairs={{0,8},{2,10},{4,12},{6,14},{8,0},{10,2},{12,4},{14,6},{16,24},{18,... | collective-permute-start | bytes 24584 | tf_op jit(solution)/shard_map/ppermute | solution.py:458
  35.8 3.8 %collective-permute-start.6 = (f32[2,20,128]{2,1,0:T(8,128)S(1)}, f32[2,20,128]{2,1,0:T(8,128)S(1)}, u32[]{:S(2)}, u32[]{:S(2)}) collective-permute-start(f32[2,20,128]{2,1,0:T(8,128)S(1)} %get-tuple-element.28), channel_id=1, source_target_pairs={{0,1},{1,0},{2,3},{3,2},{4,5},{5,4},{6,7},{7,6},{8,9},{9,8},{10,11... | collective-permute-start | bytes 61448 | tf_op jit(solution)/shard_map/ppermute | solution.py:430
  37.5 3.7 %collective-permute-start.14 = (f32[16,128]{1,0:T(8,128)S(1)}, f32[16,128]{1,0:T(8,128)S(1)}, u32[]{:S(2)}, u32[]{:S(2)}) collective-permute-start(f32[16,128]{1,0:T(8,128)S(1)} %add_add_fusion), channel_id=1, source_target_pairs={{0,1},{1,0},{2,3},{3,2},{4,5},{5,4},{6,7},{7,6},{8,9},{9,8},{10,11... | collective-permute-start | bytes 24584 | tf_op jit(solution)/shard_map/ppermute | solution.py:458
  39.7 2.1 %collective-permute-start.7 = (f32[5,8,128]{2,1,0:T(8,128)S(1)}, f32[5,8,128]{2,1,0:T(8,128)S(1)}, u32[]{:S(2)}, u32[]{:S(2)}) collective-permute-start(f32[5,8,128]{2,1,0:T(8,128)S(1)} %get-tuple-element.29), channel_id=1, source_target_pairs={{0,30},{2,0},{4,2},{6,4},{8,6},{10,8},{12,10},{14,12},{16,14},{18,... | collective-permute-start | bytes 61448 | tf_op jit(solution)/shard_map/ppermute | solution.py:440
  39.7 6.0 %collective-permute-start.8 = (f32[5,8,128]{2,1,0:T(8,128)S(1)}, f32[5,8,128]{2,1,0:T(8,128)S(1)}, u32[]{:S(2)}, u32[]{:S(2)}) collective-permute-start(f32[5,8,128]{2,1,0:T(8,128)S(1)} %get-tuple-element.30), channel_id=1, source_target_pairs={{0,2},{2,4},{4,6},{6,8},{8,10},{10,12},{12,14},{14,16},{16,18},{18... | collective-permute-start | bytes 61448 | tf_op jit(solution)/shard_map/ppermute | solution.py:441

commit v2 on v1

v2 whole, which is shorter than its diff:
```python
import jax
import jax.numpy as jnp
from jax import lax
from jax.experimental import pallas as pl
from jax.experimental.pallas import tpu as pltpu
from jax.sharding import PartitionSpec as P

VELOCITIES = (
    (0, 0, 0),
    (1, 0, 0),
    (-1, 0, 0),
    (0, 1, 0),
    (0, -1, 0),
    (0, 0, 1),
    (0, 0, -1),
    (1, 1, 0),
    (-1, -1, 0),
    (1, -1, 0),
    (-1, 1, 0),
    (1, 0, 1),
    (-1, 0, -1),
    (1, 0, -1),
    (-1, 0, 1),
    (0, 1, 1),
    (0, -1, -1),
    (0, 1, -1),
    (0, -1, 1),
)
OPPOSITE = (0, 2, 1, 4, 3, 6, 5, 8, 7, 10, 9, 12, 11, 14, 13, 16, 15, 18, 17)
WEIGHTS = tuple([1.0 / 3.0] + [1.0 / 18.0] * 6 + [1.0 / 36.0] * 12)
MEAN_FLOW = 0.1
TAU_BASE = 0.51
SMAG_COEF = 18.0 * 1.4142135623730951 * 0.17 * 0.17
QUAD_FLOOR = 0.0001

X_UP = (1, 7, 9, 11, 13)
X_DOWN = (2, 8, 10, 12, 14)
Y_UP = (3, 7, 10, 15, 17)
Y_DOWN = (4, 8, 9, 16, 18)

KEEP, MASS, FLUX, UX, UY, UZ, Q1 = 19, 20, 21, 22, 23, 24, 25
RATE, BULK, PX, PY, PZ, DRAG, DRAG_U, GAIN = 34, 35, 36, 37, 38, 39, 40, 41
COEFS = 42

FIELDS = 21

VMEM = pltpu.VMEM


def halo_list(axis, sign):
    near = [
        (1, m) for m in range(19) if VELOCITIES[m][axis] * sign >= 0 or VELOCITIES[m][2] != 0
    ]
    return near + [(2, m) for m in range(19) if VELOCITIES[m][axis] * sign == 1]


SIGNS = (1, -1)
FACE_LIST = [halo_list(0, sign) for sign in SIGNS]
ROW_LIST = [halo_list(1, sign) for sign in SIGNS]
INNER_LIST = [[(0, m) for m in range(19) if VELOCITIES[m][1] * sign == -1] for sign in SIGNS]
PACK_LIST = [ROW_LIST[side] + INNER_LIST[side] for side in range(2)]
CORNER_LIST = [
    [
        [(far_x, far_y, m) for far_x, m in FACE_LIST[x] for far_y in (1, 2) if (far_y, m) in ROW_LIST[y]]
        for y in range(2)
    ]
    for x in range(2)
]
HALO = len(ROW_LIST[0])
CORNER = len(CORNER_LIST[0][0])
FACE_TILES = HALO + FIELDS


def base_values():
    values = []
    for member in range(19):
        along = float(VELOCITIES[member][0])
        values.append(
            WEIGHTS[member]
            * (
                1.0
                + 3.0 * MEAN_FLOW * along
                + 4.5 * MEAN_FLOW * MEAN_FLOW * along * along
                - 1.5 * MEAN_FLOW * MEAN_FLOW
            )
        )
    return values


def plane_coefs(pops, thrust_cell, slope_cell):
    rho = pops[0]
    for member in range(1, 19):
        rho = rho + pops[member]
    inv_rho = 1.0 / rho
    vel = []
    for axis_id in range(3):
        moment = None
        for member in range(19):
            component = VELOCITIES[member][axis_id]
            if component == 1:
                moment = pops[member] if moment is None else moment + pops[member]
            elif component == -1:
                moment = moment - pops[member]
        vel.append(moment * inv_rho)
    ux, uy, uz = vel
    speed_sq = ux * ux + uy * uy + uz * uz
    rest = 1.0 - 1.5 * speed_sq
    part = []
    for member in range(19):
        if member == 0:
            part.append(pops[0] - (WEIGHTS[0] * rho) * rest)
            continue
        proj = None
        for axis_id in range(3):
            component = VELOCITIES[member][axis_id]
            if component == 1:
                proj = vel[axis_id] if proj is None else proj + vel[axis_id]
            elif component == -1:
                proj = -vel[axis_id] if proj is None else proj - vel[axis_id]
        part.append(pops[member] - (WEIGHTS[member] * rho) * (rest + 3.0 * proj + 4.5 * proj * proj))

    def pair(member):
        return part[member] + part[member + 1]

    in_xy, in_xz, in_yz = pair(7) + pair(9), pair(11) + pair(13), pair(15) + pair(17)
    pxx, pyy, pzz = pair(1) + in_xy + in_xz, pair(3) + in_xy + in_yz, pair(5) + in_xz + in_yz
    pxy, pxz, pyz = pair(7) - pair(9), pair(11) - pair(13), pair(15) - pair(17)
    square = (
        pxx * pxx + pyy * pyy + pzz * pzz + 2.0 * (pxy * pxy + pxz * pxz + pyz * pyz) + QUAD_FLOOR
    )
    size = jnp.sqrt(square)
    root = jnp.sqrt(TAU_BASE * TAU_BASE + SMAG_COEF * size * inv_rho)
    omega = 1.0 / (0.5 * (TAU_BASE + root))
    pux = pxx * ux + pxy * uy + pxz * uz
    puy = pxy * ux + pyy * uy + pyz * uz
    puz = pxz * ux + pyz * uy + pzz * uz
    flux = omega * (3.0 / 36.0)
    drag = (3.0 / 36.0) * thrust_cell * jnp.abs(ux) * inv_rho
    result = list(part)
    result.append(1.0 - omega)
    result.append((omega * (1.0 / 36.0)) * (1.0 + 1.5 * speed_sq))
    result.append(flux)
    result.extend(vel)
    result.extend((pxx, pyy, pzz))
    result.extend((pxx + pyy + 2.0 * pxy, pxx + pyy - 2.0 * pxy))
    result.extend((pxx + pzz + 2.0 * pxz, pxx + pzz - 2.0 * pxz))
    result.extend((pyy + pzz + 2.0 * pyz, pyy + pzz - 2.0 * pyz))
    result.append((0.25 * SMAG_COEF) * omega * omega * inv_rho / (root * size))
    result.append(
        (pux * ux + puy * uy + puz * uz) - (pxx + pyy + pzz) * (1.0 / 3.0) - square * inv_rho
    )
    result.extend((-2.0 * pux, -2.0 * puy, -2.0 * puz))
    result.append(drag)
    result.append(drag * ux)
    if slope_cell is not None:
        result.append((-1.5 / 36.0) * ux * jnp.abs(ux) * slope_cell)
    return result


def plane_adjoint(mu, coef, wanted=range(19)):
    total, diff = {}, {}
    for member in range(1, 19, 2):
        total[member] = mu[member] + mu[member + 1]
        diff[member] = mu[member] - mu[member + 1]
    two_x, two_y, two_z = 2.0 * total[1], 2.0 * total[3], 2.0 * total[5]
    in_xy, in_xz, in_yz = total[7] + total[9], total[11] + total[13], total[15] + total[17]
    mxx, myy, mzz = two_x + in_xy + in_xz, two_y + in_xy + in_yz, two_z + in_xz + in_yz
    mxy, mxz, myz = total[7] - total[9], total[11] - total[13], total[15] - total[17]
    m0 = 12.0 * mu[0] + (two_x + two_y + two_z) + (in_xy + in_xz + in_yz)
    mx = 2.0 * diff[1] + (diff[7] + diff[9]) + (diff[11] + diff[13])
    my = 2.0 * diff[3] + (diff[7] - diff[9]) + (diff[15] + diff[17])
    mz = 2.0 * diff[5] + (diff[11] - diff[13]) + (diff[15] - diff[17])
    ux, uy, uz = coef(UX), coef(UY), coef(UZ)
    vx = mxx * ux + mxy * uy + mxz * uz
    vy = mxy * ux + myy * uy + myz * uz
    vz = mxz * ux + myz * uy + mzz * uz
    along = [mu[member] * coef(member) for member in range(19)]
    while len(along) > 1:
        along = [
            along[k] + along[k + 1] if k + 1 < len(along) else along[k]
            for k in range(0, len(along), 2)
        ]
    gamma = along[0] * coef(RATE)
    flux = coef(FLUX)
    alpha = (
        coef(MASS) * m0
        - 1.5 * flux * (vx * ux + vy * uy + vz * uz)
        + gamma * coef(BULK)
        + mx * coef(DRAG_U)
    )
    beta_x = flux * (mx + 3.0 * vx - ux * m0) + gamma * coef(PX) - mx * coef(DRAG)
    beta_y = flux * (my + 3.0 * vy - uy * m0) + gamma * coef(PY)
    beta_z = flux * (mz + 3.0 * vz - uz * m0) + gamma * coef(PZ)
    keep = coef(KEEP)
    odd = {
        1: beta_x,
        3: beta_y,
        5: beta_z,
        7: beta_x + beta_y,
        9: beta_x - beta_y,
        11: beta_x + beta_z,
        13: beta_x - beta_z,
        15: beta_y + beta_z,
        17: beta_y - beta_z,
    }
    result = {}
    for member in wanted:
        if member == 0:
            result[0] = keep * mu[0] + alpha
            continue
        forward = member - 1 + member % 2
        even = alpha + gamma * coef(Q1 + forward // 2)
        if member == forward:
            result[member] = keep * mu[member] + (even + odd[forward])
        else:
            result[member] = keep * mu[member] + (even - odd[forward])
    return result, mx


def turbine_cells(ids, thrust_ref, slope):
    ratio = jnp.zeros(ids.shape, jnp.float32)
    for turbine in range(thrust_ref.shape[0]):
        ratio = jnp.where(ids == jnp.asarray(turbine, ids.dtype), thrust_ref[turbine], ratio)
    root = jnp.sqrt(1.0 - ratio)
    square = (1.0 + root) * (1.0 + root)
    inside = ids >= 0
    thrust_cell = jnp.where(inside, 4.0 * ratio / square, 0.0)
    return thrust_cell, jnp.where(inside, 4.0 / (root * square), 0.0) if slope else None


def decode(scale_ref, pops_ref, instant, plane):
    base = base_values()
    scale = scale_ref[instant, plane]
    return [
        base[member] * (1.0 + scale * pops_ref[instant, member, plane].astype(jnp.float32))
        for member in range(19)
    ]


def coef_kernel(thrust_ref, map_ref, scale_ref, pops_ref, *out_refs):
    for plane in range(pops_ref.shape[2]):
        thrust_cell, slope_cell = turbine_cells(map_ref[plane], thrust_ref, True)
        for instant, out_ref in enumerate(out_refs):
            pops = decode(scale_ref, pops_ref, instant, plane)
            for index, value in enumerate(plane_coefs(pops, thrust_cell, slope_cell)):
                out_ref[index, plane] = value


def pack_kernel(last, thrust_ref, map_ref, scale_ref, pops_ref, lam_ref, fields_ref, rows_ref):
    width, span = lam_ref.shape[1], lam_ref.shape[2]
    for plane in range(width):
        for index, value in enumerate(decode(scale_ref, pops_ref, last, plane)):
            fields_ref[index, plane] = value
        fields_ref[19, plane] = map_ref[plane].astype(jnp.float32)
        _, slope_cell = turbine_cells(map_ref[plane], thrust_ref, True)
        pops = decode(scale_ref, pops_ref, 0, plane)
        rho, momentum = pops[0], None
        for member in range(1, 19):
            rho = rho + pops[member]
        for member in X_UP:
            pair = pops[member] - pops[member + 1]
            momentum = pair if momentum is None else momentum + pair
        ux = momentum / rho
        fields_ref[20, plane] = (-1.5 / 36.0) * ux * jnp.abs(ux) * slope_cell
    for side in range(2):
        for index, (far, member) in enumerate(ROW_LIST[side]):
            row = far - 1 if side == 0 else span - far
            rows_ref[side, index * width : (index + 1) * width, :] = lam_ref[member, :, row, :]
        row = 0 if side == 0 else span - 1
        for field in range(FIELDS):
            start = (HALO + field) * width
            rows_ref[side, start : start + width, :] = fields_ref[field, :, row, :]


def faces_kernel(lam_ref, fields_ref, rows_ref, *out_refs):
    width = lam_ref.shape[1]
    for x_side, out_ref in enumerate(out_refs):

        def plane(far, x_side=x_side):
            return far - 1 if x_side == 0 else width - far

        for index, (far, member) in enumerate(FACE_LIST[x_side]):
            out_ref[index] = lam_ref[member, plane(far)]
        for field in range(FIELDS):
            out_ref[HALO + field] = fields_ref[field, plane(1)]
        slot = 0
        for y_side in range(2):
            picks = [
                ROW_LIST[y_side].index((far_y, member)) * width + plane(far_x)
                for far_x, far_y, member in CORNER_LIST[x_side][y_side]
            ]
            picks += [(HALO + field) * width + plane(1) for field in range(FIELDS)]
            for pick in picks:
                tile, row = FACE_TILES + slot // 8, slot % 8
                out_ref[tile, row : row + 1, :] = rows_ref[y_side, pick : pick + 1, :]
                slot += 1


def span_shift(value, move, row):
    span = value.shape[0]
    place = lax.broadcasted_iota(jnp.int32, value.shape, 0)
    if move == 1:
        return jnp.where(place == span - 1, row, pltpu.roll(value, span - 1, 0))
    return jnp.where(place == 0, row, pltpu.roll(value, 1, 0))


def gather_mu(source, row_of, plane, first, last):
    mu = []
    for member in range(19):
        move_x, move_y, move_z = VELOCITIES[member]
        value = source(plane + move_x, member)
        if move_y != 0:
            side = 0 if move_y == 1 else 1
            value = span_shift(value, move_y, row_of(side, plane + move_x, member))
        mu.append(bounce(value, move_z, source, plane, member, first, last))
    return mu


def bounce(value, move_z, source, plane, member, first, last):
    height = value.shape[1]
    if move_z == 1:
        return jnp.where(
            last, source(plane, OPPOSITE[member]), pltpu.roll(value, height - 1, 1)
        )
    if move_z == -1:
        return jnp.where(first, source(plane, OPPOSITE[member]), pltpu.roll(value, 1, 1))
    return value


def pair_kernel(thrust_ref, lam_ref, rows_ref, above_ref, below_ref, late_ref, early_ref, fields_ref,
                out_ref, next_ref, pack_ref, field_ref, mid_ref, face_ref, edge_ref):
    width, span, height = lam_ref.shape[1:]
    faces = (above_ref, below_ref)
    lane = lax.broadcasted_iota(jnp.int32, (span, height), 1)
    first, last = lane == 0, lane == height - 1
    pack_lane = lax.broadcasted_iota(jnp.int32, pack_ref.shape[2:], 1)
    pack_first, pack_last = pack_lane == 0, pack_lane == height - 1

    def seed(plane, member):
        if plane >= width:
            return above_ref[FACE_LIST[0].index((plane - width + 1, member))]
        if plane < 0:
            return below_ref[FACE_LIST[1].index((-plane, member))]
        return lam_ref[member, plane]

    outside = {0: (width + 2, 1), 1: (1, -1)}
    pack_ref[...] = jnp.zeros(pack_ref.shape, jnp.float32)
    field_ref[...] = jnp.zeros(field_ref.shape, jnp.float32)
    for y_side in range(2):
        inner = span - 1 if y_side == 0 else 0
        for index, (far, member) in enumerate(PACK_LIST[y_side]):
            if far > 0:
                pack_ref[y_side, index, 2 : width + 2, :] = rows_ref[
                    y_side, index * width : (index + 1) * width, :
                ]
                continue
            pack_ref[y_side, index, 2 : width + 2, :] = lam_ref[member, :, inner, :]
            for x_side in range(2):
                start, step = outside[x_side]
                for far_x in (1, 2):
                    if (far_x, member) in FACE_LIST[x_side]:
                        place = start + step * (far_x - 1)
                        tile = FACE_LIST[x_side].index((far_x, member))
                        pack_ref[y_side, index, place : place + 1, :] = faces[x_side][
                            tile, inner : inner + 1, :
                        ]
        for field in range(FIELDS):
            start = (HALO + field) * width
            field_ref[y_side, field, 2 : width + 2, :] = rows_ref[y_side, start : start + width, :]
        for x_side in range(2):
            start, step = outside[x_side]
            slot = y_side * (CORNER + FIELDS)
            for far_x, far_y, member in CORNER_LIST[x_side][y_side]:
                place = start + step * (far_x - 1)
                index = PACK_LIST[y_side].index((far_y, member))
                tile, row = FACE_TILES + slot // 8, slot % 8
                pack_ref[y_side, index, place : place + 1, :] = faces[x_side][tile, row : row + 1, :]
                slot += 1
            for field in range(FIELDS):
                tile, row = FACE_TILES + slot // 8, slot % 8
                field_ref[y_side, field, start : start + 1, :] = faces[x_side][
                    tile, row : row + 1, :
                ]
                slot += 1

    def seed_row(side, plane, member):
        index = PACK_LIST[side].index((1, member))
        return pack_ref[side, index, plane + 2 : plane + 3, :]

    totals = []
    for plane in range(-1, width + 1):
        mu = gather_mu(seed, seed_row, plane, first, last)
        if 0 <= plane < width:
            lam, mx = plane_adjoint(mu, lambda index: late_ref[index, plane])
            for member in range(19):
                mid_ref[member, plane] = lam[member]
            totals.append(mx * late_ref[GAIN, plane])
            continue
        side, wanted = (0, X_UP) if plane >= width else (1, X_DOWN)
        pops = [faces[side][HALO + member] for member in range(19)]
        thrust_cell, _ = turbine_cells(faces[side][HALO + 19], thrust_ref, False)
        coefs = plane_coefs(pops, thrust_cell, None)
        lam, _ = plane_adjoint(mu, lambda index: coefs[index], wanted)
        for index, member in enumerate(wanted):
            face_ref[side, index] = lam[member]
    for side, (sign, wanted) in enumerate(((1, Y_UP), (-1, Y_DOWN))):

        def edge(_, member, side=side):
            return pack_ref[side, PACK_LIST[side].index((1, member))]

        mu = []
        for member in range(19):
            move_x, move_y, move_z = VELOCITIES[member]
            value = pack_ref[side, PACK_LIST[side].index((1 + sign * move_y, member))]
            if move_x != 0:
                value = pltpu.roll(value, (-move_x) % value.shape[0], 0)
            mu.append(bounce(value, move_z, edge, None, member, pack_first, pack_last))
        pops = [field_ref[side, member] for member in range(19)]
        thrust_cell, _ = turbine_cells(field_ref[side, 19], thrust_ref, False)
        coefs = plane_coefs(pops, thrust_cell, None)
        lam, _ = plane_adjoint(mu, lambda index: coefs[index], wanted)
        for index, member in enumerate(wanted):
            edge_ref[side, index] = lam[member]

    def middle(plane, member):
        if plane >= width:
            return face_ref[0, X_UP.index(member)]
        if plane < 0:
            return face_ref[1, X_DOWN.index(member)]
        return mid_ref[member, plane]

    def middle_row(side, plane, member):
        index = (Y_UP, Y_DOWN)[side].index(member)
        return edge_ref[side, index, plane + 2 : plane + 3, :]

    for plane in range(width):
        mu = gather_mu(middle, middle_row, plane, first, last)
        lam, mx = plane_adjoint(mu, lambda index: early_ref[index, plane])
        for member in range(19):
            out_ref[member, plane] = lam[member]
        totals[plane] = totals[plane] + mx * early_ref[GAIN, plane]

    for side, (members, row) in enumerate(((Y_UP, 0), (Y_DOWN, span - 1))):
        for index, member in enumerate(members):
            start = (5 * side + index) * width
            next_ref[start : start + width, :] = out_ref[member, :, row, :]

    def roll_z(value, move):
        if move == 1:
            return jnp.where(last, 0.0, pltpu.roll(value, height - 1, 1))
        return jnp.where(first, 0.0, pltpu.roll(value, 1, 1))

    nothing = jnp.zeros((1, height), jnp.float32)
    up, down = [], []
    for plane in range(width):
        up.append(
            2.0 * out_ref[1, plane]
            + span_shift(out_ref[7, plane], 1, nothing)
            + span_shift(out_ref[9, plane], -1, nothing)
            + roll_z(out_ref[11, plane], 1)
            + roll_z(out_ref[13, plane], -1)
        )
        down.append(
            2.0 * out_ref[2, plane]
            + span_shift(out_ref[8, plane], -1, nothing)
            + span_shift(out_ref[10, plane], 1, nothing)
            + roll_z(out_ref[12, plane], -1)
            + roll_z(out_ref[14, plane], 1)
        )
    tiles = []
    for plane in range(-1, width + 1):
        value = None
        if plane + 1 < width:
            value = up[plane + 1]
        if plane >= 1:
            value = -down[plane - 1] if value is None else value - down[plane - 1]
        if plane < 0 or plane >= width:
            face = below_ref if plane < 0 else above_ref
            tiles.append((face[HALO + 20] * value, face[HALO + 19]))
            continue
        value = value + jnp.where(last, out_ref[12, plane] - out_ref[13, plane], 0.0)
        value = value + jnp.where(first, out_ref[14, plane] - out_ref[11, plane], 0.0)
        tiles.append((totals[plane] + fields_ref[20, plane] * value, fields_ref[19, plane]))
    for side, (upward, downward, row) in enumerate(((9, 8, span - 1), (7, 10, 0))):
        pack_ref[side, 0] = jnp.zeros(pack_ref.shape[2:], jnp.float32)
        pack_ref[side, 1] = jnp.zeros(pack_ref.shape[2:], jnp.float32)
        pack_ref[side, 0, 1 : width + 1, :] = out_ref[upward, :, row, :]
        pack_ref[side, 1, 3 : width + 3, :] = out_ref[downward, :, row, :]
        tiles.append(
            (
                (pack_ref[side, 0] - pack_ref[side, 1]) * field_ref[side, 20],
                field_ref[side, 19],
            )
        )
    start = 10 * width
    next_ref[start:, :] = jnp.zeros((next_ref.shape[0] - start, height), jnp.float32)
    for turbine in range(thrust_ref.shape[0]):
        row = None
        for value, ids in tiles:
            kept = jnp.sum(jnp.where(ids == float(turbine), value, 0.0), axis=0, keepdims=True)
            row = kept if row is None else row + kept
        next_ref[start + turbine : start + turbine + 1, :] = row


def by_parity(even):
    odd = lax.rem(lax.axis_index("gx"), 2) == 1
    pl.when(jnp.logical_not(odd))(lambda: even(True))
    pl.when(odd)(lambda: even(False))


def last_faces_kernel(lam_ref, rows_ref, sums_ref, near_ref, far_ref):
    width = lam_ref.shape[1]

    def row_of(side, plane, member):
        place = (5 * side + (Y_UP, Y_DOWN)[side].index(member)) * width + plane
        return rows_ref[place : place + 1, :]

    def write(even):
        outs = (far_ref, near_ref) if even else (near_ref, far_ref)
        for members, plane, out_ref in ((X_UP, 0, outs[0]), (X_DOWN, width - 1, outs[1])):
            for index, member in enumerate(members):
                move_y = VELOCITIES[member][1]
                value = lam_ref[member, plane]
                if move_y != 0:
                    value = span_shift(
                        value, move_y, row_of(0 if move_y == 1 else 1, plane, member)
                    )
                out_ref[index] = value

    by_parity(write)
    for tile in range(near_ref.shape[0] - 5):
        near_ref[5 + tile] = sums_ref[8 * tile : 8 * tile + 8, :]


def last_far_kernel(far_ref, near_ref, got_ref, out_ref):
    for tile in range(5):
        out_ref[tile] = far_ref[tile]
    for tile in range(5, out_ref.shape[0]):
        out_ref[tile] = near_ref[tile] + got_ref[tile]


def last_kernel(lam_ref, rows_ref, near_ref, far_ref, coef_ref, out_ref):
    width, span, height = lam_ref.shape[1:]
    lane = lax.broadcasted_iota(jnp.int32, (span, height), 1)
    first, last = lane == 0, lane == height - 1
    odd = jnp.full((span, height), lax.rem(lax.axis_index("gx"), 2)) == 1

    def source(plane, member):
        if plane >= width:
            index = X_UP.index(member)
            return jnp.where(odd, far_ref[index], near_ref[index])
        if plane < 0:
            index = X_DOWN.index(member)
            return jnp.where(odd, near_ref[index], far_ref[index])
        value, move_y = lam_ref[member, plane], VELOCITIES[member][1]
        if move_y == 0:
            return value
        side = 0 if move_y == 1 else 1
        place = (5 * side + (Y_UP, Y_DOWN)[side].index(member)) * width + plane
        return span_shift(value, move_y, rows_ref[place : place + 1, :])

    for plane in range(width):
        mu = []
        for member in range(19):
            move_x, _, move_z = VELOCITIES[member]
            value = source(plane + move_x, member)
            if move_z == 1:
                value = jnp.where(
                    last, lam_ref[OPPOSITE[member], plane], pltpu.roll(value, height - 1, 1)
                )
            elif move_z == -1:
                value = jnp.where(first, lam_ref[OPPOSITE[member], plane], pltpu.roll(value, 1, 1))
            mu.append(value)
        lam, _ = plane_adjoint(mu, lambda index: coef_ref[index, plane])
        for member in range(19):
            out_ref[member, plane] = lam[member]


def call(kernel, outs, *args, scratch=(), smem_first=False, micros=1):
    specs = [pl.BlockSpec(memory_space=VMEM)] * len(args)
    if smem_first:
        specs[0] = pl.BlockSpec(memory_space=pltpu.SMEM)
    return pl.pallas_call(
        kernel,
        out_shape=tuple(jax.ShapeDtypeStruct(shape, jnp.float32) for shape in outs),
        in_specs=specs,
        out_specs=tuple(pl.BlockSpec(memory_space=VMEM) for _ in outs),
        scratch_shapes=[pltpu.VMEM(shape, jnp.float32) for shape in scratch],
        cost_estimate=pl.CostEstimate(
            flops=int(1e6 * micros), bytes_accessed=int(2e6 * micros), transcendentals=0
        ),
        compiler_params=pltpu.CompilerParams(vmem_limit_bytes=32 * 1024 * 1024),
    )(*args)


def ring(axis, step):
    count = lax.axis_size(axis)
    return [(i, (i + step) % count) for i in range(count)]


def swap_rows(low, high):
    return lax.ppermute(low, "gy", ring("gy", -1)), lax.ppermute(high, "gy", ring("gy", 1))


def flips(value, axis, flip_list):
    count = lax.axis_size(axis)
    parts = [lax.ppermute(value, axis, [(i, i ^ flip) for i in range(count)]) for flip in flip_list]
    return sum(parts, value)


def sum_bits(value, axis, start):
    count = lax.axis_size(axis)
    while start < count:
        stop = min(4 * start, count)
        value = flips(value, axis, range(start, stop, start))
        start = stop
    return value


def last_exchange(lam, packed, turbine_rows, has_pairs):
    width, height = lam.shape[1], lam.shape[3]
    rows_count = 10 * width
    if lax.axis_size("gy") == 2:
        got = lax.ppermute(packed, "gy", ring("gy", 1))
        rows, sums = got, packed[rows_count:] + got[rows_count:]
    else:
        low, high = swap_rows(packed[: rows_count // 2], packed[rows_count // 2 : rows_count])
        rows = jnp.concatenate([low, high])
        count = lax.axis_size("gy")
        if count & (count - 1):
            sums = lax.psum(packed[rows_count:], "gy")
        else:
            sums = sum_bits(packed[rows_count:], "gy", 1)
    tiles = 5 + turbine_rows // 8
    near, far = call(
        last_faces_kernel,
        [(tiles, lam.shape[2], height), (5, lam.shape[2], height)],
        lam,
        rows,
        sums,
        micros=0.1,
    )
    count = lax.axis_size("gx")
    got_near = lax.ppermute(near, "gx", [(i, i ^ 1) for i in range(count)])
    (far,) = call(last_far_kernel, [near.shape], far, near, got_near, micros=0.1)
    got_far = lax.ppermute(
        far, "gx", [(i, (i + 1 if i % 2 else i - 1) % count) for i in range(count)]
    )
    sums = far[5:] + got_far[5:]
    if count & (count - 1):
        sums = 0.25 * lax.psum(sums, "gx")
    else:
        sums = sum_bits(sums, "gx", 4)
    return rows, got_near, got_far, sums.reshape(turbine_rows, height)


def shards(fwd_pops, fwd_scale, seed_adjoint, turbine_map, thrust):
    steps, _, width, span, height = fwd_pops.shape
    assert steps == 3 and span == 8
    turbines = thrust.shape[0]
    turbine_rows = -(-turbines // 8) * 8
    sublanes = -(-(width + 4) // 8) * 8
    whole = (19, width, span, height)
    static = (thrust, turbine_map, fwd_scale, fwd_pops)
    row_count = (HALO + FIELDS) * width
    fields, rows = call(
        lambda *refs: pack_kernel(steps - 1, *refs),
        [(FIELDS, width, span, height), (2, row_count, height)],
        *static,
        seed_adjoint,
        smem_first=True,
        micros=0.3,
    )
    if lax.axis_size("gy") == 2:
        rows = lax.ppermute(rows, "gy", ring("gy", 1))
    else:
        rows = jnp.stack(swap_rows(rows[0], rows[1]))
    coefs = call(
        coef_kernel,
        [(COEFS, width, span, height)] * steps,
        *static,
        smem_first=True,
        micros=1.5,
    )
    face = (FACE_TILES + -(-2 * (CORNER + FIELDS) // 8), span, height)
    low, high = call(faces_kernel, [face, face], seed_adjoint, fields, rows, micros=0.3)
    above = lax.ppermute(low, "gx", ring("gx", -1))
    below = lax.ppermute(high, "gx", ring("gx", 1))
    lam, packed = call(
        pair_kernel,
        [whole, (10 * width + turbine_rows, height)],
        thrust,
        seed_adjoint,
        rows,
        above,
        below,
        coefs[2],
        coefs[1],
        fields,
        scratch=[
            (2, len(PACK_LIST[0]), sublanes, height),
            (2, FIELDS, sublanes, height),
            whole,
            (2, 5, span, height),
            (2, 5, sublanes, height),
        ],
        smem_first=True,
        micros=1.5,
    )
    rows, near, far, sums = last_exchange(lam, packed, turbine_rows, True)
    (lam,) = call(last_kernel, [whole], lam, rows, near, far, coefs[0], micros=0.5)
    thrust_grad = jnp.sum(sums, axis=1)[:turbines]
    return (lam, thrust_grad)


def solution(mesh):
    placed = (
        P(None, None, "gx", "gy", None),
        P(None, "gx", "gy", None),
        P(None, "gx", "gy", None),
        P("gx", "gy", None),
        P(),
    )
    return jax.shard_map(
        shards,
        mesh=mesh,
        in_specs=placed,
        out_specs=(P(None, "gx", "gy", None), P()),
        check_vma=False,
    )
```

time: 46.7 us -> 44.2 us (0.946)
  waiting for transfers between devices: 24.9 us -> 20.5 us
  local copies, waits for them, and re-layouts: 0.99 us -> 4.76 us
  starting transfers between devices: 16.5 us -> 13.3 us
  Pallas kernels: 2.81 us -> 4.5 us
  other arithmetic: 0.64 us -> 0.09 us
    ppermute x15 -> x9, waiting for transfers between devices: 24.9 us -> 20.5 us  [the longest x1 5.1 us: last_exchange(): lax.ppermute(far, 'gx', [(i, (i + 1 if i % 2 else i - 1) % count) for i i...]
    unnamed x12 -> x14, local copies, waits for them, and re-layouts: 0.99 us -> 4.16 us
    ppermute x15 -> x9, starting transfers between devices: 16.5 us -> 13.3 us  [the longest x3 4.38 us: flips(): lax.ppermute(value, axis, [(i, i ^ flip) for i in range(count)])]
    pallas_call x8 -> x7, Pallas kernels: 2.81 us -> 4.5 us  [call(): pl.pallas_call(kernel, out_shape=tuple((jax.ShapeDtypeStruct(shape, jnp.f...]
    reduce_sum x0 -> x1, local copies, waits for them, and re-layouts: none -> 0.6 us  [shards(): thrust_grad = jnp.sum(sums, axis=1)[:turbines]]
    reduce_sum x1, other arithmetic: 0.62 us -> 0.09 us  [shards(): thrust_grad = jnp.sum(sums, axis=1)[:turbines]]
  transfers between devices with their start and end apart: 15 -> 9, of which waited for: 12 -> 8; matrix products, arithmetic and copies ran while one was open for 1% -> 0% of each run, Pallas kernels for 3% -> 5%
where the time goes in v2:
time: 44.2 us; the launch traced here: 43.9 us
  waiting for transfers between devices  20.5 us (46%)
  starting transfers between devices  13.3 us (30%)
  local copies, waits for them, and re-layouts  4.76 us (11%)
  Pallas kernels  4.5 us (10%)
  between operations  0.71 us (2%)
    ppermute x1, waiting for transfers between devices, last_exchange(): lax.ppermute(far, 'gx', [(i, (i + 1 if i % 2 else i - 1) % count) for i i...  5.1 us
    ppermute x1, waiting for transfers between devices, shards(): below = lax.ppermute(high, 'gx', ring('gx', 1))  4.6 us
    pallas_call x7, Pallas kernels, call(): pl.pallas_call(kernel, out_shape=tuple((jax.ShapeDtypeStruct(shape, jnp.f...  4.5 us
    ppermute x3, starting transfers between devices, flips(): lax.ppermute(value, axis, [(i, i ^ flip) for i in range(count)])  4.38 us
    ppermute x1, waiting for transfers between devices, shards(): rows = lax.ppermute(rows, 'gy', ring('gy', 1))  4.37 us
    unnamed x14, local copies, waits for them, and re-layouts  4.16 us
    ppermute x1, starting transfers between devices, shards(): above = lax.ppermute(low, 'gx', ring('gx', -1))  3.43 us
    ppermute x1, starting transfers between devices, shards(): rows = lax.ppermute(rows, 'gy', ring('gy', 1))  3 us
  transfers between devices with their start and end apart: 9, of which 8 were waited for; matrix products, arithmetic and copies ran while one was open for 0% of the time, Pallas kernels for 5%

profile of v2, /device:TPU:0, one launch (start us, length us, event | category | flops | bytes accessed | tf_op | source)
XLA Modules:
  0.0 43.9 jit_solution(14707156088330032187)
XLA Ops:
  0.6 0.0 copy-start
  0.6 1.0 %copy-done = f32[19,4,8,128]{3,2,1,0:T(8,128)S(1)} copy-done((f32[19,4,8,128]{3,2,1,0:T(8,128)S(1)}, f32[19,4,8,128]{3,2,1,0:T(8,128)}, u32[]{:S(2)}) %copy-start) | copy-done | bytes 311320
  1.6 0.0 copy-start.2
  1.6 1.0 %copy-done.2 = bf16[3,19,4,8,128]{4,3,2,1,0:T(8,128)(2,1)S(1)} copy-done((bf16[3,19,4,8,128]{4,3,2,1,0:T(8,128)(2,1)S(1)}, bf16[3,19,4,8,128]{4,3,2,1,0:T(8,128)(2,1)}, u32[]{:S(2)}) %copy-start.2) | copy-done | bytes 466968
  2.6 0.0 copy-start.4
  2.6 0.8 %copy-done.4 = f32[3,4,8,128]{3,2,1,0:T(8,128)S(1)} copy-done((f32[3,4,8,128]{3,2,1,0:T(8,128)S(1)}, f32[3,4,8,128]{3,2,1,0:T(8,128)}, u32[]{:S(2)}) %copy-start.4) | copy-done | bytes 49176
  3.4 0.0 copy-start.5
  3.4 0.7 %copy-done.5 = s32[4,8,128]{2,1,0:T(8,128)S(1)} copy-done((s32[4,8,128]{2,1,0:T(8,128)S(1)}, s32[4,8,128]{2,1,0:T(8,128)}, u32[]{:S(2)}) %copy-start.5) | copy-done | bytes 16408
  4.1 0.0 copy-start.6
  4.1 0.7 %copy-done.6 = f32[10]{0:T(128)S(1)} copy-done((f32[10]{0:T(128)S(1)}, f32[10]{0:T(128)}, u32[]{:S(2)}) %copy-start.6) | copy-done | bytes 64
  4.8 0.0 copy-start.1
  4.8 0.8 %shard_map.68 = (f32[21,4,8,128]{3,2,1,0:T(8,128)S(1)}, f32[2,168,128]{2,1,0:T(8,128)S(1)}) custom-call(f32[10]{0:T(128)S(1)} %copy-done.6, s32[4,8,128]{2,1,0:T(8,128)S(1)} %copy-done.5, f32[3,4,8,128]{3,2,1,0:T(8,128)S(1)} %copy-done.4, bf16[3,19,4,8,128]{4,3,2,1,0:T(8,128)(2,1)S(1)} %copy-done.2, f32[19,4,8,128]{3,2,1,0:T(8,128)S(1)} %copy-done), custom_call_target="tpu_custom_call" | custom-call | flops 300000 | bytes 600000 | tf_op jit(solution)/shard_map/pallas_call | solution.py:583
  5.6 0.0 copy-start.3
  5.6 3.0 %collective-permute-start = (f32[2,168,128]{2,1,0:T(8,128)S(1)}, f32[2,168,128]{2,1,0:T(8,128)S(1)}, u32[]{:S(2)}, u32[]{:S(2)}) collective-permute-start(f32[2,168,128]{2,1,0:T(8,128)S(1)} %get-tuple-element.13), channel_id=1, source_target_pairs={{0,1},{1,0},{2,3},{3,2},{4,5},{5,4},{6,7},{7,6},{8,9},{9,8},{10,11... | collective-permute-start | bytes 516104 | tf_op jit(solution)/shard_map/ppermute | solution.py:675
  8.6 4.4 %collective-permute-done.rows_ref = f32[2,168,128]{2,1,0:T(8,128)S(1)} collective-permute-done((f32[2,168,128]{2,1,0:T(8,128)S(1)}, f32[2,168,128]{2,1,0:T(8,128)S(1)}, u32[]{:S(2)}, u32[]{:S(2)}) %collective-permute-start) | collective-permute-done | bytes 172064 | tf_op jit(solution)/shard_map/ppermute | solution.py:675
  13.0 0.0 copy-done.1
  13.0 0.1 shard_map.69
  13.0 3.4 %collective-permute-start.1 = (f32[53,8,128]{2,1,0:T(8,128)S(1)}, f32[53,8,128]{2,1,0:T(8,128)S(1)}, u32[]{:S(2)}, u32[]{:S(2)}) collective-permute-start(f32[53,8,128]{2,1,0:T(8,128)S(1)} %get-tuple-element.15), channel_id=1, source_target_pairs={{0,30},{2,0},{4,2},{6,4},{8,6},{10,8},{12,10},{14,12},{16,14},{18,... | collective-permute-start | bytes 651272 | tf_op jit(solution)/shard_map/ppermute | solution.py:687
  16.5 0.0 collective-permute-start.2
  16.5 0.0 copy-done.3
  16.5 1.3 %shard_map.70 = (f32[42,4,8,128]{3,2,1,0:T(8,128)S(1)}, f32[42,4,8,128]{3,2,1,0:T(8,128)S(1)}, f32[42,4,8,128]{3,2,1,0:T(8,128)S(1)}) custom-call(f32[10]{0:T(128)S(1)} %copy-done.6, s32[4,8,128]{2,1,0:T(8,128)S(1)} %copy-done.5, f32[3,4,8,128]{3,2,1,0:T(8,128)S(1)} %copy-done.4, bf16[3,19,4,8,128]{4,3,2,1,0:T(8,128)(2,1)S(1)} %copy-done.3), custom_call_target="tpu_custom_call" | custom-call | flops 1500000 | bytes 3000000 | tf_op jit(solution)/shard_map/pallas_call | solution.py:583
  17.7 2.1 %collective-permute-done.1.above_ref = f32[53,8,128]{2,1,0:T(8,128)S(1)} collective-permute-done((f32[53,8,128]{2,1,0:T(8,128)S(1)}, f32[53,8,128]{2,1,0:T(8,128)S(1)}, u32[]{:S(2)}, u32[]{:S(2)}) %collective-permute-start.1) | collective-permute-done | bytes 217120 | tf_op jit(solution)/shard_map/ppermute | solution.py:687
  19.9 4.6 %collective-permute-done.2.below_ref = f32[53,8,128]{2,1,0:T(8,128)S(1)} collective-permute-done((f32[53,8,128]{2,1,0:T(8,128)S(1)}, f32[53,8,128]{2,1,0:T(8,128)S(1)}, u32[]{:S(2)}, u32[]{:S(2)}) %collective-permute-start.2) | collective-permute-done | bytes 217120 | tf_op jit(solution)/shard_map/ppermute | solution.py:688
  24.5 1.4 %shard_map.71 = (f32[19,4,8,128]{3,2,1,0:T(8,128)S(1)}, f32[56,128]{1,0:T(8,128)S(1)}) custom-call(f32[10]{0:T(128)S(1)} %copy-done.6, f32[19,4,8,128]{3,2,1,0:T(8,128)S(1)} %copy-done.1, f32[2,168,128]{2,1,0:T(8,128)S(1)} %collective-permute-done.rows_ref, f32[53,8,128]{2,1,0:T(8,128)S(1)} %collective-permute-done.1.above_ref, ...), custom_call_target="tpu_custom_call" | custom-call | flops 1500000 | bytes 3000000 | tf_op jit(solution)/shard_map/pallas_call | solution.py:583
  25.9 1.6 %collective-permute-start.3 = (f32[56,128]{1,0:T(8,128)S(1)}, f32[56,128]{1,0:T(8,128)S(1)}, u32[]{:S(2)}, u32[]{:S(2)}) collective-permute-start(f32[56,128]{1,0:T(8,128)S(1)} %get-tuple-element.20), channel_id=1, source_target_pairs={{0,1},{1,0},{2,3},{3,2},{4,5},{5,4},{6,7},{7,6},{8,9},{9,8},{10,11... | collective-permute-start | bytes 86024 | tf_op jit(solution)/shard_map/ppermute | solution.py:624
  27.5 2.4 %collective-permute-done.3.rows_ref = f32[56,128]{1,0:T(8,128)S(1)} collective-permute-done((f32[56,128]{1,0:T(8,128)S(1)}, f32[56,128]{1,0:T(8,128)S(1)}, u32[]{:S(2)}, u32[]{:S(2)}) %collective-permute-start.3) | collective-permute-done | bytes 28704 | tf_op jit(solution)/shard_map/ppermute | solution.py:624
  29.9 0.1 collective-permute-start.4
  30.0 1.2 %collective-permute-done.4.got_ref.near_ref = f32[7,8,128]{2,1,0:T(8,128)S(1)} collective-permute-done((f32[7,8,128]{2,1,0:T(8,128)S(1)}, f32[7,8,128]{2,1,0:T(8,128)S(1)}, u32[]{:S(2)}, u32[]{:S(2)}) %collective-permute-start.4) | collective-permute-done | bytes 28704 | tf_op jit(solution)/shard_map/ppermute | solution.py:644
  31.2 0.9 %collective-permute-start.5 = (f32[7,8,128]{2,1,0:T(8,128)S(1)}, f32[7,8,128]{2,1,0:T(8,128)S(1)}, u32[]{:S(2)}, u32[]{:S(2)}) collective-permute-start(f32[7,8,128]{2,1,0:T(8,128)S(1)} %shard_map.73), channel_id=1, source_target_pairs={{0,30},{2,4},{4,2},{6,8},{8,6},{10,12},{12,10},{14,16},{16,14},{18... | collective-permute-start | bytes 86024 | tf_op jit(solution)/shard_map/ppermute | solution.py:646
  32.1 5.1 %collective-permute-done.5.far_ref = f32[7,8,128]{2,1,0:T(8,128)S(1)} collective-permute-done((f32[7,8,128]{2,1,0:T(8,128)S(1)}, f32[7,8,128]{2,1,0:T(8,128)S(1)}, u32[]{:S(2)}, u32[]{:S(2)}) %collective-permute-start.5) | collective-permute-done | bytes 28704 | tf_op jit(solution)/shard_map/ppermute | solution.py:646
  37.2 0.0 collective-permute-start.8
  37.2 0.0 collective-permute-start.7
  37.2 4.4 %collective-permute-start.6 = (f32[2,8,128]{2,1,0:T(8,128)S(1)}, f32[2,8,128]{2,1,0:T(8,128)S(1)}, u32[]{:S(2)}, u32[]{:S(2)}) collective-permute-start(f32[2,8,128]{2,1,0:T(8,128)S(1)} %slice_add_fusion), channel_id=1, source_target_pairs={{0,8},{2,10},{4,12},{6,14},{8,0},{10,2},{12,4},{14,6},{16,24},{18,... | collective-permute-start | bytes 24584 | tf_op jit(solution)/shard_map/ppermute | solution.py:607
  41.5 0.9 %shard_map.74 = f32[19,4,8,128]{3,2,1,0:T(8,128)} custom-call(f32[19,4,8,128]{3,2,1,0:T(8,128)S(1)} %get-tuple-element.19.lam_ref, f32[56,128]{1,0:T(8,128)S(1)} %collective-permute-done.3.rows_ref, f32[7,8,128]{2,1,0:T(8,128)S(1)} %collective-permute-done.4.got_ref.near_ref, f32[7,8,128]{2,1,0:T(8,128)S(1)} %collective-permute-done.5.far_ref, ...), custom_call_target="tpu_custom_call" | custom-call | flops 500000 | bytes 1000000 | tf_op jit(solution)/shard_map/pallas_call | solution.py:583
  42.5 0.1 collective-permute-done.8
  42.6 0.0 collective-permute-done.7
  42.6 0.6 %collective-permute-done.6 = f32[2,8,128]{2,1,0:T(8,128)S(1)} collective-permute-done((f32[2,8,128]{2,1,0:T(8,128)S(1)}, f32[2,8,128]{2,1,0:T(8,128)S(1)}, u32[]{:S(2)}, u32[]{:S(2)}) %collective-permute-start.6) | collective-permute-done | bytes 8224 | tf_op jit(solution)/shard_map/ppermute | solution.py:607
  43.2 0.1 add_reduce_fusion
  43.3 0.6 %reduce_sum.12 = f32[16]{0:T(128)} reshape(f32[2,8]{1,0:T(2,128)S(1)} %add_reduce_fusion) | data formatting | bytes 128 | tf_op jit(solution)/shard_map/reduce_sum | solution.py:712
  (4 shorter events, 0.0 us)
Async XLA Ops:
  0.6 1.0 %copy-start = (f32[19,4,8,128]{3,2,1,0:T(8,128)S(1)}, f32[19,4,8,128]{3,2,1,0:T(8,128)}, u32[]{:S(2)}) copy-start(f32[19,4,8,128]{3,2,1,0:T(8,128)} %lam_ref.3) | copy-start | bytes 933892
  1.6 1.0 %copy-start.2 = (bf16[3,19,4,8,128]{4,3,2,1,0:T(8,128)(2,1)S(1)}, bf16[3,19,4,8,128]{4,3,2,1,0:T(8,128)(2,1)}, u32[]{:S(2)}) copy-start(bf16[3,19,4,8,128]{4,3,2,1,0:T(8,128)(2,1)} %pops_ref.1) | copy-start | bytes 1400836
  2.6 0.8 %copy-start.4 = (f32[3,4,8,128]{3,2,1,0:T(8,128)S(1)}, f32[3,4,8,128]{3,2,1,0:T(8,128)}, u32[]{:S(2)}) copy-start(f32[3,4,8,128]{3,2,1,0:T(8,128)} %scale_ref.1) | copy-start | bytes 147460
  3.4 0.7 %copy-start.5 = (s32[4,8,128]{2,1,0:T(8,128)S(1)}, s32[4,8,128]{2,1,0:T(8,128)}, u32[]{:S(2)}) copy-start(s32[4,8,128]{2,1,0:T(8,128)} %map_ref.1) | copy-start | bytes 49156
  4.1 0.7 %copy-start.6 = (f32[10]{0:T(128)S(1)}, f32[10]{0:T(128)}, u32[]{:S(2)}) copy-start(f32[10]{0:T(128)} %thrust_ref.3) | copy-start | bytes 124
  4.8 8.2 %copy-start.1 = (f32[19,4,8,128]{3,2,1,0:T(8,128)S(1)}, f32[19,4,8,128]{3,2,1,0:T(8,128)}, u32[]{:S(2)}) copy-start(f32[19,4,8,128]{3,2,1,0:T(8,128)} %lam_ref.3) | copy-start | bytes 933892
  5.6 10.9 %copy-start.3 = (bf16[3,19,4,8,128]{4,3,2,1,0:T(8,128)(2,1)S(1)}, bf16[3,19,4,8,128]{4,3,2,1,0:T(8,128)(2,1)}, u32[]{:S(2)}) copy-start(bf16[3,19,4,8,128]{4,3,2,1,0:T(8,128)(2,1)} %pops_ref.1) | copy-start | bytes 1400836
  5.6 7.4 %collective-permute-start = (f32[2,168,128]{2,1,0:T(8,128)S(1)}, f32[2,168,128]{2,1,0:T(8,128)S(1)}, u32[]{:S(2)}, u32[]{:S(2)}) collective-permute-start(f32[2,168,128]{2,1,0:T(8,128)S(1)} %get-tuple-element.13), channel_id=1, source_target_pairs={{0,1},{1,0},{2,3},{3,2},{4,5},{5,4},{6,7},{7,6},{8,9},{9,8},{10,11... | collective-permute-start | bytes 516104 | tf_op jit(solution)/shard_map/ppermute | solution.py:675
  13.0 6.8 %collective-permute-start.1 = (f32[53,8,128]{2,1,0:T(8,128)S(1)}, f32[53,8,128]{2,1,0:T(8,128)S(1)}, u32[]{:S(2)}, u32[]{:S(2)}) collective-permute-start(f32[53,8,128]{2,1,0:T(8,128)S(1)} %get-tuple-element.15), channel_id=1, source_target_pairs={{0,30},{2,0},{4,2},{6,4},{8,6},{10,8},{12,10},{14,12},{16,14},{18,... | collective-permute-start | bytes 651272 | tf_op jit(solution)/shard_map/ppermute | solution.py:687
  16.5 8.0 %collective-permute-start.2 = (f32[53,8,128]{2,1,0:T(8,128)S(1)}, f32[53,8,128]{2,1,0:T(8,128)S(1)}, u32[]{:S(2)}, u32[]{:S(2)}) collective-permute-start(f32[53,8,128]{2,1,0:T(8,128)S(1)} %get-tuple-element.16), channel_id=1, source_target_pairs={{0,2},{2,4},{4,6},{6,8},{8,10},{10,12},{12,14},{14,16},{16,18},{18... | collective-permute-start | bytes 651272 | tf_op jit(solution)/shard_map/ppermute | solution.py:688
  25.9 3.9 %collective-permute-start.3 = (f32[56,128]{1,0:T(8,128)S(1)}, f32[56,128]{1,0:T(8,128)S(1)}, u32[]{:S(2)}, u32[]{:S(2)}) collective-permute-start(f32[56,128]{1,0:T(8,128)S(1)} %get-tuple-element.20), channel_id=1, source_target_pairs={{0,1},{1,0},{2,3},{3,2},{4,5},{5,4},{6,7},{7,6},{8,9},{9,8},{10,11... | collective-permute-start | bytes 86024 | tf_op jit(solution)/shard_map/ppermute | solution.py:624
  29.9 1.3 %collective-permute-start.4 = (f32[7,8,128]{2,1,0:T(8,128)S(1)}, f32[7,8,128]{2,1,0:T(8,128)S(1)}, u32[]{:S(2)}, u32[]{:S(2)}) collective-permute-start(f32[7,8,128]{2,1,0:T(8,128)S(1)} %get-tuple-element.21.near_ref), channel_id=1, source_target_pairs={{0,2},{2,0},{4,6},{6,4},{8,10},{10,8},{12,14},{14,12},{16,18},{18,... | collective-permute-start | bytes 86024 | tf_op jit(solution)/shard_map/ppermute | solution.py:644
  31.2 6.0 %collective-permute-start.5 = (f32[7,8,128]{2,1,0:T(8,128)S(1)}, f32[7,8,128]{2,1,0:T(8,128)S(1)}, u32[]{:S(2)}, u32[]{:S(2)}) collective-permute-start(f32[7,8,128]{2,1,0:T(8,128)S(1)} %shard_map.73), channel_id=1, source_target_pairs={{0,30},{2,4},{4,2},{6,8},{8,6},{10,12},{12,10},{14,16},{16,14},{18... | collective-permute-start | bytes 86024 | tf_op jit(solution)/shard_map/ppermute | solution.py:646
  37.2 5.4 %collective-permute-start.8 = (f32[2,8,128]{2,1,0:T(8,128)S(1)}, f32[2,8,128]{2,1,0:T(8,128)S(1)}, u32[]{:S(2)}, u32[]{:S(2)}) collective-permute-start(f32[2,8,128]{2,1,0:T(8,128)S(1)} %slice_add_fusion), channel_id=1, source_target_pairs={{0,24},{2,26},{4,28},{6,30},{8,16},{10,18},{12,20},{14,22},{16,8},... | collective-permute-start | bytes 24584 | tf_op jit(solution)/shard_map/ppermute | solution.py:607
  37.2 5.4 %collective-permute-start.7 = (f32[2,8,128]{2,1,0:T(8,128)S(1)}, f32[2,8,128]{2,1,0:T(8,128)S(1)}, u32[]{:S(2)}, u32[]{:S(2)}) collective-permute-start(f32[2,8,128]{2,1,0:T(8,128)S(1)} %slice_add_fusion), channel_id=1, source_target_pairs={{0,16},{2,18},{4,20},{6,22},{8,24},{10,26},{12,28},{14,30},{16,0},... | collective-permute-start | bytes 24584 | tf_op jit(solution)/shard_map/ppermute | solution.py:607
  37.2 6.0 %collective-permute-start.6 = (f32[2,8,128]{2,1,0:T(8,128)S(1)}, f32[2,8,128]{2,1,0:T(8,128)S(1)}, u32[]{:S(2)}, u32[]{:S(2)}) collective-permute-start(f32[2,8,128]{2,1,0:T(8,128)S(1)} %slice_add_fusion), channel_id=1, source_target_pairs={{0,8},{2,10},{4,12},{6,14},{8,0},{10,2},{12,4},{14,6},{16,24},{18,... | collective-permute-start | bytes 24584 | tf_op jit(solution)/shard_map/ppermute | solution.py:607

commit v3 on v2

v3 whole, which is shorter than its diff:
```python
import jax
import jax.numpy as jnp
from jax import lax
from jax.experimental import pallas as pl
from jax.experimental.pallas import tpu as pltpu
from jax.sharding import PartitionSpec as P

VELOCITIES = (
    (0, 0, 0),
    (1, 0, 0),
    (-1, 0, 0),
    (0, 1, 0),
    (0, -1, 0),
    (0, 0, 1),
    (0, 0, -1),
    (1, 1, 0),
    (-1, -1, 0),
    (1, -1, 0),
    (-1, 1, 0),
    (1, 0, 1),
    (-1, 0, -1),
    (1, 0, -1),
    (-1, 0, 1),
    (0, 1, 1),
    (0, -1, -1),
    (0, 1, -1),
    (0, -1, 1),
)
OPPOSITE = (0, 2, 1, 4, 3, 6, 5, 8, 7, 10, 9, 12, 11, 14, 13, 16, 15, 18, 17)
WEIGHTS = tuple([1.0 / 3.0] + [1.0 / 18.0] * 6 + [1.0 / 36.0] * 12)
MEAN_FLOW = 0.1
TAU_BASE = 0.51
SMAG_COEF = 18.0 * 1.4142135623730951 * 0.17 * 0.17
QUAD_FLOOR = 0.0001

X_UP = (1, 7, 9, 11, 13)
X_DOWN = (2, 8, 10, 12, 14)
Y_UP = (3, 7, 10, 15, 17)
Y_DOWN = (4, 8, 9, 16, 18)

KEEP, MASS, FLUX, UX, UY, UZ, Q1 = 19, 20, 21, 22, 23, 24, 25
RATE, BULK, PX, PY, PZ, DRAG, DRAG_U, GAIN = 34, 35, 36, 37, 38, 39, 40, 41
COEFS = 42

FIELDS = 21

VMEM = pltpu.VMEM


def halo_list(axis, sign):
    near = [
        (1, m) for m in range(19) if VELOCITIES[m][axis] * sign >= 0 or VELOCITIES[m][2] != 0
    ]
    return near + [(2, m) for m in range(19) if VELOCITIES[m][axis] * sign == 1]


SIGNS = (1, -1)
ROW_LIST = [halo_list(1, sign) for sign in SIGNS]
INNER_LIST = [[(0, m) for m in range(19) if VELOCITIES[m][1] * sign == -1] for sign in SIGNS]
PACK_LIST = [ROW_LIST[side] + INNER_LIST[side] for side in range(2)]
HALO = len(ROW_LIST[0])
CORNER = 6 + FIELDS
FACE_TILES = 10 + -(-2 * CORNER // 8)


def base_values():
    values = []
    for member in range(19):
        along = float(VELOCITIES[member][0])
        values.append(
            WEIGHTS[member]
            * (
                1.0
                + 3.0 * MEAN_FLOW * along
                + 4.5 * MEAN_FLOW * MEAN_FLOW * along * along
                - 1.5 * MEAN_FLOW * MEAN_FLOW
            )
        )
    return values


def plane_coefs(pops, thrust_cell):
    rho = pops[0]
    for member in range(1, 19):
        rho = rho + pops[member]
    inv_rho = 1.0 / rho
    vel = []
    for axis_id in range(3):
        moment = None
        for member in range(19):
            component = VELOCITIES[member][axis_id]
            if component == 1:
                moment = pops[member] if moment is None else moment + pops[member]
            elif component == -1:
                moment = moment - pops[member]
        vel.append(moment * inv_rho)
    ux, uy, uz = vel
    speed_sq = ux * ux + uy * uy + uz * uz
    rest = 1.0 - 1.5 * speed_sq
    part = []
    for member in range(19):
        if member == 0:
            part.append(pops[0] - (WEIGHTS[0] * rho) * rest)
            continue
        proj = None
        for axis_id in range(3):
            component = VELOCITIES[member][axis_id]
            if component == 1:
                proj = vel[axis_id] if proj is None else proj + vel[axis_id]
            elif component == -1:
                proj = -vel[axis_id] if proj is None else proj - vel[axis_id]
        part.append(pops[member] - (WEIGHTS[member] * rho) * (rest + 3.0 * proj + 4.5 * proj * proj))

    def pair(member):
        return part[member] + part[member + 1]

    in_xy, in_xz, in_yz = pair(7) + pair(9), pair(11) + pair(13), pair(15) + pair(17)
    pxx, pyy, pzz = pair(1) + in_xy + in_xz, pair(3) + in_xy + in_yz, pair(5) + in_xz + in_yz
    pxy, pxz, pyz = pair(7) - pair(9), pair(11) - pair(13), pair(15) - pair(17)
    square = (
        pxx * pxx + pyy * pyy + pzz * pzz + 2.0 * (pxy * pxy + pxz * pxz + pyz * pyz) + QUAD_FLOOR
    )
    size = jnp.sqrt(square)
    root = jnp.sqrt(TAU_BASE * TAU_BASE + SMAG_COEF * size * inv_rho)
    omega = 1.0 / (0.5 * (TAU_BASE + root))
    pux = pxx * ux + pxy * uy + pxz * uz
    puy = pxy * ux + pyy * uy + pyz * uz
    puz = pxz * ux + pyz * uy + pzz * uz
    flux = omega * (3.0 / 36.0)
    drag = (3.0 / 36.0) * thrust_cell * jnp.abs(ux) * inv_rho
    result = list(part)
    result.append(1.0 - omega)
    result.append((omega * (1.0 / 36.0)) * (1.0 + 1.5 * speed_sq))
    result.append(flux)
    result.extend(vel)
    result.extend((pxx, pyy, pzz))
    result.extend((pxx + pyy + 2.0 * pxy, pxx + pyy - 2.0 * pxy))
    result.extend((pxx + pzz + 2.0 * pxz, pxx + pzz - 2.0 * pxz))
    result.extend((pyy + pzz + 2.0 * pyz, pyy + pzz - 2.0 * pyz))
    result.append((0.25 * SMAG_COEF) * omega * omega * inv_rho / (root * size))
    result.append(
        (pux * ux + puy * uy + puz * uz) - (pxx + pyy + pzz) * (1.0 / 3.0) - square * inv_rho
    )
    result.extend((-2.0 * pux, -2.0 * puy, -2.0 * puz))
    result.append(drag)
    result.append(drag * ux)
    result.append((-1.5 / 36.0) * ux * jnp.abs(ux))
    return result


def plus(*values):
    kept = [value for value in values if value is not None]
    return sum(kept[1:], kept[0]) if kept else None


def minus(left, right):
    if right is None:
        return left
    return -right if left is None else left - right


def times(left, right):
    return None if left is None or right is None else left * right


def plane_adjoint(mu, coef, wanted=range(19)):
    total, diff = {}, {}
    for member in range(1, 19, 2):
        total[member] = plus(mu[member], mu[member + 1])
        diff[member] = minus(mu[member], mu[member + 1])
    two_x, two_y, two_z = times(total[1], 2.0), times(total[3], 2.0), times(total[5], 2.0)
    in_xy, in_xz = plus(total[7], total[9]), plus(total[11], total[13])
    in_yz = plus(total[15], total[17])
    mxx, myy, mzz = plus(two_x, in_xy, in_xz), plus(two_y, in_xy, in_yz), plus(two_z, in_xz, in_yz)
    mxy, mxz = minus(total[7], total[9]), minus(total[11], total[13])
    myz = minus(total[15], total[17])
    m0 = plus(times(mu[0], 12.0), plus(two_x, two_y, two_z), plus(in_xy, in_xz, in_yz))
    mx = plus(times(diff[1], 2.0), plus(diff[7], diff[9]), plus(diff[11], diff[13]))
    my = plus(times(diff[3], 2.0), minus(diff[7], diff[9]), plus(diff[15], diff[17]))
    mz = plus(times(diff[5], 2.0), minus(diff[11], diff[13]), minus(diff[15], diff[17]))
    ux, uy, uz = coef(UX), coef(UY), coef(UZ)
    vx = plus(times(mxx, ux), times(mxy, uy), times(mxz, uz))
    vy = plus(times(mxy, ux), times(myy, uy), times(myz, uz))
    vz = plus(times(mxz, ux), times(myz, uy), times(mzz, uz))
    along = [mu[member] * coef(member) for member in range(19) if mu[member] is not None]
    while len(along) > 1:
        along = [
            along[k] + along[k + 1] if k + 1 < len(along) else along[k]
            for k in range(0, len(along), 2)
        ]
    gamma = along[0] * coef(RATE)
    flux = coef(FLUX)
    alpha = (
        coef(MASS) * m0
        - 1.5 * flux * (vx * ux + vy * uy + vz * uz)
        + gamma * coef(BULK)
        + mx * coef(DRAG_U)
    )
    beta_x = flux * (plus(mx, 3.0 * vx) - ux * m0) + gamma * coef(PX) - mx * coef(DRAG)
    beta_y = flux * (plus(my, 3.0 * vy) - uy * m0) + gamma * coef(PY)
    beta_z = flux * (plus(mz, 3.0 * vz) - uz * m0) + gamma * coef(PZ)
    keep = coef(KEEP)
    odd = {
        1: beta_x,
        3: beta_y,
        5: beta_z,
        7: beta_x + beta_y,
        9: beta_x - beta_y,
        11: beta_x + beta_z,
        13: beta_x - beta_z,
        15: beta_y + beta_z,
        17: beta_y - beta_z,
    }
    result = {}
    for member in wanted:
        if member == 0:
            result[0] = plus(times(mu[0], keep), alpha)
            continue
        forward = member - 1 + member % 2
        even = alpha + gamma * coef(Q1 + forward // 2)
        rest = even + odd[forward] if member == forward else even - odd[forward]
        result[member] = plus(times(mu[member], keep), rest)
    return result, mx


def turbine_cells(ids, thrust_ref):
    ratio = jnp.zeros(ids.shape, jnp.float32)
    for turbine in range(thrust_ref.shape[0]):
        ratio = jnp.where(ids == jnp.asarray(turbine, ids.dtype), thrust_ref[turbine], ratio)
    return jnp.where(ids >= 0, local_thrust(ratio), 0.0)


def local_thrust(values):
    return 4.0 * values / jnp.square(1.0 + jnp.sqrt(1.0 - values))


def decode(scale_ref, pops_ref, instant, plane):
    base = base_values()
    scale = scale_ref[instant, plane]
    return [
        base[member] * (1.0 + scale * pops_ref[instant, member, plane].astype(jnp.float32))
        for member in range(19)
    ]


def coef_kernel(thrust_ref, map_ref, scale_ref, pops_ref, _, *out_refs):
    for plane in range(pops_ref.shape[2]):
        thrust_cell = turbine_cells(map_ref[plane], thrust_ref)
        for instant, out_ref in enumerate(out_refs):
            pops = decode(scale_ref, pops_ref, instant, plane)
            for index, value in enumerate(plane_coefs(pops, thrust_cell)):
                out_ref[index, plane] = value


def edge_coef_kernel(thrust_ref, fields_ref, out_ref):
    for index, plane in enumerate((0, fields_ref.shape[1] - 1)):
        pops = [fields_ref[member, plane] for member in range(19)]
        coefs = plane_coefs(pops, turbine_cells(fields_ref[19, plane], thrust_ref))
        for coef, value in enumerate(coefs):
            out_ref[coef, index] = value


def by_parity(even):
    odd = lax.rem(lax.axis_index("gx"), 2) == 1
    pl.when(jnp.logical_not(odd))(lambda: even(True))
    pl.when(odd)(lambda: even(False))


def hand_out(low, high, near_ref, far_ref):
    def write(even):
        for source, out_ref in ((low, far_ref), (high, near_ref)) if even else ((low, near_ref), (high, far_ref)):
            for index in range(out_ref.shape[0]):
                out_ref[index] = source(index)

    by_parity(write)


def take_in(near_ref, far_ref, above_ref, below_ref):
    def write(even):
        for source, out_ref in ((near_ref, above_ref if even else below_ref), (far_ref, below_ref if even else above_ref)):
            for index in range(out_ref.shape[0]):
                out_ref[index] = source[index]

    by_parity(write)


def start_kernel(out_ref):
    out_ref[...] = jnp.zeros(out_ref.shape, jnp.float32)


def pack_kernel(_, map_ref, scale_ref, pops_ref, lam_ref, fields_ref, rows_ref, near_ref, far_ref):
    width, span = lam_ref.shape[1], lam_ref.shape[2]
    for side in range(2):
        for index, (far, member) in enumerate(ROW_LIST[side]):
            row = far - 1 if side == 0 else span - far
            rows_ref[side, index * width : (index + 1) * width, :] = lam_ref[member, :, row, :]
    last = pops_ref.shape[0] - 1
    for plane in range(width):
        for index, value in enumerate(decode(scale_ref, pops_ref, last, plane)):
            fields_ref[index, plane] = value
        fields_ref[19, plane] = map_ref[plane].astype(jnp.float32)
        pops = decode(scale_ref, pops_ref, 0, plane)
        rho, momentum = pops[0], None
        for member in range(1, 19):
            rho = rho + pops[member]
        for member in X_UP:
            pair = pops[member] - pops[member + 1]
            momentum = pair if momentum is None else momentum + pair
        ux = momentum / rho
        fields_ref[20, plane] = (-1.5 / 36.0) * ux * jnp.abs(ux)
    for side in range(2):
        row = 0 if side == 0 else span - 1
        for field in range(FIELDS):
            start = (HALO + field) * width
            rows_ref[side, start : start + width, :] = fields_ref[field, :, row, :]
    hand_out(
        lambda field: fields_ref[field, 0],
        lambda field: fields_ref[field, width - 1],
        near_ref,
        far_ref,
    )


def span_shift(value, move, row):
    span = value.shape[0]
    place = lax.broadcasted_iota(jnp.int32, value.shape, 0)
    if move == 1:
        return jnp.where(place == span - 1, row, pltpu.roll(value, span - 1, 0))
    return jnp.where(place == 0, row, pltpu.roll(value, 1, 0))


def roll_z(value, move, edges, walls=None):
    height = value.shape[1]
    if move == 0:
        return value
    shift, edge = (height - 1, edges[1]) if move == 1 else (1, edges[0])
    return jnp.where(edge, 0.0 if walls is None else walls, pltpu.roll(value, shift, 1))


def wall_masks(shape):
    lane = lax.broadcasted_iota(jnp.int32, shape, 1)
    return lane == 0, lane == shape[1] - 1


def gather_mu(source, row_of, plane, edges):
    mu = []
    for member in range(19):
        move_x, move_y, move_z = VELOCITIES[member]
        value = source(plane + move_x, member)
        if value is not None and move_y != 0:
            side = 0 if move_y == 1 else 1
            value = span_shift(value, move_y, row_of(side, plane + move_x, member))
        if move_z != 0:
            walls = source(plane, OPPOSITE[member])
            if value is None:
                value = jnp.where(edges[1 if move_z == 1 else 0], walls, 0.0)
            else:
                value = roll_z(value, move_z, edges, walls)
        mu.append(value)
    return mu


def own_lam(lam_ref):
    def source(plane, member):
        return lam_ref[member, plane] if 0 <= plane < lam_ref.shape[1] else None

    return source


def got_row(rows_ref, width):
    def row_of(side, plane, member):
        place = ROW_LIST[side].index((1, member)) * width + plane
        return rows_ref[side, place : place + 1, :]

    return row_of


def corner_row(face_ref, side, index):
    slot = side * CORNER + index
    return face_ref[10 + slot // 8, slot % 8 : slot % 8 + 1, :]


def faces_kernel(thrust_ref, lam_ref, rows_ref, coef_ref, near_ref, far_ref, field_ref, part_ref, pack_ref, low_ref, high_ref):
    width, span = lam_ref.shape[1], lam_ref.shape[2]
    edges = wall_masks(lam_ref.shape[2:])
    source, row_of = own_lam(lam_ref), got_row(rows_ref, width)
    pack_ref[...] = jnp.zeros(pack_ref.shape, jnp.float32)
    field_ref[...] = jnp.zeros(field_ref.shape, jnp.float32)
    for side in range(2):
        for index, (far, member) in enumerate(PACK_LIST[side]):
            if far > 0:
                rows = rows_ref[side, index * width : (index + 1) * width, :]
            else:
                rows = lam_ref[member, :, span - 1 if side == 0 else 0, :]
            pack_ref[side, index, 2 : width + 2, :] = rows
        for field in range(FIELDS):
            start = (HALO + field) * width
            field_ref[side, field, 2 : width + 2, :] = rows_ref[side, start : start + width, :]
    place = lax.broadcasted_iota(jnp.int32, pack_ref.shape[2:], 0)
    inside = jnp.logical_and(place >= 2, place < width + 2)
    pack_edges = wall_masks(pack_ref.shape[2:])
    for side, (sign, wanted) in enumerate(((1, Y_UP), (-1, Y_DOWN))):
        mu = []
        for member in range(19):
            move_x, move_y, move_z = VELOCITIES[member]
            value = pack_ref[side, PACK_LIST[side].index((1 + sign * move_y, member))]
            if move_x != 0:
                value = pltpu.roll(value, (-move_x) % value.shape[0], 0)
            if move_z != 0:
                walls = pack_ref[side, PACK_LIST[side].index((1, OPPOSITE[member]))]
                value = roll_z(value, move_z, pack_edges, walls)
            mu.append(value)
        pops = [field_ref[side, member] for member in range(19)]
        coefs = plane_coefs(pops, turbine_cells(field_ref[side, 19], thrust_ref))
        lam, _ = plane_adjoint(mu, lambda index: coefs[index], wanted)
        for index, member in enumerate(wanted):
            part_ref[side, index] = jnp.where(inside, lam[member], 0.0)
    for out_ref, plane, members in ((low_ref, 0, X_UP), (high_ref, width - 1, X_DOWN)):
        lam, _ = plane_adjoint(
            gather_mu(source, row_of, plane, edges),
            lambda index: coef_ref[index, min(plane, 1)],
            members,
        )
        for index, member in enumerate(members):
            value, move_y = lam_ref[member, plane], VELOCITIES[member][1]
            if move_y != 0:
                value = span_shift(value, move_y, row_of(0 if move_y == 1 else 1, plane, member))
            out_ref[index] = value
            out_ref[5 + index] = lam[member]
        for side, (sign, wanted) in enumerate(((1, Y_UP), (-1, Y_DOWN))):
            sources = [
                pack_ref.at[side, PACK_LIST[side].index((1 + sign * VELOCITIES[member][1], member))]
                for member in members
            ]
            corner = VELOCITIES.index((VELOCITIES[members[0]][0], sign, 0))
            sources.append(part_ref.at[side, wanted.index(corner)])
            sources += [field_ref.at[side, field] for field in range(FIELDS)]
            for index, ref in enumerate(sources):
                slot = side * CORNER + index
                out_ref[10 + slot // 8, slot % 8 : slot % 8 + 1, :] = ref[plane + 2 : plane + 3, :]
    hand_out(lambda index: low_ref[index], lambda index: high_ref[index], near_ref, far_ref)


def middle_kernel(thrust_ref, lam_ref, rows_ref, coef_ref, near_ref, far_ref, mid_ref, cell_ref, face_ref, ids_ref, gains_ref, above_ref, below_ref):
    width = lam_ref.shape[1]
    edges = wall_masks(lam_ref.shape[2:])
    source, row_of = own_lam(lam_ref), got_row(rows_ref, width)
    take_in(near_ref, far_ref, above_ref, below_ref)
    for side, fields_ref in enumerate((above_ref, below_ref)):
        ids_ref[side], gains_ref[side] = fields_ref[19], fields_ref[20]
    for plane in range(width):
        mu = gather_mu(source, row_of, plane, edges)
        lam, mx = plane_adjoint(mu, lambda index: coef_ref[index, plane])
        for member in range(19):
            mid_ref[member, plane] = lam[member]
        cell_ref[plane] = mx * coef_ref[GAIN, plane]
    for side, (fields_ref, plane, members, wanted) in enumerate(
        ((above_ref, width - 1, X_DOWN, X_UP), (below_ref, 0, X_UP, X_DOWN))
    ):
        mu = [None] * 19
        for member in members:
            value, (_, move_y, move_z) = lam_ref[member, plane], VELOCITIES[member]
            if move_y != 0:
                value = span_shift(value, move_y, row_of(0 if move_y == 1 else 1, plane, member))
            mu[member] = roll_z(value, move_z, edges)
        pops = [fields_ref[member] for member in range(19)]
        coefs = plane_coefs(pops, turbine_cells(fields_ref[19], thrust_ref))
        lam, _ = plane_adjoint(mu, lambda index: coefs[index], wanted)
        for index, member in enumerate(wanted):
            face_ref[side, index] = lam[member]


def pair_kernel(thrust_ref, lam_ref, rows_ref, near_ref, far_ref, late_ref, early_ref, fields_ref,
                part_mid_ref, part_cell_ref, part_face_ref, ids_ref, gains_ref, part_edge_ref, pack_ref,
                out_ref, next_ref, mid_ref, edge_ref, line_ref, above_ref, below_ref):
    width, span, height = lam_ref.shape[1:]
    take_in(near_ref, far_ref, above_ref, below_ref)
    edges = wall_masks((span, height))
    pack_shape = pack_ref.shape[2:]
    pack_edges = wall_masks(pack_shape)
    place = lax.broadcasted_iota(jnp.int32, pack_shape, 0)
    totals = [part_cell_ref[plane] for plane in range(width)]
    for face_ref, plane, members in ((above_ref, width - 1, X_UP), (below_ref, 0, X_DOWN)):
        mu = [None] * 19
        for index, member in enumerate(members):
            mu[member] = roll_z(face_ref[index], VELOCITIES[member][2], edges)
        lam, mx = plane_adjoint(mu, lambda index: late_ref[index, plane])
        for member in range(19):
            mid_ref[member, 0 if plane == 0 else 1] = part_mid_ref[member, plane] + lam[member]
        totals[plane] = totals[plane] + mx * late_ref[GAIN, plane]

    def beyond(below, above, rest):
        return jnp.where(place == 1, below, jnp.where(place == width + 2, above, rest))

    halo_tiles = []
    for side, (sign, wanted) in enumerate(((1, Y_UP), (-1, Y_DOWN))):
        mu = [None] * 19
        for members, got_ref, got_place, own_place in (
            (X_UP, above_ref, width + 1, 1),
            (X_DOWN, below_ref, 2, width + 2),
        ):
            plane = 0 if own_place == 1 else width - 1
            for index, member in enumerate(members):
                far = 1 + sign * VELOCITIES[member][1]
                if far > 0:
                    start = ROW_LIST[side].index((far, member)) * width + plane
                    own = rows_ref[side, start : start + 1, :]
                else:
                    inner = span - 1 if side == 0 else 0
                    own = lam_ref[member, plane, inner : inner + 1, :]
                value = jnp.where(
                    place == got_place,
                    corner_row(got_ref, side, index),
                    jnp.where(place == own_place, own, 0.0),
                )
                mu[member] = roll_z(value, VELOCITIES[member][2], pack_edges)
        fields = [
            beyond(
                corner_row(below_ref, side, 6 + field),
                corner_row(above_ref, side, 6 + field),
                pack_ref[side, field],
            )
            for field in range(FIELDS)
        ]
        coefs = plane_coefs(fields[:19], turbine_cells(fields[19], thrust_ref))
        lam, _ = plane_adjoint(mu, lambda index: coefs[index], wanted)
        for index, member in enumerate(wanted):
            value = part_edge_ref[side, index] + lam[member]
            if VELOCITIES[member][0] == 1:
                value = value + jnp.where(place == width + 2, corner_row(above_ref, side, 5), 0.0)
            elif VELOCITIES[member][0] == -1:
                value = value + jnp.where(place == 1, corner_row(below_ref, side, 5), 0.0)
            edge_ref[side, index] = value
        halo_tiles.append((fields[20], fields[19]))

    def middle(plane, member):
        if plane >= width:
            index = X_UP.index(member)
            return above_ref[5 + index] + part_face_ref[0, index]
        if plane < 0:
            index = X_DOWN.index(member)
            return below_ref[5 + index] + part_face_ref[1, index]
        if plane in (0, width - 1):
            return mid_ref[member, 0 if plane == 0 else 1]
        return part_mid_ref[member, plane]

    def middle_row(side, plane, member):
        index = (Y_UP, Y_DOWN)[side].index(member)
        return edge_ref[side, index, plane + 2 : plane + 3, :]

    for plane in range(width):
        mu = gather_mu(middle, middle_row, plane, edges)
        lam, mx = plane_adjoint(mu, lambda index: early_ref[index, plane])
        for member in range(19):
            out_ref[member, plane] = lam[member]
        totals[plane] = totals[plane] + mx * early_ref[GAIN, plane]

    for side, (members, row) in enumerate(((Y_UP, 0), (Y_DOWN, span - 1))):
        for index, member in enumerate(members):
            start = (5 * side + index) * width
            next_ref[start : start + width, :] = out_ref[member, :, row, :]

    nothing = jnp.zeros((1, height), jnp.float32)
    up, down = [], []
    for plane in range(width):
        up.append(
            2.0 * out_ref[1, plane]
            + span_shift(out_ref[7, plane], 1, nothing)
            + span_shift(out_ref[9, plane], -1, nothing)
            + roll_z(out_ref[11, plane], 1, edges)
            + roll_z(out_ref[13, plane], -1, edges)
        )
        down.append(
            2.0 * out_ref[2, plane]
            + span_shift(out_ref[8, plane], -1, nothing)
            + span_shift(out_ref[10, plane], 1, nothing)
            + roll_z(out_ref[12, plane], -1, edges)
            + roll_z(out_ref[14, plane], 1, edges)
        )
    tiles = []
    for plane in range(-1, width + 1):
        value = None
        if plane + 1 < width:
            value = up[plane + 1]
        if plane >= 1:
            value = -down[plane - 1] if value is None else value - down[plane - 1]
        if plane < 0 or plane >= width:
            side = 1 if plane < 0 else 0
            tiles.append((gains_ref[side] * value, ids_ref[side]))
            continue
        value = value + jnp.where(edges[1], out_ref[12, plane] - out_ref[13, plane], 0.0)
        value = value + jnp.where(edges[0], out_ref[14, plane] - out_ref[11, plane], 0.0)
        tiles.append((totals[plane] + fields_ref[20, plane] * value, fields_ref[19, plane]))
    line_ref[...] = jnp.zeros(line_ref.shape, jnp.float32)
    for side, (upward, downward, row) in enumerate(((9, 8, span - 1), (7, 10, 0))):
        line_ref[side, 0, 1 : width + 1, :] = out_ref[upward, :, row, :]
        line_ref[side, 1, 3 : width + 3, :] = out_ref[downward, :, row, :]
        gain, ids = halo_tiles[side]
        tiles.append(((line_ref[side, 0] - line_ref[side, 1]) * gain, ids))
    start = 10 * width
    next_ref[start:, :] = jnp.zeros((next_ref.shape[0] - start, height), jnp.float32)
    for turbine in range(thrust_ref.shape[0]):
        row = None
        for value, ids in tiles:
            kept = jnp.sum(jnp.where(ids == float(turbine), value, 0.0), axis=0, keepdims=True)
            row = kept if row is None else row + kept
        next_ref[start + turbine : start + turbine + 1, :] = row


def last_faces_kernel(lam_ref, rows_ref, sums_ref, near_ref, far_ref):
    width = lam_ref.shape[1]

    def row_of(side, plane, member):
        place = (5 * side + (Y_UP, Y_DOWN)[side].index(member)) * width + plane
        return rows_ref[place : place + 1, :]

    def moved(members, plane):
        def tile(index):
            member = members[index]
            value, move_y = lam_ref[member, plane], VELOCITIES[member][1]
            if move_y == 0:
                return value
            return span_shift(value, move_y, row_of(0 if move_y == 1 else 1, plane, member))

        return tile

    hand_out(moved(X_UP, 0), moved(X_DOWN, width - 1), near_ref.at[0:5], far_ref)
    for tile in range(near_ref.shape[0] - 5):
        near_ref[5 + tile] = sums_ref[8 * tile : 8 * tile + 8, :]


def last_kernel(lam_ref, rows_ref, near_ref, far_ref, coef_ref, out_ref):
    width, span, height = lam_ref.shape[1:]
    lane = lax.broadcasted_iota(jnp.int32, (span, height), 1)
    first, last = lane == 0, lane == height - 1
    odd = jnp.full((span, height), lax.rem(lax.axis_index("gx"), 2)) == 1

    def source(plane, member):
        if plane >= width:
            index = X_UP.index(member)
            return jnp.where(odd, far_ref[index], near_ref[index])
        if plane < 0:
            index = X_DOWN.index(member)
            return jnp.where(odd, near_ref[index], far_ref[index])
        value, move_y = lam_ref[member, plane], VELOCITIES[member][1]
        if move_y == 0:
            return value
        side = 0 if move_y == 1 else 1
        place = (5 * side + (Y_UP, Y_DOWN)[side].index(member)) * width + plane
        return span_shift(value, move_y, rows_ref[place : place + 1, :])

    for plane in range(width):
        mu = []
        for member in range(19):
            move_x, _, move_z = VELOCITIES[member]
            value = source(plane + move_x, member)
            if move_z == 1:
                value = jnp.where(
                    last, lam_ref[OPPOSITE[member], plane], pltpu.roll(value, height - 1, 1)
                )
            elif move_z == -1:
                value = jnp.where(first, lam_ref[OPPOSITE[member], plane], pltpu.roll(value, 1, 1))
            mu.append(value)
        lam, _ = plane_adjoint(mu, lambda index: coef_ref[index, plane])
        for member in range(19):
            out_ref[member, plane] = lam[member]


def call(kernel, outs, *args, scratch=(), smem_first=False, micros=1):
    specs = [pl.BlockSpec(memory_space=VMEM)] * len(args)
    if smem_first:
        specs[0] = pl.BlockSpec(memory_space=pltpu.SMEM)
    return pl.pallas_call(
        kernel,
        out_shape=tuple(jax.ShapeDtypeStruct(shape, jnp.float32) for shape in outs),
        in_specs=specs,
        out_specs=tuple(pl.BlockSpec(memory_space=VMEM) for _ in outs),
        scratch_shapes=[pltpu.VMEM(shape, jnp.float32) for shape in scratch],
        cost_estimate=pl.CostEstimate(
            flops=int(1e6 * micros), bytes_accessed=int(2e6 * micros), transcendentals=0
        ),
        compiler_params=pltpu.CompilerParams(vmem_limit_bytes=32 * 1024 * 1024),
    )(*args)


def ring(axis, step):
    count = lax.axis_size(axis)
    return [(i, (i + step) % count) for i in range(count)]


def swap_rows(low, high):
    return lax.ppermute(low, "gy", ring("gy", -1)), lax.ppermute(high, "gy", ring("gy", 1))


def swap_planes(near, far):
    count = lax.axis_size("gx")
    assert count % 2 == 0
    got_near = lax.ppermute(near, "gx", [(i, i ^ 1) for i in range(count)])
    got_far = lax.ppermute(
        far, "gx", [(i, (i + 1 if i % 2 else i - 1) % count) for i in range(count)]
    )
    return got_near, got_far


def flips(value, axis, flip_list):
    count = lax.axis_size(axis)
    parts = [lax.ppermute(value, axis, [(i, i ^ flip) for i in range(count)]) for flip in flip_list]
    return sum(parts, value)


def sum_bits(value, axis, start):
    count = lax.axis_size(axis)
    while start < count:
        stop = min(4 * start, count)
        value = flips(value, axis, range(start, stop, start))
        start = stop
    return value


def last_exchange(lam, packed, turbine_rows):
    width, height = lam.shape[1], lam.shape[3]
    rows_count = 10 * width
    if lax.axis_size("gy") == 2:
        got = lax.ppermute(packed, "gy", ring("gy", 1))
        rows, sums = got, packed[rows_count:] + got[rows_count:]
    else:
        low, high = swap_rows(packed[: rows_count // 2], packed[rows_count // 2 : rows_count])
        rows = jnp.concatenate([low, high])
        count = lax.axis_size("gy")
        if count & (count - 1):
            sums = lax.psum(packed[rows_count:], "gy")
        else:
            sums = sum_bits(packed[rows_count:], "gy", 1)
    tiles = 5 + turbine_rows // 8
    near, far = call(
        last_faces_kernel,
        [(tiles, lam.shape[2], height), (5, lam.shape[2], height)],
        lam,
        rows,
        sums,
        micros=0.1,
    )
    got_near, got_far = swap_planes(near, far)
    count = lax.axis_size("gx")
    if count & (count - 1):
        sums = lax.psum(sums, "gx")
    else:
        sums = near[5:] + got_near[5:]
        if count > 2:
            sums = sum_bits(flips(sums, "gx", [2]), "gx", 4)
    return rows, got_near, got_far, sums.reshape(turbine_rows, height)


def shards(fwd_pops, fwd_scale, seed_adjoint, turbine_map, thrust):
    steps, _, width, span, height = fwd_pops.shape
    assert steps == 3 and span == 8
    turbines = thrust.shape[0]
    turbine_rows = -(-turbines // 8) * 8
    sublanes = -(-(width + 4) // 8) * 8
    whole = (19, width, span, height)
    static = (thrust, turbine_map, fwd_scale, fwd_pops)
    (begun,) = call(start_kernel, [(8, height)], micros=400)
    fields, rows, near_fields, far_fields = call(
        pack_kernel,
        [
            (FIELDS, width, span, height),
            (2, (HALO + FIELDS) * width, height),
            (FIELDS, span, height),
            (FIELDS, span, height),
        ],
        begun,
        *static[1:],
        seed_adjoint,
        micros=0.6,
    )
    if lax.axis_size("gy") == 2:
        rows = lax.ppermute(rows, "gy", ring("gy", 1))
    else:
        rows = jnp.stack(swap_rows(rows[0], rows[1]))
    near_fields, far_fields = swap_planes(near_fields, far_fields)
    (edge_coefs,) = call(
        edge_coef_kernel, [(COEFS, 2, span, height)], thrust, fields, smem_first=True, micros=0.3
    )
    face, edge = (FACE_TILES, span, height), (2, 5, sublanes, height)
    near, far, pack, part_edge = call(
        faces_kernel,
        [face, face, (2, FIELDS, sublanes, height), edge],
        thrust,
        seed_adjoint,
        rows,
        edge_coefs,
        scratch=[(2, len(PACK_LIST[0]), sublanes, height), face, face],
        smem_first=True,
        micros=0.6,
    )
    near, far = swap_planes(near, far)
    coefs = call(
        coef_kernel,
        [(COEFS, width, span, height)] * steps,
        *static,
        rows,
        smem_first=True,
        micros=1.5,
    )
    halo = (FIELDS, span, height)
    parts = call(
        middle_kernel,
        [whole, (width, span, height), (2, 5, span, height), (2, span, height), (2, span, height)],
        thrust,
        seed_adjoint,
        rows,
        coefs[2],
        near_fields,
        far_fields,
        scratch=[halo, halo],
        smem_first=True,
        micros=0.6,
    )
    lam, packed = call(
        pair_kernel,
        [whole, (10 * width + turbine_rows, height)],
        thrust,
        seed_adjoint,
        rows,
        near,
        far,
        coefs[2],
        coefs[1],
        fields,
        *parts,
        part_edge,
        pack,
        scratch=[(19, 2, span, height), edge, (2, 2, sublanes, height), face, face],
        smem_first=True,
        micros=0.8,
    )
    rows, near, far, sums = last_exchange(lam, packed, turbine_rows)
    (lam,) = call(last_kernel, [whole], lam, rows, near, far, coefs[0], micros=0.5)
    _, slope = jax.vjp(local_thrust, thrust)
    thrust_grad = slope(jnp.sum(sums[:turbines], axis=1))[0]
    return (lam, thrust_grad)


def solution(mesh):
    placed = (
        P(None, None, "gx", "gy", None),
        P(None, "gx", "gy", None),
        P(None, "gx", "gy", None),
        P("gx", "gy", None),
        P(),
    )
    return jax.shard_map(
        shards,
        mesh=mesh,
        in_specs=placed,
        out_specs=(P(None, "gx", "gy", None), P()),
        check_vma=False,
    )
```

time: 44.2 us -> 36.2 us (0.82)
  waiting for transfers between devices: 20.5 us -> 7.41 us
  starting transfers between devices: 13.3 us -> 20.1 us
  local copies, waits for them, and re-layouts: 4.76 us -> 1.13 us
  Pallas kernels: 4.5 us -> 5.99 us
  other arithmetic: 0.09 us -> 0.67 us
    ppermute x4 -> x6, waiting for transfers between devices: 13 us -> 0.37 us  [the longest x3 0.37 us: swap_planes(): lax.ppermute(far, 'gx', [(i, (i + 1 if i % 2 else i - 1) % count) for i i...]
    ppermute x4 -> x6, starting transfers between devices: 4.4 us -> 11.5 us  [the longest x3 11.4 us: swap_planes(): lax.ppermute(far, 'gx', [(i, (i + 1 if i % 2 else i - 1) % count) for i i...]
    ppermute x1, waiting for transfers between devices: 4.37 us -> 0.01 us  [shards(): rows = lax.ppermute(rows, 'gy', ring('gy', 1))]
    ppermute x3 -> x4, waiting for transfers between devices: 0.68 us -> 4.32 us  [flips(): lax.ppermute(value, axis, [(i, i ^ flip) for i in range(count)])]
    unnamed x14 -> x10, local copies, waits for them, and re-layouts: 4.16 us -> 1.13 us
    pallas_call x7 -> x9, Pallas kernels: 4.5 us -> 5.99 us  [call(): pl.pallas_call(kernel, out_shape=tuple((jax.ShapeDtypeStruct(shape, jnp.f...]
    reduce_sum x1 -> x0, local copies, waits for them, and re-layouts: 0.6 us -> none  [shards(): thrust_grad = jnp.sum(sums, axis=1)[:turbines]]
    add_any x0 -> x1, other arithmetic: none -> 0.54 us  [local_thrust(): return 4.0 * values / jnp.square(1.0 + jnp.sqrt(1.0 - values))]
  transfers between devices with their start and end apart: 9 -> 12, of which waited for: 8 -> 5; matrix products, arithmetic and copies ran while one was open for 0% -> 0% of each run, Pallas kernels for 5% -> 13%
where the time goes in v3:
time: 36.2 us; the launch traced here: 36.1 us
  starting transfers between devices  20.1 us (56%)
  waiting for transfers between devices  7.41 us (20%)
  Pallas kernels  5.99 us (17%)
  local copies, waits for them, and re-layouts  1.13 us (3%)
  between operations  0.79 us (2%)
  other arithmetic  0.67 us (2%)
    ppermute x3, starting transfers between devices, swap_planes(): lax.ppermute(far, 'gx', [(i, (i + 1 if i % 2 else i - 1) % count) for i i...  11.4 us
    pallas_call x9, Pallas kernels, call(): pl.pallas_call(kernel, out_shape=tuple((jax.ShapeDtypeStruct(shape, jnp.f...  5.99 us
    ppermute x4, starting transfers between devices, flips(): lax.ppermute(value, axis, [(i, i ^ flip) for i in range(count)])  4.38 us
    ppermute x4, waiting for transfers between devices, flips(): lax.ppermute(value, axis, [(i, i ^ flip) for i in range(count)])  4.32 us
    ppermute x1, starting transfers between devices, shards(): rows = lax.ppermute(rows, 'gy', ring('gy', 1))  3 us
    ppermute x1, waiting for transfers between devices, last_exchange(): got = lax.ppermute(packed, 'gy', ring('gy', 1))  2.72 us
    ppermute x1, starting transfers between devices, last_exchange(): got = lax.ppermute(packed, 'gy', ring('gy', 1))  1.21 us
    unnamed x10, local copies, waits for them, and re-layouts  1.13 us
  transfers between devices with their start and end apart: 12, of which 5 were waited for; matrix products, arithmetic and copies ran while one was open for 0% of the time, Pallas kernels for 13%

profile of v3, /device:TPU:0, one launch (start us, length us, event | category | flops | bytes accessed | tf_op | source)
XLA Modules:
  0.0 36.1 jit_solution(9023782839903417695)
XLA Ops:
  0.6 0.0 copy-start
  0.6 0.0 copy-start.3
  0.7 0.0 copy-start.2
  0.7 0.0 copy-start.1
  0.7 0.9 %copy-done = f32[19,4,8,128]{3,2,1,0:T(8,128)S(1)} copy-done((f32[19,4,8,128]{3,2,1,0:T(8,128)S(1)}, f32[19,4,8,128]{3,2,1,0:T(8,128)}, u32[]{:S(2)}) %copy-start) | copy-done | bytes 311320
  1.6 0.0 copy-done.3
  1.6 0.0 copy-done.2
  1.6 0.2 copy-done.1
  1.8 0.2 shard_map.69
  2.0 3.0 %collective-permute-start = (f32[2,168,128]{2,1,0:T(8,128)S(1)}, f32[2,168,128]{2,1,0:T(8,128)S(1)}, u32[]{:S(2)}, u32[]{:S(2)}) collective-permute-start(f32[2,168,128]{2,1,0:T(8,128)S(1)} %get-tuple-element.22), channel_id=1, source_target_pairs={{0,1},{1,0},{2,3},{3,2},{4,5},{5,4},{6,7},{7,6},{8,9},{9,8},{10,11... | collective-permute-start | bytes 516104 | tf_op jit(solution)/shard_map/ppermute | solution.py:777
  5.0 0.0 collective-permute-start.3
  5.0 0.0 copy-start.4
  5.0 4.7 %collective-permute-start.4 = (f32[21,8,128]{2,1,0:T(8,128)S(1)}, f32[21,8,128]{2,1,0:T(8,128)S(1)}, u32[]{:S(2)}, u32[]{:S(2)}) collective-permute-start(f32[21,8,128]{2,1,0:T(8,128)S(1)} %get-tuple-element.29), channel_id=1, source_target_pairs={{0,30},{2,4},{4,2},{6,8},{8,6},{10,12},{12,10},{14,16},{16,14},{18... | collective-permute-start | bytes 258056 | tf_op jit(solution)/shard_map/ppermute | solution.py:699
  9.7 0.0 copy-done.4
  9.7 0.7 %shard_map.70.coef_ref = f32[42,2,8,128]{3,2,1,0:T(8,128)S(1)} custom-call(f32[10]{0:T(128)S(1)} %copy-done.4, f32[21,4,8,128]{3,2,1,0:T(8,128)S(1)} %get-tuple-element.23.fields_ref), custom_call_target="tpu_custom_call" | custom-call | flops 300000 | bytes 600000 | tf_op jit(solution)/shard_map/pallas_call | solution.py:673
  10.4 0.0 collective-permute-done.rows_ref._
  10.4 0.8 %shard_map.71 = (f32[17,8,128]{2,1,0:T(8,128)S(1)}, f32[17,8,128]{2,1,0:T(8,128)S(1)}, f32[2,21,8,128]{3,2,1,0:T(8,128)S(1)}, f32[2,5,8,128]{3,2,1,0:T(8,128)S(1)}) custom-call(f32[10]{0:T(128)S(1)} %copy-done.4, f32[19,4,8,128]{3,2,1,0:T(8,128)S(1)} %copy-done, f32[2,168,128]{2,1,0:T(8,128)S(1)} %collective-permute-done.rows_ref._, ...), custom_call_target="tpu_custom_call" | custom-call | flops 600000 | bytes 1200000 | tf_op jit(solution)/shard_map/pallas_call | solution.py:673
  11.2 0.1 collective-permute-start.1
  11.3 3.9 %collective-permute-start.2 = (f32[17,8,128]{2,1,0:T(8,128)S(1)}, f32[17,8,128]{2,1,0:T(8,128)S(1)}, u32[]{:S(2)}, u32[]{:S(2)}) collective-permute-start(f32[17,8,128]{2,1,0:T(8,128)S(1)} %get-tuple-element.25), channel_id=1, source_target_pairs={{0,30},{2,4},{4,2},{6,8},{8,6},{10,12},{12,10},{14,16},{16,14},{18... | collective-permute-start | bytes 208904 | tf_op jit(solution)/shard_map/ppermute | solution.py:699
  15.2 1.2 %shard_map.72 = (f32[42,4,8,128]{3,2,1,0:T(8,128)S(1)}, f32[42,4,8,128]{3,2,1,0:T(8,128)S(1)}, f32[42,4,8,128]{3,2,1,0:T(8,128)S(1)}) custom-call(f32[10]{0:T(128)S(1)} %copy-done.4, s32[4,8,128]{2,1,0:T(8,128)S(1)} %copy-done.3, f32[3,4,8,128]{3,2,1,0:T(8,128)S(1)} %copy-done.2, bf16[3,19,4,8,128]{4,3,2,1,0:T(8,128)(2,1)S(1)} %copy-done.1, ...), custom_call_target="tpu_custom_call" | custom-call | flops 1500000 | bytes 3000000 | tf_op jit(solution)/shard_map/pallas_call | solution.py:673
  16.5 0.0 collective-permute-done.3.near_ref
  16.5 0.0 collective-permute-done.4.far_ref
  16.5 0.9 %shard_map.73 = (f32[19,4,8,128]{3,2,1,0:T(8,128)S(1)}, f32[4,8,128]{2,1,0:T(8,128)S(1)}, f32[2,5,8,128]{3,2,1,0:T(8,128)S(1)}, f32[2,8,128]{2,1,0:T(8,128)S(1)}, f32[2,8,128]{2,1,0:T(8,128)S(1)}) custom-call(f32[10]{0:T(128)S(1)} %copy-done.4, f32[19,4,8,128]{3,2,1,0:T(8,128)S(1)} %copy-done, f32[2,168,128]{2,1,0:T(8,128)S(1)} %collective-permute-done.rows_ref._, ...), custom_call_target="tpu_custom_call" | custom-call | flops 600000 | bytes 1200000 | tf_op jit(solution)/shard_map/pallas_call | solution.py:673
  17.5 0.0 collective-permute-done.1.near_ref
  17.5 0.4 %collective-permute-done.2.far_ref = f32[17,8,128]{2,1,0:T(8,128)S(1)} collective-permute-done((f32[17,8,128]{2,1,0:T(8,128)S(1)}, f32[17,8,128]{2,1,0:T(8,128)S(1)}, u32[]{:S(2)}, u32[]{:S(2)}) %collective-permute-start.2) | collective-permute-done | bytes 69664 | tf_op jit(solution)/shard_map/ppermute | solution.py:699
  17.8 1.1 %shard_map.74 = (f32[19,4,8,128]{3,2,1,0:T(8,128)S(1)}, f32[56,128]{1,0:T(8,128)S(1)}) custom-call(f32[10]{0:T(128)S(1)} %copy-done.4, f32[19,4,8,128]{3,2,1,0:T(8,128)S(1)} %copy-done, f32[2,168,128]{2,1,0:T(8,128)S(1)} %collective-permute-done.rows_ref._, f32[17,8,128]{2,1,0:T(8,128)S(1)} %collective-permute-done.1.near_ref, ...), custom_call_target="tpu_custom_call" | custom-call | flops 800000 | bytes 1600000 | tf_op jit(solution)/shard_map/pallas_call | solution.py:673
  19.0 1.2 %collective-permute-start.5 = (f32[56,128]{1,0:T(8,128)S(1)}, f32[56,128]{1,0:T(8,128)S(1)}, u32[]{:S(2)}, u32[]{:S(2)}) collective-permute-start(f32[56,128]{1,0:T(8,128)S(1)} %get-tuple-element.38), channel_id=1, source_target_pairs={{0,1},{1,0},{2,3},{3,2},{4,5},{5,4},{6,7},{7,6},{8,9},{9,8},{10,11... | collective-permute-start | bytes 86024 | tf_op jit(solution)/shard_map/ppermute | solution.py:724
  20.2 2.7 %collective-permute-done.5.rows_ref = f32[56,128]{1,0:T(8,128)S(1)} collective-permute-done((f32[56,128]{1,0:T(8,128)S(1)}, f32[56,128]{1,0:T(8,128)S(1)}, u32[]{:S(2)}, u32[]{:S(2)}) %collective-permute-start.5) | collective-permute-done | bytes 28704 | tf_op jit(solution)/shard_map/ppermute | solution.py:724
  22.9 0.1 collective-permute-start.6
  23.0 2.8 %collective-permute-start.7 = (f32[5,8,128]{2,1,0:T(8,128)S(1)}, f32[5,8,128]{2,1,0:T(8,128)S(1)}, u32[]{:S(2)}, u32[]{:S(2)}) collective-permute-start(f32[5,8,128]{2,1,0:T(8,128)S(1)} %get-tuple-element.40), channel_id=1, source_target_pairs={{0,30},{2,4},{4,2},{6,8},{8,6},{10,12},{12,10},{14,16},{16,14},{18... | collective-permute-start | bytes 61448 | tf_op jit(solution)/shard_map/ppermute | solution.py:699
  25.8 0.0 collective-permute-done.6.near_ref
  25.8 0.0 collective-permute-start.8
  25.8 3.6 %collective-permute-done.8 = f32[2,8,128]{2,1,0:T(8,128)S(1)} collective-permute-done((f32[2,8,128]{2,1,0:T(8,128)S(1)}, f32[2,8,128]{2,1,0:T(8,128)S(1)}, u32[]{:S(2)}, u32[]{:S(2)}) %collective-permute-start.8) | collective-permute-done | bytes 8224 | tf_op jit(solution)/shard_map/ppermute | solution.py:707
  29.4 0.0 collective-permute-start.11
  29.4 0.0 collective-permute-start.10
  29.4 4.4 %collective-permute-start.9 = (f32[2,8,128]{2,1,0:T(8,128)S(1)}, f32[2,8,128]{2,1,0:T(8,128)S(1)}, u32[]{:S(2)}, u32[]{:S(2)}) collective-permute-start(f32[2,8,128]{2,1,0:T(8,128)S(1)} %add.23), channel_id=1, source_target_pairs={{0,8},{2,10},{4,12},{6,14},{8,0},{10,2},{12,4},{14,6},{16,24},{18,... | collective-permute-start | bytes 24584 | tf_op jit(solution)/shard_map/ppermute | solution.py:707
  33.8 0.0 collective-permute-done.7.far_ref
  33.8 1.0 %shard_map.76 = f32[19,4,8,128]{3,2,1,0:T(8,128)} custom-call(f32[19,4,8,128]{3,2,1,0:T(8,128)S(1)} %get-tuple-element.37.lam_ref, f32[56,128]{1,0:T(8,128)S(1)} %collective-permute-done.5.rows_ref, f32[7,8,128]{2,1,0:T(8,128)S(1)} %collective-permute-done.6.near_ref, f32[5,8,128]{2,1,0:T(8,128)S(1)} %collective-permute-done.7.far_ref, ...), custom_call_target="tpu_custom_call" | custom-call | flops 500000 | bytes 1000000 | tf_op jit(solution)/shard_map/pallas_call | solution.py:673
  34.8 0.1 collective-permute-done.11
  34.9 0.0 collective-permute-done.10
  34.9 0.6 %collective-permute-done.9 = f32[2,8,128]{2,1,0:T(8,128)S(1)} collective-permute-done((f32[2,8,128]{2,1,0:T(8,128)S(1)}, f32[2,8,128]{2,1,0:T(8,128)S(1)}, u32[]{:S(2)}, u32[]{:S(2)}) %collective-permute-start.9) | collective-permute-done | bytes 8224 | tf_op jit(solution)/shard_map/ppermute | solution.py:707
  35.4 0.1 slice_reduce_fusion
  35.6 0.5 %multiply_add_fusion = f32[10]{0:T(128)} fusion(f32[10]{0:T(128)S(1)} %slice_reduce_fusion, f32[10]{0:T(128)S(1)} %copy-done.4), kind=kLoop, calls=%fused_computation.7 | loop fusion | flops 170 | bytes 120 | tf_op jit(solution)/shard_map/transpose(jvp())/add_any | solution.py:234
  (6 shorter events, 0.0 us)
Async XLA Ops:
  0.6 1.0 %copy-start = (f32[19,4,8,128]{3,2,1,0:T(8,128)S(1)}, f32[19,4,8,128]{3,2,1,0:T(8,128)}, u32[]{:S(2)}) copy-start(f32[19,4,8,128]{3,2,1,0:T(8,128)} %lam_ref.7) | copy-start | bytes 933892
  0.6 1.0 %copy-start.3 = (s32[4,8,128]{2,1,0:T(8,128)S(1)}, s32[4,8,128]{2,1,0:T(8,128)}, u32[]{:S(2)}) copy-start(s32[4,8,128]{2,1,0:T(8,128)} %map_ref.3) | copy-start | bytes 49156
  0.7 1.0 %copy-start.2 = (f32[3,4,8,128]{3,2,1,0:T(8,128)S(1)}, f32[3,4,8,128]{3,2,1,0:T(8,128)}, u32[]{:S(2)}) copy-start(f32[3,4,8,128]{3,2,1,0:T(8,128)} %scale_ref.3) | copy-start | bytes 147460
  0.7 1.1 %copy-start.1 = (bf16[3,19,4,8,128]{4,3,2,1,0:T(8,128)(2,1)S(1)}, bf16[3,19,4,8,128]{4,3,2,1,0:T(8,128)(2,1)}, u32[]{:S(2)}) copy-start(bf16[3,19,4,8,128]{4,3,2,1,0:T(8,128)(2,1)} %pops_ref.3) | copy-start | bytes 1400836
  2.0 8.4 %collective-permute-start = (f32[2,168,128]{2,1,0:T(8,128)S(1)}, f32[2,168,128]{2,1,0:T(8,128)S(1)}, u32[]{:S(2)}, u32[]{:S(2)}) collective-permute-start(f32[2,168,128]{2,1,0:T(8,128)S(1)} %get-tuple-element.22), channel_id=1, source_target_pairs={{0,1},{1,0},{2,3},{3,2},{4,5},{5,4},{6,7},{7,6},{8,9},{9,8},{10,11... | collective-permute-start | bytes 516104 | tf_op jit(solution)/shard_map/ppermute | solution.py:777
  5.0 11.5 %collective-permute-start.3 = (f32[21,8,128]{2,1,0:T(8,128)S(1)}, f32[21,8,128]{2,1,0:T(8,128)S(1)}, u32[]{:S(2)}, u32[]{:S(2)}) collective-permute-start(f32[21,8,128]{2,1,0:T(8,128)S(1)} %get-tuple-element.28), channel_id=1, source_target_pairs={{0,2},{2,0},{4,6},{6,4},{8,10},{10,8},{12,14},{14,12},{16,18},{18,... | collective-permute-start | bytes 258056 | tf_op jit(solution)/shard_map/ppermute | solution.py:698
  5.0 4.7 %copy-start.4 = (f32[10]{0:T(128)S(1)}, f32[10]{0:T(128)}, u32[]{:S(2)}) copy-start(f32[10]{0:T(128)} %thrust_ref.9) | copy-start | bytes 124
  5.0 11.5 %collective-permute-start.4 = (f32[21,8,128]{2,1,0:T(8,128)S(1)}, f32[21,8,128]{2,1,0:T(8,128)S(1)}, u32[]{:S(2)}, u32[]{:S(2)}) collective-permute-start(f32[21,8,128]{2,1,0:T(8,128)S(1)} %get-tuple-element.29), channel_id=1, source_target_pairs={{0,30},{2,4},{4,2},{6,8},{8,6},{10,12},{12,10},{14,16},{16,14},{18... | collective-permute-start | bytes 258056 | tf_op jit(solution)/shard_map/ppermute | solution.py:699
  11.2 6.2 %collective-permute-start.1 = (f32[17,8,128]{2,1,0:T(8,128)S(1)}, f32[17,8,128]{2,1,0:T(8,128)S(1)}, u32[]{:S(2)}, u32[]{:S(2)}) collective-permute-start(f32[17,8,128]{2,1,0:T(8,128)S(1)} %get-tuple-element.24), channel_id=1, source_target_pairs={{0,2},{2,0},{4,6},{6,4},{8,10},{10,8},{12,14},{14,12},{16,18},{18,... | collective-permute-start | bytes 208904 | tf_op jit(solution)/shard_map/ppermute | solution.py:698
  11.3 6.5 %collective-permute-start.2 = (f32[17,8,128]{2,1,0:T(8,128)S(1)}, f32[17,8,128]{2,1,0:T(8,128)S(1)}, u32[]{:S(2)}, u32[]{:S(2)}) collective-permute-start(f32[17,8,128]{2,1,0:T(8,128)S(1)} %get-tuple-element.25), channel_id=1, source_target_pairs={{0,30},{2,4},{4,2},{6,8},{8,6},{10,12},{12,10},{14,16},{16,14},{18... | collective-permute-start | bytes 208904 | tf_op jit(solution)/shard_map/ppermute | solution.py:699
  19.0 3.9 %collective-permute-start.5 = (f32[56,128]{1,0:T(8,128)S(1)}, f32[56,128]{1,0:T(8,128)S(1)}, u32[]{:S(2)}, u32[]{:S(2)}) collective-permute-start(f32[56,128]{1,0:T(8,128)S(1)} %get-tuple-element.38), channel_id=1, source_target_pairs={{0,1},{1,0},{2,3},{3,2},{4,5},{5,4},{6,7},{7,6},{8,9},{9,8},{10,11... | collective-permute-start | bytes 86024 | tf_op jit(solution)/shard_map/ppermute | solution.py:724
  22.9 2.8 %collective-permute-start.6 = (f32[7,8,128]{2,1,0:T(8,128)S(1)}, f32[7,8,128]{2,1,0:T(8,128)S(1)}, u32[]{:S(2)}, u32[]{:S(2)}) collective-permute-start(f32[7,8,128]{2,1,0:T(8,128)S(1)} %get-tuple-element.39), channel_id=1, source_target_pairs={{0,2},{2,0},{4,6},{6,4},{8,10},{10,8},{12,14},{14,12},{16,18},{18,... | collective-permute-start | bytes 86024 | tf_op jit(solution)/shard_map/ppermute | solution.py:698
  23.0 10.8 %collective-permute-start.7 = (f32[5,8,128]{2,1,0:T(8,128)S(1)}, f32[5,8,128]{2,1,0:T(8,128)S(1)}, u32[]{:S(2)}, u32[]{:S(2)}) collective-permute-start(f32[5,8,128]{2,1,0:T(8,128)S(1)} %get-tuple-element.40), channel_id=1, source_target_pairs={{0,30},{2,4},{4,2},{6,8},{8,6},{10,12},{12,10},{14,16},{16,14},{18... | collective-permute-start | bytes 61448 | tf_op jit(solution)/shard_map/ppermute | solution.py:699
  25.8 3.7 %collective-permute-start.8 = (f32[2,8,128]{2,1,0:T(8,128)S(1)}, f32[2,8,128]{2,1,0:T(8,128)S(1)}, u32[]{:S(2)}, u32[]{:S(2)}) collective-permute-start(f32[2,8,128]{2,1,0:T(8,128)S(1)} %slice_add_fusion), channel_id=1, source_target_pairs={{0,4},{2,6},{4,0},{6,2},{8,12},{10,14},{12,8},{14,10},{16,20},{18,... | collective-permute-start | bytes 24584 | tf_op jit(solution)/shard_map/ppermute | solution.py:707
  29.4 5.4 %collective-permute-start.11 = (f32[2,8,128]{2,1,0:T(8,128)S(1)}, f32[2,8,128]{2,1,0:T(8,128)S(1)}, u32[]{:S(2)}, u32[]{:S(2)}) collective-permute-start(f32[2,8,128]{2,1,0:T(8,128)S(1)} %add.23), channel_id=1, source_target_pairs={{0,24},{2,26},{4,28},{6,30},{8,16},{10,18},{12,20},{14,22},{16,8},... | collective-permute-start | bytes 24584 | tf_op jit(solution)/shard_map/ppermute | solution.py:707
  29.4 5.4 %collective-permute-start.10 = (f32[2,8,128]{2,1,0:T(8,128)S(1)}, f32[2,8,128]{2,1,0:T(8,128)S(1)}, u32[]{:S(2)}, u32[]{:S(2)}) collective-permute-start(f32[2,8,128]{2,1,0:T(8,128)S(1)} %add.23), channel_id=1, source_target_pairs={{0,16},{2,18},{4,20},{6,22},{8,24},{10,26},{12,28},{14,30},{16,0},... | collective-permute-start | bytes 24584 | tf_op jit(solution)/shard_map/ppermute | solution.py:707
  29.4 6.0 %collective-permute-start.9 = (f32[2,8,128]{2,1,0:T(8,128)S(1)}, f32[2,8,128]{2,1,0:T(8,128)S(1)}, u32[]{:S(2)}, u32[]{:S(2)}) collective-permute-start(f32[2,8,128]{2,1,0:T(8,128)S(1)} %add.23), channel_id=1, source_target_pairs={{0,8},{2,10},{4,12},{6,14},{8,0},{10,2},{12,4},{14,6},{16,24},{18,... | collective-permute-start | bytes 24584 | tf_op jit(solution)/shard_map/ppermute | solution.py:707

commit v4 on v3

--- a/solution.py
+++ b/solution.py
@@ -226,7 +226,8 @@
 def turbine_cells(ids, thrust_ref):
     ratio = jnp.zeros(ids.shape, jnp.float32)
     for turbine in range(thrust_ref.shape[0]):
-        ratio = jnp.where(ids == jnp.asarray(turbine, ids.dtype), thrust_ref[turbine], ratio)
+        row = thrust_ref[turbine : turbine + 1, :]
+        ratio = jnp.where(ids == jnp.asarray(turbine, ids.dtype), row, ratio)
     return jnp.where(ids >= 0, local_thrust(ratio), 0.0)
 
 
@@ -243,7 +244,8 @@
     ]
 
 
-def coef_kernel(thrust_ref, map_ref, scale_ref, pops_ref, _, *out_refs):
+def coef_kernel(thrust_ref, map_ref, scale_ref, pops_ref, near_ref, pass_ref, *out_refs):
+    pass_ref[...] = near_ref[...]
     for plane in range(pops_ref.shape[2]):
         thrust_cell = turbine_cells(map_ref[plane], thrust_ref)
         for instant, out_ref in enumerate(out_refs):
@@ -252,12 +254,13 @@
                 out_ref[index, plane] = value
 
 
-def edge_coef_kernel(thrust_ref, fields_ref, out_ref):
+def edge_coef_kernel(thrust_ref, fields_ref, near_ref, out_ref, pass_ref):
     for index, plane in enumerate((0, fields_ref.shape[1] - 1)):
         pops = [fields_ref[member, plane] for member in range(19)]
         coefs = plane_coefs(pops, turbine_cells(fields_ref[19, plane], thrust_ref))
         for coef, value in enumerate(coefs):
             out_ref[coef, index] = value
+    pass_ref[...] = near_ref[...]
 
 
 def by_parity(even):
@@ -286,6 +289,16 @@
 
 def start_kernel(out_ref):
     out_ref[...] = jnp.zeros(out_ref.shape, jnp.float32)
+
+
+def thrust_kernel(thrust_ref, _, thrust_rows_ref, slope_rows_ref):
+    thrust_rows_ref[...] = jnp.zeros(thrust_rows_ref.shape, jnp.float32)
+    for turbine in range(thrust_ref.shape[0]):
+        thrust_rows_ref[turbine : turbine + 1, :] = jnp.full(
+            (1, thrust_rows_ref.shape[1]), thrust_ref[turbine], jnp.float32
+        )
+    root = jnp.sqrt(1.0 - thrust_rows_ref[...])
+    slope_rows_ref[...] = 4.0 / (root * jnp.square(1.0 + root))
 
 
 def pack_kernel(_, map_ref, scale_ref, pops_ref, lam_ref, fields_ref, rows_ref, near_ref, far_ref):
@@ -470,7 +483,7 @@
             face_ref[side, index] = lam[member]
 
 
-def pair_kernel(thrust_ref, lam_ref, rows_ref, near_ref, far_ref, late_ref, early_ref, fields_ref,
+def pair_kernel(turbines, thrust_ref, lam_ref, rows_ref, near_ref, far_ref, late_ref, early_ref, fields_ref,
                 part_mid_ref, part_cell_ref, part_face_ref, ids_ref, gains_ref, part_edge_ref, pack_ref,
                 out_ref, next_ref, mid_ref, edge_ref, line_ref, above_ref, below_ref):
     width, span, height = lam_ref.shape[1:]
@@ -599,7 +612,7 @@
         tiles.append(((line_ref[side, 0] - line_ref[side, 1]) * gain, ids))
     start = 10 * width
     next_ref[start:, :] = jnp.zeros((next_ref.shape[0] - start, height), jnp.float32)
-    for turbine in range(thrust_ref.shape[0]):
+    for turbine in range(turbines):
         row = None
         for value, ids in tiles:
             kept = jnp.sum(jnp.where(ids == float(turbine), value, 0.0), axis=0, keepdims=True)
@@ -607,7 +620,7 @@
         next_ref[start + turbine : start + turbine + 1, :] = row
 
 
-def last_faces_kernel(lam_ref, rows_ref, sums_ref, near_ref, far_ref):
+def last_faces_kernel(lam_ref, rows_ref, sums_ref, got_ref, near_ref, far_ref, total_ref):
     width = lam_ref.shape[1]
 
     def row_of(side, plane, member):
@@ -624,9 +637,8 @@
 
         return tile
 
-    hand_out(moved(X_UP, 0), moved(X_DOWN, width - 1), near_ref.at[0:5], far_ref)
-    for tile in range(near_ref.shape[0] - 5):
-        near_ref[5 + tile] = sums_ref[8 * tile : 8 * tile + 8, :]
+    total_ref[...] = sums_ref[...] + got_ref[...]
+    hand_out(moved(X_UP, 0), moved(X_DOWN, width - 1), near_ref, far_ref)
 
 
 def last_kernel(lam_ref, rows_ref, near_ref, far_ref, coef_ref, out_ref):
@@ -692,14 +704,17 @@
     return lax.ppermute(low, "gy", ring("gy", -1)), lax.ppermute(high, "gy", ring("gy", 1))
 
 
-def swap_planes(near, far):
+def swap_near(near):
     count = lax.axis_size("gx")
     assert count % 2 == 0
-    got_near = lax.ppermute(near, "gx", [(i, i ^ 1) for i in range(count)])
-    got_far = lax.ppermute(
+    return lax.ppermute(near, "gx", [(i, i ^ 1) for i in range(count)])
+
+
+def swap_far(far):
+    count = lax.axis_size("gx")
+    return lax.ppermute(
         far, "gx", [(i, (i + 1 if i % 2 else i - 1) % count) for i in range(count)]
     )
-    return got_near, got_far
 
 
 def flips(value, axis, flip_list):
@@ -717,38 +732,38 @@
     return value
 
 
-def last_exchange(lam, packed, turbine_rows):
+def last_exchange(lam, packed):
     width, height = lam.shape[1], lam.shape[3]
     rows_count = 10 * width
+    sums = packed[rows_count:]
     if lax.axis_size("gy") == 2:
         got = lax.ppermute(packed, "gy", ring("gy", 1))
-        rows, sums = got, packed[rows_count:] + got[rows_count:]
+        rows, got = got[:rows_count], got[rows_count:]
     else:
-        low, high = swap_rows(packed[: rows_count // 2], packed[rows_count // 2 : rows_count])
-        rows = jnp.concatenate([low, high])
+        rows = jnp.concatenate(
+            swap_rows(packed[: rows_count // 2], packed[rows_count // 2 : rows_count])
+        )
         count = lax.axis_size("gy")
-        if count & (count - 1):
-            sums = lax.psum(packed[rows_count:], "gy")
-        else:
-            sums = sum_bits(packed[rows_count:], "gy", 1)
-    tiles = 5 + turbine_rows // 8
-    near, far = call(
+        got = (lax.psum(sums, "gy") if count & (count - 1) else sum_bits(sums, "gy", 1)) - sums
+    near, far, sums = call(
         last_faces_kernel,
-        [(tiles, lam.shape[2], height), (5, lam.shape[2], height)],
+        [(5, lam.shape[2], height), (5, lam.shape[2], height), sums.shape],
         lam,
         rows,
         sums,
+        got,
         micros=0.1,
     )
-    got_near, got_far = swap_planes(near, far)
     count = lax.axis_size("gx")
-    if count & (count - 1):
+    apart = count & (count - 1) == 0 and count > 2
+    if apart:
+        sums = flips(sums, "gx", [2])
+    got_near, got_far = swap_near(near), swap_far(far)
+    if apart:
+        sums = sum_bits(flips(sums, "gx", [1]), "gx", 4)
+    else:
         sums = lax.psum(sums, "gx")
-    else:
-        sums = near[5:] + got_near[5:]
-        if count > 2:
-            sums = sum_bits(flips(sums, "gx", [2]), "gx", 4)
-    return rows, got_near, got_far, sums.reshape(turbine_rows, height)
+    return rows, got_near, got_far, sums
 
 
 def shards(fwd_pops, fwd_scale, seed_adjoint, turbine_map, thrust):
@@ -758,7 +773,6 @@
     turbine_rows = -(-turbines // 8) * 8
     sublanes = -(-(width + 4) // 8) * 8
     whole = (19, width, span, height)
-    static = (thrust, turbine_map, fwd_scale, fwd_pops)
     (begun,) = call(start_kernel, [(8, height)], micros=400)
     fields, rows, near_fields, far_fields = call(
         pack_kernel,
@@ -769,57 +783,74 @@
             (FIELDS, span, height),
         ],
         begun,
-        *static[1:],
+        turbine_map,
+        fwd_scale,
+        fwd_pops,
         seed_adjoint,
         micros=0.6,
+    )
+    thrust_rows, slope_rows = call(
+        thrust_kernel,
+        [(turbine_rows, height)] * 2,
+        thrust,
+        fields,
+        smem_first=True,
+        micros=0.3,
     )
     if lax.axis_size("gy") == 2:
         rows = lax.ppermute(rows, "gy", ring("gy", 1))
     else:
         rows = jnp.stack(swap_rows(rows[0], rows[1]))
-    near_fields, far_fields = swap_planes(near_fields, far_fields)
-    (edge_coefs,) = call(
-        edge_coef_kernel, [(COEFS, 2, span, height)], thrust, fields, smem_first=True, micros=0.3
-    )
+    far_fields = swap_far(far_fields)
+    edge_coefs, near_fields = call(
+        edge_coef_kernel,
+        [(COEFS, 2, span, height), near_fields.shape],
+        thrust_rows,
+        fields,
+        near_fields,
+        micros=0.3,
+    )
+    near_fields = swap_near(near_fields)
     face, edge = (FACE_TILES, span, height), (2, 5, sublanes, height)
     near, far, pack, part_edge = call(
         faces_kernel,
         [face, face, (2, FIELDS, sublanes, height), edge],
-        thrust,
+        thrust_rows,
         seed_adjoint,
         rows,
         edge_coefs,
         scratch=[(2, len(PACK_LIST[0]), sublanes, height), face, face],
-        smem_first=True,
         micros=0.6,
     )
-    near, far = swap_planes(near, far)
-    coefs = call(
+    far = swap_far(far)
+    near, *coefs = call(
         coef_kernel,
-        [(COEFS, width, span, height)] * steps,
-        *static,
-        rows,
-        smem_first=True,
+        [near.shape] + [(COEFS, width, span, height)] * steps,
+        thrust_rows,
+        turbine_map,
+        fwd_scale,
+        fwd_pops,
+        near,
         micros=1.5,
     )
+    near = swap_near(near)
     halo = (FIELDS, span, height)
     parts = call(
         middle_kernel,
         [whole, (width, span, height), (2, 5, span, height), (2, span, height), (2, span, height)],
-        thrust,
+        thrust_rows,
         seed_adjoint,
         rows,
         coefs[2],
         near_fields,
         far_fields,
         scratch=[halo, halo],
-        smem_first=True,
         micros=0.6,
     )
     lam, packed = call(
-        pair_kernel,
+        lambda *refs: pair_kernel(turbines, *refs),
         [whole, (10 * width + turbine_rows, height)],
-        thrust,
+        thrust_rows,
         seed_adjoint,
         rows,
         near,
@@ -831,13 +862,11 @@
         part_edge,
         pack,
         scratch=[(19, 2, span, height), edge, (2, 2, sublanes, height), face, face],
-        smem_first=True,
         micros=0.8,
     )
-    rows, near, far, sums = last_exchange(lam, packed, turbine_rows)
+    rows, near, far, sums = last_exchange(lam, packed)
     (lam,) = call(last_kernel, [whole], lam, rows, near, far, coefs[0], micros=0.5)
-    _, slope = jax.vjp(local_thrust, thrust)
-    thrust_grad = slope(jnp.sum(sums[:turbines], axis=1))[0]
+    thrust_grad = jnp.sum((slope_rows * sums)[:turbines], axis=1)
     return (lam, thrust_grad)
 
 

time: 36.2 us -> 33 us (0.912)
  Pallas kernels: 5.99 us -> 3.85 us
  waiting for transfers between devices: 7.41 us -> 6.74 us
  starting transfers between devices: 20.1 us -> 19.7 us
    pallas_call x9 -> x10, Pallas kernels: 5.99 us -> 3.85 us  [call(): pl.pallas_call(kernel, out_shape=tuple((jax.ShapeDtypeStruct(shape, jnp.f...]
    ppermute x4 -> x5, waiting for transfers between devices: 4.32 us -> 2.46 us  [flips(): lax.ppermute(value, axis, [(i, i ^ flip) for i in range(count)])]
    ppermute x6, waiting for transfers between devices: 0.37 us -> 2.01 us  [the longest x3 2 us: swap_far(): lax.ppermute(far, 'gx', [(i, (i + 1 if i % 2 else i - 1) % count) for i i...]
    ppermute x6, starting transfers between devices: 11.5 us -> 10.6 us  [the longest x3 10.4 us: swap_far(): lax.ppermute(far, 'gx', [(i, (i + 1 if i % 2 else i - 1) % count) for i i...]
    add_any x1 -> x0, other arithmetic: 0.54 us -> none  [local_thrust(): return 4.0 * values / jnp.square(1.0 + jnp.sqrt(1.0 - values))]
    reduce_sum x1, other arithmetic: 0.11 us -> 0.63 us  [shards(): thrust_grad = jnp.sum((slope_rows * sums)[:turbines], axis=1)]
    ppermute x1, waiting for transfers between devices: 2.72 us -> 2.27 us  [last_exchange(): got = lax.ppermute(packed, 'gy', ring('gy', 1))]
    ppermute x1, starting transfers between devices: 1.21 us -> 1.66 us  [last_exchange(): got = lax.ppermute(packed, 'gy', ring('gy', 1))]
  transfers between devices with their start and end apart: 12 -> 13, of which waited for: 5 -> 6; matrix products, arithmetic and copies ran while one was open for 0% -> 0% of each run, Pallas kernels for 13% -> 9%
where the time goes in v4:
time: 33 us; the launch traced here: 32.9 us
  starting transfers between devices  19.7 us (60%)
  waiting for transfers between devices  6.74 us (20%)
  Pallas kernels  3.85 us (12%)
  local copies, waits for them, and re-layouts  1.14 us (3%)
  between operations  0.79 us (2%)
  other arithmetic  0.64 us (2%)
    ppermute x3, starting transfers between devices, swap_far(): lax.ppermute(far, 'gx', [(i, (i + 1 if i % 2 else i - 1) % count) for i i...  10.4 us
    ppermute x5, starting transfers between devices, flips(): lax.ppermute(value, axis, [(i, i ^ flip) for i in range(count)])  4.46 us
    pallas_call x10, Pallas kernels, call(): pl.pallas_call(kernel, out_shape=tuple((jax.ShapeDtypeStruct(shape, jnp.f...  3.85 us
    ppermute x1, starting transfers between devices, shards(): rows = lax.ppermute(rows, 'gy', ring('gy', 1))  3 us
    ppermute x5, waiting for transfers between devices, flips(): lax.ppermute(value, axis, [(i, i ^ flip) for i in range(count)])  2.46 us
    ppermute x1, waiting for transfers between devices, last_exchange(): got = lax.ppermute(packed, 'gy', ring('gy', 1))  2.27 us
    ppermute x3, waiting for transfers between devices, swap_far(): lax.ppermute(far, 'gx', [(i, (i + 1 if i % 2 else i - 1) % count) for i i...  2 us
    ppermute x1, starting transfers between devices, last_exchange(): got = lax.ppermute(packed, 'gy', ring('gy', 1))  1.66 us
  transfers between devices with their start and end apart: 13, of which 6 were waited for; matrix products, arithmetic and copies ran while one was open for 0% of the time, Pallas kernels for 9%

profile of v4, /device:TPU:0, one launch (start us, length us, event | category | flops | bytes accessed | tf_op | source)
XLA Modules:
  0.0 32.9 jit_solution(18223534908353092157)
XLA Ops:
  0.6 0.0 copy-start
  0.6 0.0 copy-start.3
  0.7 0.0 copy-start.2
  0.7 0.0 copy-start.1
  0.7 0.9 %copy-done = f32[19,4,8,128]{3,2,1,0:T(8,128)S(1)} copy-done((f32[19,4,8,128]{3,2,1,0:T(8,128)S(1)}, f32[19,4,8,128]{3,2,1,0:T(8,128)}, u32[]{:S(2)}) %copy-start) | copy-done | bytes 311320
  1.6 0.0 copy-done.3
  1.6 0.0 copy-done.2
  1.6 0.2 copy-done.1
  1.8 0.2 shard_map.69
  2.0 3.0 %collective-permute-start = (f32[2,168,128]{2,1,0:T(8,128)S(1)}, f32[2,168,128]{2,1,0:T(8,128)S(1)}, u32[]{:S(2)}, u32[]{:S(2)}) collective-permute-start(f32[2,168,128]{2,1,0:T(8,128)S(1)} %get-tuple-element.30), channel_id=1, source_target_pairs={{0,1},{1,0},{2,3},{3,2},{4,5},{5,4},{6,7},{7,6},{8,9},{9,8},{10,11... | collective-permute-start | bytes 516104 | tf_op jit(solution)/shard_map/ppermute | solution.py:801
  5.0 0.0 copy-start.4
  5.0 3.7 %collective-permute-start.4 = (f32[21,8,128]{2,1,0:T(8,128)S(1)}, f32[21,8,128]{2,1,0:T(8,128)S(1)}, u32[]{:S(2)}, u32[]{:S(2)}) collective-permute-start(f32[21,8,128]{2,1,0:T(8,128)S(1)} %get-tuple-element.39), channel_id=1, source_target_pairs={{0,30},{2,4},{4,2},{6,8},{8,6},{10,12},{12,10},{14,16},{16,14},{18... | collective-permute-start | bytes 258056 | tf_op jit(solution)/shard_map/ppermute | solution.py:715
  8.7 0.0 copy-done.4
  8.7 0.6 %shard_map.70 = (f32[16,128]{1,0:T(8,128)S(1)}, f32[16,128]{1,0:T(8,128)S(1)}) custom-call(f32[10]{0:T(128)S(1)} %copy-done.4, f32[21,4,8,128]{3,2,1,0:T(8,128)S(1)} %get-tuple-element.28._.fields_ref.refs_7_), custom_call_target="tpu_custom_call" | custom-call | flops 300000 | bytes 600000 | tf_op jit(solution)/shard_map/pallas_call | solution.py:685
  9.3 0.1 shard_map.71
  9.4 0.1 collective-permute-start.3
  9.5 0.0 collective-permute-done.rows_ref.refs_2_
  9.5 0.3 shard_map.72
  9.9 3.3 %collective-permute-start.2 = (f32[17,8,128]{2,1,0:T(8,128)S(1)}, f32[17,8,128]{2,1,0:T(8,128)S(1)}, u32[]{:S(2)}, u32[]{:S(2)}) collective-permute-start(f32[17,8,128]{2,1,0:T(8,128)S(1)} %get-tuple-element.35), channel_id=1, source_target_pairs={{0,30},{2,4},{4,2},{6,8},{8,6},{10,12},{12,10},{14,16},{16,14},{18... | collective-permute-start | bytes 208904 | tf_op jit(solution)/shard_map/ppermute | solution.py:715
  13.2 0.7 %shard_map.73 = (f32[17,8,128]{2,1,0:T(8,128)S(1)}, f32[42,4,8,128]{3,2,1,0:T(8,128)S(1)}, f32[42,4,8,128]{3,2,1,0:T(8,128)S(1)}, f32[42,4,8,128]{3,2,1,0:T(8,128)S(1)}) custom-call(f32[16,128]{1,0:T(8,128)S(1)} %get-tuple-element.29.thrust_ref.refs_0_, s32[4,8,128]{2,1,0:T(8,128)S(1)} %copy-done.3, f32[3,4,8,128]{3,2,1,0:T(8,128)S(1)} %copy-done.2, ...), custom_call_target="tpu_custom_call" | custom-call | flops 1500000 | bytes 3000000 | tf_op jit(solution)/shard_map/pallas_call | solution.py:685
  13.9 0.1 collective-permute-start.1
  14.0 0.0 collective-permute-done.4.far_ref
  14.0 0.0 collective-permute-done.3.near_ref
  14.0 0.4 %shard_map.74 = (f32[19,4,8,128]{3,2,1,0:T(8,128)S(1)}, f32[4,8,128]{2,1,0:T(8,128)S(1)}, f32[2,5,8,128]{3,2,1,0:T(8,128)S(1)}, f32[2,8,128]{2,1,0:T(8,128)S(1)}, f32[2,8,128]{2,1,0:T(8,128)S(1)}) custom-call(f32[16,128]{1,0:T(8,128)S(1)} %get-tuple-element.29.thrust_ref.refs_0_, f32[19,4,8,128]{3,2,1,0:T(8,128)S(1)} %copy-done, ...), custom_call_target="tpu_custom_call" | custom-call | flops 600000 | bytes 1200000 | tf_op jit(solution)/shard_map/pallas_call | solution.py:685
  14.4 2.0 %collective-permute-done.2.refs_4_ = f32[17,8,128]{2,1,0:T(8,128)S(1)} collective-permute-done((f32[17,8,128]{2,1,0:T(8,128)S(1)}, f32[17,8,128]{2,1,0:T(8,128)S(1)}, u32[]{:S(2)}, u32[]{:S(2)}) %collective-permute-start.2) | collective-permute-done | bytes 69664 | tf_op jit(solution)/shard_map/ppermute | solution.py:715
  16.4 0.0 collective-permute-done.1.refs_3_
  16.4 0.6 %shard_map.75 = (f32[19,4,8,128]{3,2,1,0:T(8,128)S(1)}, f32[56,128]{1,0:T(8,128)S(1)}) custom-call(f32[16,128]{1,0:T(8,128)S(1)} %get-tuple-element.29.thrust_ref.refs_0_, f32[19,4,8,128]{3,2,1,0:T(8,128)S(1)} %copy-done, f32[2,168,128]{2,1,0:T(8,128)S(1)} %collective-permute-done.rows_ref.refs_2_, f32[17,8,128]{2,1,0:T(8,128)S(1)} %collective-permute-done.1.refs_3_, ...), custom_call_target="tpu_custom_call" | custom-call | flops 800000 | bytes 1600000 | tf_op jit(solution)/shard_map/pallas_call | solution.py:685
  16.9 1.7 %collective-permute-start.5 = (f32[56,128]{1,0:T(8,128)S(1)}, f32[56,128]{1,0:T(8,128)S(1)}, u32[]{:S(2)}, u32[]{:S(2)}) collective-permute-start(f32[56,128]{1,0:T(8,128)S(1)} %get-tuple-element.48), channel_id=1, source_target_pairs={{0,1},{1,0},{2,3},{3,2},{4,5},{5,4},{6,7},{7,6},{8,9},{9,8},{10,11... | collective-permute-start | bytes 86024 | tf_op jit(solution)/shard_map/ppermute | solution.py:740
  18.6 2.3 %collective-permute-done.5 = f32[56,128]{1,0:T(8,128)S(1)} collective-permute-done((f32[56,128]{1,0:T(8,128)S(1)}, f32[56,128]{1,0:T(8,128)S(1)}, u32[]{:S(2)}, u32[]{:S(2)}) %collective-permute-start.5) | collective-permute-done | bytes 28704 | tf_op jit(solution)/shard_map/ppermute | solution.py:740
  20.9 0.1 collective-permute-start.8
  21.0 0.1 collective-permute-start.6
  21.1 3.4 %collective-permute-start.7 = (f32[5,8,128]{2,1,0:T(8,128)S(1)}, f32[5,8,128]{2,1,0:T(8,128)S(1)}, u32[]{:S(2)}, u32[]{:S(2)}) collective-permute-start(f32[5,8,128]{2,1,0:T(8,128)S(1)} %get-tuple-element.50), channel_id=1, source_target_pairs={{0,30},{2,4},{4,2},{6,8},{8,6},{10,12},{12,10},{14,16},{16,14},{18... | collective-permute-start | bytes 61448 | tf_op jit(solution)/shard_map/ppermute | solution.py:715
  24.5 0.2 collective-permute-done.8
  24.6 0.0 collective-permute-start.9
  24.6 1.2 %collective-permute-done.9 = f32[16,128]{1,0:T(8,128)S(1)} collective-permute-done((f32[16,128]{1,0:T(8,128)S(1)}, f32[16,128]{1,0:T(8,128)S(1)}, u32[]{:S(2)}, u32[]{:S(2)}) %collective-permute-start.9) | collective-permute-done | bytes 8224 | tf_op jit(solution)/shard_map/ppermute | solution.py:722
  25.8 1.9 %collective-permute-start.12 = (f32[16,128]{1,0:T(8,128)S(1)}, f32[16,128]{1,0:T(8,128)S(1)}, u32[]{:S(2)}, u32[]{:S(2)}) collective-permute-start(f32[16,128]{1,0:T(8,128)S(1)} %add.16), channel_id=1, source_target_pairs={{0,24},{2,26},{4,28},{6,30},{8,16},{10,18},{12,20},{14,22},{16,8},... | collective-permute-start | bytes 24584 | tf_op jit(solution)/shard_map/ppermute | solution.py:722
  27.7 0.0 collective-permute-start.11
  27.7 2.5 %collective-permute-start.10 = (f32[16,128]{1,0:T(8,128)S(1)}, f32[16,128]{1,0:T(8,128)S(1)}, u32[]{:S(2)}, u32[]{:S(2)}) collective-permute-start(f32[16,128]{1,0:T(8,128)S(1)} %add.16), channel_id=1, source_target_pairs={{0,8},{2,10},{4,12},{6,14},{8,0},{10,2},{12,4},{14,6},{16,24},{18,... | collective-permute-start | bytes 24584 | tf_op jit(solution)/shard_map/ppermute | solution.py:722
  30.2 0.0 collective-permute-done.6.near_ref
  30.2 0.0 collective-permute-done.7.far_ref
  30.2 0.9 %shard_map.77 = f32[19,4,8,128]{3,2,1,0:T(8,128)} custom-call(f32[19,4,8,128]{3,2,1,0:T(8,128)S(1)} %get-tuple-element.47.lam_ref, f32[40,128]{1,0:T(8,128)S(1)} %slice.16.rows_ref, f32[5,8,128]{2,1,0:T(8,128)S(1)} %collective-permute-done.6.near_ref, f32[5,8,128]{2,1,0:T(8,128)S(1)} %collective-permute-done.7.far_ref, ...), custom_call_target="tpu_custom_call" | custom-call | flops 500000 | bytes 1000000 | tf_op jit(solution)/shard_map/pallas_call | solution.py:685
  31.1 0.1 collective-permute-done.12
  31.3 1.0 %collective-permute-done.11 = f32[16,128]{1,0:T(8,128)S(1)} collective-permute-done((f32[16,128]{1,0:T(8,128)S(1)}, f32[16,128]{1,0:T(8,128)S(1)}, u32[]{:S(2)}, u32[]{:S(2)}) %collective-permute-start.11) | collective-permute-done | bytes 8224 | tf_op jit(solution)/shard_map/ppermute | solution.py:722
  32.3 0.0 collective-permute-done.10
  32.3 0.6 %fusion = f32[10]{0:T(128)} fusion(f32[16,128]{1,0:T(8,128)S(1)} %get-tuple-element.52, f32[16,128]{1,0:T(8,128)S(1)} %collective-permute-done.12, f32[16,128]{1,0:T(8,128)S(1)} %collective-permute-done.11, f32[16,128]{1,0:T(8,128)S(1)} %collective-permute-done.10, f32[16,128]{1,0:T(8,128)S(1)} %add.16), kind=kLoop, calls=%fused_computation.1 | loop fusion | flops 6390 | bytes 25640 | tf_op jit(solution)/shard_map/reduce_sum | solution.py:869
  (7 shorter events, 0.0 us)
Async XLA Ops:
  0.6 1.0 %copy-start = (f32[19,4,8,128]{3,2,1,0:T(8,128)S(1)}, f32[19,4,8,128]{3,2,1,0:T(8,128)}, u32[]{:S(2)}) copy-start(f32[19,4,8,128]{3,2,1,0:T(8,128)} %refs_1_.1) | copy-start | bytes 933892
  0.6 1.0 %copy-start.3 = (s32[4,8,128]{2,1,0:T(8,128)S(1)}, s32[4,8,128]{2,1,0:T(8,128)}, u32[]{:S(2)}) copy-start(s32[4,8,128]{2,1,0:T(8,128)} %map_ref.3) | copy-start | bytes 49156
  0.7 1.0 %copy-start.2 = (f32[3,4,8,128]{3,2,1,0:T(8,128)S(1)}, f32[3,4,8,128]{3,2,1,0:T(8,128)}, u32[]{:S(2)}) copy-start(f32[3,4,8,128]{3,2,1,0:T(8,128)} %scale_ref.3) | copy-start | bytes 147460
  0.7 1.1 %copy-start.1 = (bf16[3,19,4,8,128]{4,3,2,1,0:T(8,128)(2,1)S(1)}, bf16[3,19,4,8,128]{4,3,2,1,0:T(8,128)(2,1)}, u32[]{:S(2)}) copy-start(bf16[3,19,4,8,128]{4,3,2,1,0:T(8,128)(2,1)} %pops_ref.3) | copy-start | bytes 1400836
  2.0 7.5 %collective-permute-start = (f32[2,168,128]{2,1,0:T(8,128)S(1)}, f32[2,168,128]{2,1,0:T(8,128)S(1)}, u32[]{:S(2)}, u32[]{:S(2)}) collective-permute-start(f32[2,168,128]{2,1,0:T(8,128)S(1)} %get-tuple-element.30), channel_id=1, source_target_pairs={{0,1},{1,0},{2,3},{3,2},{4,5},{5,4},{6,7},{7,6},{8,9},{9,8},{10,11... | collective-permute-start | bytes 516104 | tf_op jit(solution)/shard_map/ppermute | solution.py:801
  5.0 3.7 %copy-start.4 = (f32[10]{0:T(128)S(1)}, f32[10]{0:T(128)}, u32[]{:S(2)}) copy-start(f32[10]{0:T(128)} %thrust_ref.1) | copy-start | bytes 124
  5.0 8.9 %collective-permute-start.4 = (f32[21,8,128]{2,1,0:T(8,128)S(1)}, f32[21,8,128]{2,1,0:T(8,128)S(1)}, u32[]{:S(2)}, u32[]{:S(2)}) collective-permute-start(f32[21,8,128]{2,1,0:T(8,128)S(1)} %get-tuple-element.39), channel_id=1, source_target_pairs={{0,30},{2,4},{4,2},{6,8},{8,6},{10,12},{12,10},{14,16},{16,14},{18... | collective-permute-start | bytes 258056 | tf_op jit(solution)/shard_map/ppermute | solution.py:715
  9.4 4.5 %collective-permute-start.3 = (f32[21,8,128]{2,1,0:T(8,128)S(1)}, f32[21,8,128]{2,1,0:T(8,128)S(1)}, u32[]{:S(2)}, u32[]{:S(2)}) collective-permute-start(f32[21,8,128]{2,1,0:T(8,128)S(1)} %get-tuple-element.38), channel_id=1, source_target_pairs={{0,2},{2,0},{4,6},{6,4},{8,10},{10,8},{12,14},{14,12},{16,18},{18,... | collective-permute-start | bytes 258056 | tf_op jit(solution)/shard_map/ppermute | solution.py:710
  9.9 6.5 %collective-permute-start.2 = (f32[17,8,128]{2,1,0:T(8,128)S(1)}, f32[17,8,128]{2,1,0:T(8,128)S(1)}, u32[]{:S(2)}, u32[]{:S(2)}) collective-permute-start(f32[17,8,128]{2,1,0:T(8,128)S(1)} %get-tuple-element.35), channel_id=1, source_target_pairs={{0,30},{2,4},{4,2},{6,8},{8,6},{10,12},{12,10},{14,16},{16,14},{18... | collective-permute-start | bytes 208904 | tf_op jit(solution)/shard_map/ppermute | solution.py:715
  13.9 2.5 %collective-permute-start.1 = (f32[17,8,128]{2,1,0:T(8,128)S(1)}, f32[17,8,128]{2,1,0:T(8,128)S(1)}, u32[]{:S(2)}, u32[]{:S(2)}) collective-permute-start(f32[17,8,128]{2,1,0:T(8,128)S(1)} %get-tuple-element.34), channel_id=1, source_target_pairs={{0,2},{2,0},{4,6},{6,4},{8,10},{10,8},{12,14},{14,12},{16,18},{18,... | collective-permute-start | bytes 208904 | tf_op jit(solution)/shard_map/ppermute | solution.py:710
  16.9 3.9 %collective-permute-start.5 = (f32[56,128]{1,0:T(8,128)S(1)}, f32[56,128]{1,0:T(8,128)S(1)}, u32[]{:S(2)}, u32[]{:S(2)}) collective-permute-start(f32[56,128]{1,0:T(8,128)S(1)} %get-tuple-element.48), channel_id=1, source_target_pairs={{0,1},{1,0},{2,3},{3,2},{4,5},{5,4},{6,7},{7,6},{8,9},{9,8},{10,11... | collective-permute-start | bytes 86024 | tf_op jit(solution)/shard_map/ppermute | solution.py:740
  20.9 3.7 %collective-permute-start.8 = (f32[16,128]{1,0:T(8,128)S(1)}, f32[16,128]{1,0:T(8,128)S(1)}, u32[]{:S(2)}, u32[]{:S(2)}) collective-permute-start(f32[16,128]{1,0:T(8,128)S(1)} %get-tuple-element.53), channel_id=1, source_target_pairs={{0,4},{2,6},{4,0},{6,2},{8,12},{10,14},{12,8},{14,10},{16,20},{18,... | collective-permute-start | bytes 24584 | tf_op jit(solution)/shard_map/ppermute | solution.py:722
  21.0 9.2 %collective-permute-start.6 = (f32[5,8,128]{2,1,0:T(8,128)S(1)}, f32[5,8,128]{2,1,0:T(8,128)S(1)}, u32[]{:S(2)}, u32[]{:S(2)}) collective-permute-start(f32[5,8,128]{2,1,0:T(8,128)S(1)} %get-tuple-element.49), channel_id=1, source_target_pairs={{0,2},{2,0},{4,6},{6,4},{8,10},{10,8},{12,14},{14,12},{16,18},{18,... | collective-permute-start | bytes 61448 | tf_op jit(solution)/shard_map/ppermute | solution.py:710
  21.1 9.1 %collective-permute-start.7 = (f32[5,8,128]{2,1,0:T(8,128)S(1)}, f32[5,8,128]{2,1,0:T(8,128)S(1)}, u32[]{:S(2)}, u32[]{:S(2)}) collective-permute-start(f32[5,8,128]{2,1,0:T(8,128)S(1)} %get-tuple-element.50), channel_id=1, source_target_pairs={{0,30},{2,4},{4,2},{6,8},{8,6},{10,12},{12,10},{14,16},{16,14},{18... | collective-permute-start | bytes 61448 | tf_op jit(solution)/shard_map/ppermute | solution.py:715
  24.6 1.2 %collective-permute-start.9 = (f32[16,128]{1,0:T(8,128)S(1)}, f32[16,128]{1,0:T(8,128)S(1)}, u32[]{:S(2)}, u32[]{:S(2)}) collective-permute-start(f32[16,128]{1,0:T(8,128)S(1)} %add.15), channel_id=1, source_target_pairs={{0,2},{2,0},{4,6},{6,4},{8,10},{10,8},{12,14},{14,12},{16,18},{18,... | collective-permute-start | bytes 24584 | tf_op jit(solution)/shard_map/ppermute | solution.py:722
  25.8 5.5 %collective-permute-start.12 = (f32[16,128]{1,0:T(8,128)S(1)}, f32[16,128]{1,0:T(8,128)S(1)}, u32[]{:S(2)}, u32[]{:S(2)}) collective-permute-start(f32[16,128]{1,0:T(8,128)S(1)} %add.16), channel_id=1, source_target_pairs={{0,24},{2,26},{4,28},{6,30},{8,16},{10,18},{12,20},{14,22},{16,8},... | collective-permute-start | bytes 24584 | tf_op jit(solution)/shard_map/ppermute | solution.py:722
  27.7 4.5 %collective-permute-start.11 = (f32[16,128]{1,0:T(8,128)S(1)}, f32[16,128]{1,0:T(8,128)S(1)}, u32[]{:S(2)}, u32[]{:S(2)}) collective-permute-start(f32[16,128]{1,0:T(8,128)S(1)} %add.16), channel_id=1, source_target_pairs={{0,16},{2,18},{4,20},{6,22},{8,24},{10,26},{12,28},{14,30},{16,0},... | collective-permute-start | bytes 24584 | tf_op jit(solution)/shard_map/ppermute | solution.py:722
  27.7 4.5 %collective-permute-start.10 = (f32[16,128]{1,0:T(8,128)S(1)}, f32[16,128]{1,0:T(8,128)S(1)}, u32[]{:S(2)}, u32[]{:S(2)}) collective-permute-start(f32[16,128]{1,0:T(8,128)S(1)} %add.16), channel_id=1, source_target_pairs={{0,8},{2,10},{4,12},{6,14},{8,0},{10,2},{12,4},{14,6},{16,24},{18,... | collective-permute-start | bytes 24584 | tf_op jit(solution)/shard_map/ppermute | solution.py:722

commit v5 on v4

--- a/solution.py
+++ b/solution.py
@@ -60,7 +60,14 @@
 PACK_LIST = [ROW_LIST[side] + INNER_LIST[side] for side in range(2)]
 HALO = len(ROW_LIST[0])
 CORNER = 6 + FIELDS
-FACE_TILES = 10 + -(-2 * CORNER // 8)
+NEXT_LIST = [
+    [[(far, m) for far, m in ROW_LIST[y] if VELOCITIES[m][0] == sign] for y in range(2)]
+    for sign in SIGNS
+]
+FIRST_ROWS = -(-(HALO + len(NEXT_LIST[0][0]) + FIELDS) // 8) * 8
+MIRROR = [VELOCITIES.index((a, -b, c)) for a, b, c in VELOCITIES]
+STATIC = 10 + -(-2 * CORNER // 8)
+FACE_TILES = STATIC + FIELDS
 
 
 def base_values():
@@ -244,8 +251,7 @@
     ]
 
 
-def coef_kernel(thrust_ref, map_ref, scale_ref, pops_ref, near_ref, pass_ref, *out_refs):
-    pass_ref[...] = near_ref[...]
+def coef_kernel(thrust_ref, map_ref, scale_ref, pops_ref, *out_refs):
     for plane in range(pops_ref.shape[2]):
         thrust_cell = turbine_cells(map_ref[plane], thrust_ref)
         for instant, out_ref in enumerate(out_refs):
@@ -254,15 +260,6 @@
                 out_ref[index, plane] = value
 
 
-def edge_coef_kernel(thrust_ref, fields_ref, near_ref, out_ref, pass_ref):
-    for index, plane in enumerate((0, fields_ref.shape[1] - 1)):
-        pops = [fields_ref[member, plane] for member in range(19)]
-        coefs = plane_coefs(pops, turbine_cells(fields_ref[19, plane], thrust_ref))
-        for coef, value in enumerate(coefs):
-            out_ref[coef, index] = value
-    pass_ref[...] = near_ref[...]
-
-
 def by_parity(even):
     odd = lax.rem(lax.axis_index("gx"), 2) == 1
     pl.when(jnp.logical_not(odd))(lambda: even(True))
@@ -291,22 +288,19 @@
     out_ref[...] = jnp.zeros(out_ref.shape, jnp.float32)
 
 
-def thrust_kernel(thrust_ref, _, thrust_rows_ref, slope_rows_ref):
+def write_thrust(thrust_ref, thrust_rows_ref, slope_rows_ref):
     thrust_rows_ref[...] = jnp.zeros(thrust_rows_ref.shape, jnp.float32)
-    for turbine in range(thrust_ref.shape[0]):
-        thrust_rows_ref[turbine : turbine + 1, :] = jnp.full(
-            (1, thrust_rows_ref.shape[1]), thrust_ref[turbine], jnp.float32
+    for turbine in range(thrust_ref.shape[1]):
+        thrust_rows_ref[turbine : turbine + 1, :] = jnp.broadcast_to(
+            thrust_ref[0:1, turbine : turbine + 1], (1, thrust_rows_ref.shape[1])
         )
     root = jnp.sqrt(1.0 - thrust_rows_ref[...])
     slope_rows_ref[...] = 4.0 / (root * jnp.square(1.0 + root))
 
 
-def pack_kernel(_, map_ref, scale_ref, pops_ref, lam_ref, fields_ref, rows_ref, near_ref, far_ref):
+def pack_kernel(_, thrust_ref, map_ref, scale_ref, pops_ref, lam_ref, fields_ref, first_ref, thrust_rows_ref, slope_rows_ref):
     width, span = lam_ref.shape[1], lam_ref.shape[2]
-    for side in range(2):
-        for index, (far, member) in enumerate(ROW_LIST[side]):
-            row = far - 1 if side == 0 else span - far
-            rows_ref[side, index * width : (index + 1) * width, :] = lam_ref[member, :, row, :]
+    write_thrust(thrust_ref, thrust_rows_ref, slope_rows_ref)
     last = pops_ref.shape[0] - 1
     for plane in range(width):
         for index, value in enumerate(decode(scale_ref, pops_ref, last, plane)):
@@ -321,17 +315,31 @@
             momentum = pair if momentum is None else momentum + pair
         ux = momentum / rho
         fields_ref[20, plane] = (-1.5 / 36.0) * ux * jnp.abs(ux)
+    first_ref[...] = jnp.zeros(first_ref.shape, jnp.float32)
+
+    def write(even):
+        plane, inner = (0, 1) if even else (width - 1, width - 2)
+        for side in range(2):
+            picks = [(lam_ref, m, plane, far) for far, m in ROW_LIST[side]]
+            picks += [(lam_ref, m, inner, far) for far, m in NEXT_LIST[0 if even else 1][side]]
+            picks += [(fields_ref, field, plane, 1) for field in range(FIELDS)]
+            for index, (ref, member, at, far) in enumerate(picks):
+                row = far - 1 if side == 0 else span - far
+                first_ref[side, index : index + 1, :] = ref[member, at, row : row + 1, :]
+
+    by_parity(write)
+
+
+def rows_kernel(lam_ref, fields_ref, _, rows_ref):
+    width, span = lam_ref.shape[1], lam_ref.shape[2]
     for side in range(2):
+        for index, (far, member) in enumerate(ROW_LIST[side]):
+            row = far - 1 if side == 0 else span - far
+            rows_ref[side, index * width : (index + 1) * width, :] = lam_ref[member, :, row, :]
         row = 0 if side == 0 else span - 1
         for field in range(FIELDS):
             start = (HALO + field) * width
             rows_ref[side, start : start + width, :] = fields_ref[field, :, row, :]
-    hand_out(
-        lambda field: fields_ref[field, 0],
-        lambda field: fields_ref[field, width - 1],
-        near_ref,
-        far_ref,
-    )
 
 
 def span_shift(value, move, row):
@@ -393,7 +401,88 @@
     return face_ref[10 + slot // 8, slot % 8 : slot % 8 + 1, :]
 
 
-def faces_kernel(thrust_ref, lam_ref, rows_ref, coef_ref, near_ref, far_ref, field_ref, part_ref, pack_ref, low_ref, high_ref):
+def far_kernel(thrust_ref, lam_ref, fields_ref, first_ref, coef_ref, out_ref, pop_ref, mu_ref, wall_ref):
+    width, span = lam_ref.shape[1], lam_ref.shape[2]
+    edges = wall_masks(lam_ref.shape[2:])
+    source = own_lam(lam_ref)
+    pop_ref[...] = jnp.ones(pop_ref.shape, jnp.float32)
+
+    def write(even):
+        x_side, plane, inner, members = (0, 0, 1, X_UP) if even else (1, width - 1, width - 2, X_DOWN)
+        inward = SIGNS[x_side]
+
+        def row(side, far, member, at):
+            if far == 0:
+                last = span - 1 if side == 0 else 0
+                return lam_ref[member, at, last : last + 1, :]
+            place = (
+                ROW_LIST[side].index((far, member))
+                if at == plane
+                else HALO + NEXT_LIST[x_side][side].index((far, member))
+            )
+            return first_ref[side, place : place + 1, :]
+
+        def field(side, index):
+            place = HALO + len(NEXT_LIST[0][0]) + index
+            return first_ref[side, place : place + 1, :]
+
+        def row_of(side, at, member):
+            return row(side, 1, member, at)
+
+        for member in range(19):
+            move_x, move_y, move_z = VELOCITIES[member]
+            for side in range(2):
+                same = (member, MIRROR[member])[side]
+                wall = (OPPOSITE[member], MIRROR[OPPOSITE[member]])[side]
+                pop_ref[member, side : side + 1, :] = field(side, same)
+                if move_x != -inward:
+                    mu_ref[member, side : side + 1, :] = row(
+                        side, 1 + move_y, same, plane if move_x == 0 else inner
+                    )
+                if move_z != 0:
+                    wall_ref[member, side : side + 1, :] = row(side, 1, wall, plane)
+        for side in range(2):
+            pop_ref[19, side : side + 1, :] = field(side, 19)
+        mu = []
+        for member in range(19):
+            move_x, _, move_z = VELOCITIES[member]
+            if move_z == 0:
+                mu.append(None if move_x == -inward else mu_ref[member])
+            elif move_x == -inward:
+                mu.append(jnp.where(edges[1 if move_z == 1 else 0], wall_ref[member], 0.0))
+            else:
+                mu.append(roll_z(mu_ref[member], move_z, edges, wall_ref[member]))
+        coefs = plane_coefs(
+            [pop_ref[member] for member in range(19)], turbine_cells(pop_ref[19], thrust_ref)
+        )
+        corner = VELOCITIES.index((inward, 1, 0))
+        corners, _ = plane_adjoint(mu, lambda index: coefs[index], (corner,))
+        mu_ref[0] = corners[corner]
+        lam, _ = plane_adjoint(
+            gather_mu(source, row_of, plane, edges),
+            lambda index: coef_ref[index, plane],
+            members,
+        )
+        for index, member in enumerate(members):
+            value, move_y = lam_ref[member, plane], VELOCITIES[member][1]
+            if move_y != 0:
+                value = span_shift(value, move_y, row_of(0 if move_y == 1 else 1, plane, member))
+            out_ref[index] = value
+            out_ref[5 + index] = lam[member]
+        for side, sign in enumerate(SIGNS):
+            rows = [row(side, 1 + sign * VELOCITIES[m][1], m, plane) for m in members]
+            rows.append(mu_ref[0, side : side + 1, :])
+            rows += [field(side, index) for index in range(FIELDS)]
+            for index, value in enumerate(rows):
+                slot = side * CORNER + index
+                out_ref[10 + slot // 8, slot % 8 : slot % 8 + 1, :] = value
+        for index in range(FIELDS):
+            out_ref[STATIC + index] = fields_ref[index, plane]
+
+    by_parity(write)
+
+
+def faces_kernel(thrust_ref, lam_ref, fields_ref, rows_ref, coef_ref, near_ref, field_ref, part_ref, pack_ref, low_ref, high_ref):
     width, span = lam_ref.shape[1], lam_ref.shape[2]
     edges = wall_masks(lam_ref.shape[2:])
     source, row_of = own_lam(lam_ref), got_row(rows_ref, width)
@@ -431,7 +520,7 @@
     for out_ref, plane, members in ((low_ref, 0, X_UP), (high_ref, width - 1, X_DOWN)):
         lam, _ = plane_adjoint(
             gather_mu(source, row_of, plane, edges),
-            lambda index: coef_ref[index, min(plane, 1)],
+            lambda index: coef_ref[index, plane],
             members,
         )
         for index, member in enumerate(members):
@@ -451,41 +540,30 @@
             for index, ref in enumerate(sources):
                 slot = side * CORNER + index
                 out_ref[10 + slot // 8, slot % 8 : slot % 8 + 1, :] = ref[plane + 2 : plane + 3, :]
-    hand_out(lambda index: low_ref[index], lambda index: high_ref[index], near_ref, far_ref)
-
-
-def middle_kernel(thrust_ref, lam_ref, rows_ref, coef_ref, near_ref, far_ref, mid_ref, cell_ref, face_ref, ids_ref, gains_ref, above_ref, below_ref):
+
+    def write(even):
+        near_ref[0:STATIC] = (high_ref if even else low_ref)[0:STATIC]
+        for index in range(FIELDS):
+            near_ref[STATIC + index] = fields_ref[index, width - 1 if even else 0]
+
+    by_parity(write)
+
+
+def middle_kernel(lam_ref, rows_ref, coef_ref, mid_ref, cell_ref):
     width = lam_ref.shape[1]
     edges = wall_masks(lam_ref.shape[2:])
     source, row_of = own_lam(lam_ref), got_row(rows_ref, width)
-    take_in(near_ref, far_ref, above_ref, below_ref)
-    for side, fields_ref in enumerate((above_ref, below_ref)):
-        ids_ref[side], gains_ref[side] = fields_ref[19], fields_ref[20]
     for plane in range(width):
         mu = gather_mu(source, row_of, plane, edges)
         lam, mx = plane_adjoint(mu, lambda index: coef_ref[index, plane])
         for member in range(19):
             mid_ref[member, plane] = lam[member]
         cell_ref[plane] = mx * coef_ref[GAIN, plane]
-    for side, (fields_ref, plane, members, wanted) in enumerate(
-        ((above_ref, width - 1, X_DOWN, X_UP), (below_ref, 0, X_UP, X_DOWN))
-    ):
-        mu = [None] * 19
-        for member in members:
-            value, (_, move_y, move_z) = lam_ref[member, plane], VELOCITIES[member]
-            if move_y != 0:
-                value = span_shift(value, move_y, row_of(0 if move_y == 1 else 1, plane, member))
-            mu[member] = roll_z(value, move_z, edges)
-        pops = [fields_ref[member] for member in range(19)]
-        coefs = plane_coefs(pops, turbine_cells(fields_ref[19], thrust_ref))
-        lam, _ = plane_adjoint(mu, lambda index: coefs[index], wanted)
-        for index, member in enumerate(wanted):
-            face_ref[side, index] = lam[member]
 
 
 def pair_kernel(turbines, thrust_ref, lam_ref, rows_ref, near_ref, far_ref, late_ref, early_ref, fields_ref,
-                part_mid_ref, part_cell_ref, part_face_ref, ids_ref, gains_ref, part_edge_ref, pack_ref,
-                out_ref, next_ref, mid_ref, edge_ref, line_ref, above_ref, below_ref):
+                part_mid_ref, part_cell_ref, part_edge_ref, pack_ref,
+                out_ref, next_ref, mid_ref, edge_ref, line_ref, above_ref, below_ref, part_face_ref):
     width, span, height = lam_ref.shape[1:]
     take_in(near_ref, far_ref, above_ref, below_ref)
     edges = wall_masks((span, height))
@@ -501,6 +579,21 @@
         for member in range(19):
             mid_ref[member, 0 if plane == 0 else 1] = part_mid_ref[member, plane] + lam[member]
         totals[plane] = totals[plane] + mx * late_ref[GAIN, plane]
+
+    for side, (static_ref, plane, members, wanted) in enumerate(
+        ((above_ref, width - 1, X_DOWN, X_UP), (below_ref, 0, X_UP, X_DOWN))
+    ):
+        mu = [None] * 19
+        for member in members:
+            value, (_, move_y, move_z) = lam_ref[member, plane], VELOCITIES[member]
+            if move_y != 0:
+                value = span_shift(value, move_y, got_row(rows_ref, width)(0 if move_y == 1 else 1, plane, member))
+            mu[member] = roll_z(value, move_z, edges)
+        pops = [static_ref[STATIC + member] for member in range(19)]
+        coefs = plane_coefs(pops, turbine_cells(static_ref[STATIC + 19], thrust_ref))
+        lam, _ = plane_adjoint(mu, lambda index: coefs[index], wanted)
+        for index, member in enumerate(wanted):
+            part_face_ref[side, index] = lam[member]
 
     def beyond(below, above, rest):
         return jnp.where(place == 1, below, jnp.where(place == width + 2, above, rest))
@@ -598,8 +691,8 @@
         if plane >= 1:
             value = -down[plane - 1] if value is None else value - down[plane - 1]
         if plane < 0 or plane >= width:
-            side = 1 if plane < 0 else 0
-            tiles.append((gains_ref[side] * value, ids_ref[side]))
+            face_ref = below_ref if plane < 0 else above_ref
+            tiles.append((face_ref[STATIC + 20] * value, face_ref[STATIC + 19]))
             continue
         value = value + jnp.where(edges[1], out_ref[12, plane] - out_ref[13, plane], 0.0)
         value = value + jnp.where(edges[0], out_ref[14, plane] - out_ref[11, plane], 0.0)
@@ -638,7 +731,8 @@
         return tile
 
     total_ref[...] = sums_ref[...] + got_ref[...]
-    hand_out(moved(X_UP, 0), moved(X_DOWN, width - 1), near_ref, far_ref)
+    far_ref[5:] = jnp.zeros((far_ref.shape[0] - 5,) + far_ref.shape[1:], jnp.float32)
+    hand_out(moved(X_UP, 0), moved(X_DOWN, width - 1), near_ref, far_ref.at[0:5])
 
 
 def last_kernel(lam_ref, rows_ref, near_ref, far_ref, coef_ref, out_ref):
@@ -678,14 +772,11 @@
             out_ref[member, plane] = lam[member]
 
 
-def call(kernel, outs, *args, scratch=(), smem_first=False, micros=1):
-    specs = [pl.BlockSpec(memory_space=VMEM)] * len(args)
-    if smem_first:
-        specs[0] = pl.BlockSpec(memory_space=pltpu.SMEM)
+def call(kernel, outs, *args, scratch=(), micros=1):
     return pl.pallas_call(
         kernel,
         out_shape=tuple(jax.ShapeDtypeStruct(shape, jnp.float32) for shape in outs),
-        in_specs=specs,
+        in_specs=[pl.BlockSpec(memory_space=VMEM)] * len(args),
         out_specs=tuple(pl.BlockSpec(memory_space=VMEM) for _ in outs),
         scratch_shapes=[pltpu.VMEM(shape, jnp.float32) for shape in scratch],
         cost_estimate=pl.CostEstimate(
@@ -700,8 +791,15 @@
     return [(i, (i + step) % count) for i in range(count)]
 
 
-def swap_rows(low, high):
-    return lax.ppermute(low, "gy", ring("gy", -1)), lax.ppermute(high, "gy", ring("gy", 1))
+def swap_rows(rows):
+    if lax.axis_size("gy") == 2:
+        return lax.ppermute(rows, "gy", ring("gy", 1))
+    return jnp.stack(
+        [
+            lax.ppermute(rows[0], "gy", ring("gy", -1)),
+            lax.ppermute(rows[1], "gy", ring("gy", 1)),
+        ]
+    )
 
 
 def swap_near(near):
@@ -740,14 +838,13 @@
         got = lax.ppermute(packed, "gy", ring("gy", 1))
         rows, got = got[:rows_count], got[rows_count:]
     else:
-        rows = jnp.concatenate(
-            swap_rows(packed[: rows_count // 2], packed[rows_count // 2 : rows_count])
-        )
+        rows = swap_rows(packed[:rows_count].reshape(2, rows_count // 2, -1))
+        rows = rows.reshape(rows_count, -1)
         count = lax.axis_size("gy")
         got = (lax.psum(sums, "gy") if count & (count - 1) else sum_bits(sums, "gy", 1)) - sums
     near, far, sums = call(
         last_faces_kernel,
-        [(5, lam.shape[2], height), (5, lam.shape[2], height), sums.shape],
+        [(5, lam.shape[2], height), (6, lam.shape[2], height), sums.shape],
         lam,
         rows,
         sums,
@@ -774,77 +871,73 @@
     sublanes = -(-(width + 4) // 8) * 8
     whole = (19, width, span, height)
     (begun,) = call(start_kernel, [(8, height)], micros=400)
-    fields, rows, near_fields, far_fields = call(
+    fields, first, thrust_rows, slope_rows = call(
         pack_kernel,
         [
             (FIELDS, width, span, height),
-            (2, (HALO + FIELDS) * width, height),
-            (FIELDS, span, height),
-            (FIELDS, span, height),
+            (2, FIRST_ROWS, height),
+            (turbine_rows, height),
+            (turbine_rows, height),
         ],
         begun,
+        thrust.reshape(1, turbines),
         turbine_map,
         fwd_scale,
         fwd_pops,
         seed_adjoint,
         micros=0.6,
     )
-    thrust_rows, slope_rows = call(
-        thrust_kernel,
-        [(turbine_rows, height)] * 2,
-        thrust,
-        fields,
-        smem_first=True,
-        micros=0.3,
-    )
-    if lax.axis_size("gy") == 2:
-        rows = lax.ppermute(rows, "gy", ring("gy", 1))
-    else:
-        rows = jnp.stack(swap_rows(rows[0], rows[1]))
-    far_fields = swap_far(far_fields)
-    edge_coefs, near_fields = call(
-        edge_coef_kernel,
-        [(COEFS, 2, span, height), near_fields.shape],
-        thrust_rows,
-        fields,
-        near_fields,
-        micros=0.3,
-    )
-    near_fields = swap_near(near_fields)
-    face, edge = (FACE_TILES, span, height), (2, 5, sublanes, height)
-    near, far, pack, part_edge = call(
-        faces_kernel,
-        [face, face, (2, FIELDS, sublanes, height), edge],
-        thrust_rows,
-        seed_adjoint,
-        rows,
-        edge_coefs,
-        scratch=[(2, len(PACK_LIST[0]), sublanes, height), face, face],
-        micros=0.6,
-    )
-    far = swap_far(far)
-    near, *coefs = call(
+    first = swap_rows(first)
+    coefs = call(
         coef_kernel,
-        [near.shape] + [(COEFS, width, span, height)] * steps,
+        [(COEFS, width, span, height)] * steps,
         thrust_rows,
         turbine_map,
         fwd_scale,
         fwd_pops,
-        near,
-        micros=1.5,
+        micros=0.8,
+    )
+    (rows,) = call(
+        rows_kernel,
+        [(2, (HALO + FIELDS) * width, height)],
+        seed_adjoint,
+        fields,
+        coefs[2],
+        micros=0.1,
+    )
+    rows = swap_rows(rows)
+    face, edge = (FACE_TILES, span, height), (2, 5, sublanes, height)
+    tile = (19, span, height)
+    (far,) = call(
+        far_kernel,
+        [face],
+        thrust_rows,
+        seed_adjoint,
+        fields,
+        first,
+        coefs[2],
+        scratch=[(20, span, height), tile, tile],
+        micros=2000,
+    )
+    far = swap_far(far)
+    near, pack, part_edge = call(
+        faces_kernel,
+        [face, (2, FIELDS, sublanes, height), edge],
+        thrust_rows,
+        seed_adjoint,
+        fields,
+        rows,
+        coefs[2],
+        scratch=[(2, len(PACK_LIST[0]), sublanes, height), face, face],
+        micros=0.4,
     )
     near = swap_near(near)
-    halo = (FIELDS, span, height)
     parts = call(
         middle_kernel,
-        [whole, (width, span, height), (2, 5, span, height), (2, span, height), (2, span, height)],
-        thrust_rows,
+        [whole, (width, span, height)],
         seed_adjoint,
         rows,
         coefs[2],
-        near_fields,
-        far_fields,
-        scratch=[halo, halo],
         micros=0.6,
     )
     lam, packed = call(
@@ -861,7 +954,14 @@
         *parts,
         part_edge,
         pack,
-        scratch=[(19, 2, span, height), edge, (2, 2, sublanes, height), face, face],
+        scratch=[
+            (19, 2, span, height),
+            edge,
+            (2, 2, sublanes, height),
+            face,
+            face,
+            (2, 5, span, height),
+        ],
         micros=0.8,
     )
     rows, near, far, sums = last_exchange(lam, packed)

time: 33 us -> 32.1 us (0.973)
  starting transfers between devices: 19.7 us -> 16.3 us
  waiting for transfers between devices: 6.74 us -> 9.81 us
  Pallas kernels: 3.85 us -> 3.33 us
    ppermute x3 -> x2, starting transfers between devices: 10.4 us -> 5.64 us  [swap_far(): lax.ppermute(far, 'gx', [(i, (i + 1 if i % 2 else i - 1) % count) for i i...]
    ppermute x1 -> x2, waiting for transfers between devices: 0.01 us -> 2.28 us  [swap_rows(): return lax.ppermute(rows, 'gy', ring('gy', 1))]
    ppermute x1, starting transfers between devices: 1.66 us -> 2.55 us  [last_exchange(): got = lax.ppermute(packed, 'gy', ring('gy', 1))]
    ppermute x5, waiting for transfers between devices: 2.46 us -> 3.34 us  [flips(): lax.ppermute(value, axis, [(i, i ^ flip) for i in range(count)])]
    pallas_call x10, Pallas kernels: 3.85 us -> 3.33 us  [call(): pl.pallas_call(kernel, out_shape=tuple((jax.ShapeDtypeStruct(shape, jnp.f...]
    ppermute x5, starting transfers between devices: 4.46 us -> 4.95 us  [flips(): lax.ppermute(value, axis, [(i, i ^ flip) for i in range(count)])]
    ppermute x1, waiting for transfers between devices: 2.27 us -> 1.85 us  [last_exchange(): got = lax.ppermute(packed, 'gy', ring('gy', 1))]
    ppermute x3 -> x2, waiting for transfers between devices: 2 us -> 2.34 us  [swap_far(): lax.ppermute(far, 'gx', [(i, (i + 1 if i % 2 else i - 1) % count) for i i...]
  transfers between devices with their start and end apart: 13 -> 12, of which waited for: 6 -> 8; matrix products, arithmetic and copies ran while one was open for 0% -> 0% of each run, Pallas kernels for 9% -> 8%
where the time goes in v5:
time: 32.1 us; the launch traced here: 32 us
  starting transfers between devices  16.3 us (51%)
  waiting for transfers between devices  9.81 us (31%)
  Pallas kernels  3.33 us (10%)
  local copies, waits for them, and re-layouts  1.13 us (4%)
  between operations  0.76 us (2%)
  other arithmetic  0.64 us (2%)
    ppermute x2, starting transfers between devices, swap_far(): lax.ppermute(far, 'gx', [(i, (i + 1 if i % 2 else i - 1) % count) for i i...  5.64 us
    ppermute x5, starting transfers between devices, flips(): lax.ppermute(value, axis, [(i, i ^ flip) for i in range(count)])  4.95 us
    ppermute x5, waiting for transfers between devices, flips(): lax.ppermute(value, axis, [(i, i ^ flip) for i in range(count)])  3.34 us
    pallas_call x10, Pallas kernels, call(): pl.pallas_call(kernel, out_shape=tuple((jax.ShapeDtypeStruct(shape, jnp.f...  3.33 us
    ppermute x2, starting transfers between devices, swap_rows(): return lax.ppermute(rows, 'gy', ring('gy', 1))  3.09 us
    ppermute x1, starting transfers between devices, last_exchange(): got = lax.ppermute(packed, 'gy', ring('gy', 1))  2.55 us
    ppermute x2, waiting for transfers between devices, swap_far(): lax.ppermute(far, 'gx', [(i, (i + 1 if i % 2 else i - 1) % count) for i i...  2.34 us
    ppermute x2, waiting for transfers between devices, swap_rows(): return lax.ppermute(rows, 'gy', ring('gy', 1))  2.28 us
  transfers between devices with their start and end apart: 12, of which 8 were waited for; matrix products, arithmetic and copies ran while one was open for 0% of the time, Pallas kernels for 8%

profile of v5, /device:TPU:0, one launch (start us, length us, event | category | flops | bytes accessed | tf_op | source)
XLA Modules:
  0.0 32.0 jit_solution(4822684910820650048)
XLA Ops:
  0.6 0.0 copy-start
  0.6 0.0 copy-start.3
  0.7 0.0 copy-start.2
  0.7 0.0 copy-start.1
  0.7 0.0 copy-start.4
  0.7 0.9 %copy-done = f32[19,4,8,128]{3,2,1,0:T(8,128)S(1)} copy-done((f32[19,4,8,128]{3,2,1,0:T(8,128)S(1)}, f32[19,4,8,128]{3,2,1,0:T(8,128)}, u32[]{:S(2)}) %copy-start) | copy-done | bytes 311320
  1.6 0.0 copy-done.3
  1.6 0.0 copy-done.2
  1.6 0.2 copy-done.1
  1.8 0.0 copy-done.4
  1.8 0.1 shard_map.69
  2.0 3.0 %collective-permute-start.2 = (f32[2,48,128]{2,1,0:T(8,128)S(1)}, f32[2,48,128]{2,1,0:T(8,128)S(1)}, u32[]{:S(2)}, u32[]{:S(2)}) collective-permute-start(f32[2,48,128]{2,1,0:T(8,128)S(1)} %get-tuple-element.23), channel_id=1, source_target_pairs={{0,1},{1,0},{2,3},{3,2},{4,5},{5,4},{6,7},{7,6},{8,9},{9,8},{10,11... | collective-permute-start | bytes 147464 | tf_op jit(solution)/shard_map/ppermute | solution.py:796
  5.0 0.7 %shard_map.70 = (f32[42,4,8,128]{3,2,1,0:T(8,128)S(1)}, f32[42,4,8,128]{3,2,1,0:T(8,128)S(1)}, f32[42,4,8,128]{3,2,1,0:T(8,128)S(1)}) custom-call(f32[16,128]{1,0:T(8,128)S(1)} %get-tuple-element.19.thrust_ref.refs_0_, s32[4,8,128]{2,1,0:T(8,128)S(1)} %copy-done.3, f32[3,4,8,128]{3,2,1,0:T(8,128)S(1)} %copy-done.2, bf16[3,19,4,8,128]{4,3,2,1,0:T(8,128)(2,1)S(1)} %copy-done.1), custom_call_target="tpu_custom_call" | custom-call | flops 800000 | bytes 1600000 | tf_op jit(solution)/shard_map/pallas_call | solution.py:776
  5.7 0.1 shard_map.71
  5.8 0.1 collective-permute-start
  5.9 1.2 %collective-permute-done.2.first_ref = f32[2,48,128]{2,1,0:T(8,128)S(1)} collective-permute-done((f32[2,48,128]{2,1,0:T(8,128)S(1)}, f32[2,48,128]{2,1,0:T(8,128)S(1)}, u32[]{:S(2)}, u32[]{:S(2)}) %collective-permute-start.2) | collective-permute-done | bytes 49184 | tf_op jit(solution)/shard_map/ppermute | solution.py:796
  7.1 0.2 shard_map.73
  7.3 3.4 %collective-permute-start.3 = (f32[38,8,128]{2,1,0:T(8,128)S(1)}, f32[38,8,128]{2,1,0:T(8,128)S(1)}, u32[]{:S(2)}, u32[]{:S(2)}) collective-permute-start(f32[38,8,128]{2,1,0:T(8,128)S(1)} %shard_map.73), channel_id=1, source_target_pairs={{0,30},{2,4},{4,2},{6,8},{8,6},{10,12},{12,10},{14,16},{16,14},{18... | collective-permute-start | bytes 466952 | tf_op jit(solution)/shard_map/ppermute | solution.py:813
  10.7 1.1 %collective-permute-done.rows_ref.refs_2_ = f32[2,168,128]{2,1,0:T(8,128)S(1)} collective-permute-done((f32[2,168,128]{2,1,0:T(8,128)S(1)}, f32[2,168,128]{2,1,0:T(8,128)S(1)}, u32[]{:S(2)}, u32[]{:S(2)}) %collective-permute-start) | collective-permute-done | bytes 172064 | tf_op jit(solution)/shard_map/ppermute | solution.py:796
  11.7 0.3 shard_map.72
  12.0 0.1 collective-permute-start.1
  12.1 0.2 shard_map.74
  12.3 2.3 %collective-permute-done.3.refs_4_ = f32[38,8,128]{2,1,0:T(8,128)S(1)} collective-permute-done((f32[38,8,128]{2,1,0:T(8,128)S(1)}, f32[38,8,128]{2,1,0:T(8,128)S(1)}, u32[]{:S(2)}, u32[]{:S(2)}) %collective-permute-start.3) | collective-permute-done | bytes 155680 | tf_op jit(solution)/shard_map/ppermute | solution.py:813
  14.7 0.0 collective-permute-done.1.refs_3_
  14.7 0.7 %shard_map.75 = (f32[19,4,8,128]{3,2,1,0:T(8,128)S(1)}, f32[56,128]{1,0:T(8,128)S(1)}) custom-call(f32[16,128]{1,0:T(8,128)S(1)} %get-tuple-element.19.thrust_ref.refs_0_, f32[19,4,8,128]{3,2,1,0:T(8,128)S(1)} %copy-done, f32[2,168,128]{2,1,0:T(8,128)S(1)} %collective-permute-done.rows_ref.refs_2_, f32[38,8,128]{2,1,0:T(8,128)S(1)} %collective-permute-done.1.refs_3_, ...), custom_call_target="tpu_custom_call" | custom-call | flops 800000 | bytes 1600000 | tf_op jit(solution)/shard_map/pallas_call | solution.py:776
  15.4 2.5 %collective-permute-start.4 = (f32[56,128]{1,0:T(8,128)S(1)}, f32[56,128]{1,0:T(8,128)S(1)}, u32[]{:S(2)}, u32[]{:S(2)}) collective-permute-start(f32[56,128]{1,0:T(8,128)S(1)} %get-tuple-element.30), channel_id=1, source_target_pairs={{0,1},{1,0},{2,3},{3,2},{4,5},{5,4},{6,7},{7,6},{8,9},{9,8},{10,11... | collective-permute-start | bytes 86024 | tf_op jit(solution)/shard_map/ppermute | solution.py:838
  17.9 1.8 %collective-permute-done.4 = f32[56,128]{1,0:T(8,128)S(1)} collective-permute-done((f32[56,128]{1,0:T(8,128)S(1)}, f32[56,128]{1,0:T(8,128)S(1)}, u32[]{:S(2)}, u32[]{:S(2)}) %collective-permute-start.4) | collective-permute-done | bytes 28704 | tf_op jit(solution)/shard_map/ppermute | solution.py:838
  19.8 0.6 %collective-permute-start.7 = (f32[16,128]{1,0:T(8,128)S(1)}, f32[16,128]{1,0:T(8,128)S(1)}, u32[]{:S(2)}, u32[]{:S(2)}) collective-permute-start(f32[16,128]{1,0:T(8,128)S(1)} %get-tuple-element.35), channel_id=1, source_target_pairs={{0,4},{2,6},{4,0},{6,2},{8,12},{10,14},{12,8},{14,10},{16,20},{18,... | collective-permute-start | bytes 24584 | tf_op jit(solution)/shard_map/ppermute | solution.py:820
  20.4 2.2 %collective-permute-start.6 = (f32[6,8,128]{2,1,0:T(8,128)S(1)}, f32[6,8,128]{2,1,0:T(8,128)S(1)}, u32[]{:S(2)}, u32[]{:S(2)}) collective-permute-start(f32[6,8,128]{2,1,0:T(8,128)S(1)} %get-tuple-element.32), channel_id=1, source_target_pairs={{0,30},{2,4},{4,2},{6,8},{8,6},{10,12},{12,10},{14,16},{16,14},{18... | collective-permute-start | bytes 73736 | tf_op jit(solution)/shard_map/ppermute | solution.py:813
  22.6 0.0 collective-permute-start.5
  22.6 0.9 %collective-permute-done.7 = f32[16,128]{1,0:T(8,128)S(1)} collective-permute-done((f32[16,128]{1,0:T(8,128)S(1)}, f32[16,128]{1,0:T(8,128)S(1)}, u32[]{:S(2)}, u32[]{:S(2)}) %collective-permute-start.7) | collective-permute-done | bytes 8224 | tf_op jit(solution)/shard_map/ppermute | solution.py:820
  23.5 0.0 collective-permute-start.8
  23.6 1.2 %collective-permute-done.8 = f32[16,128]{1,0:T(8,128)S(1)} collective-permute-done((f32[16,128]{1,0:T(8,128)S(1)}, f32[16,128]{1,0:T(8,128)S(1)}, u32[]{:S(2)}, u32[]{:S(2)}) %collective-permute-start.8) | collective-permute-done | bytes 8224 | tf_op jit(solution)/shard_map/ppermute | solution.py:820
  24.7 2.0 %collective-permute-start.11 = (f32[16,128]{1,0:T(8,128)S(1)}, f32[16,128]{1,0:T(8,128)S(1)}, u32[]{:S(2)}, u32[]{:S(2)}) collective-permute-start(f32[16,128]{1,0:T(8,128)S(1)} %add.16), channel_id=1, source_target_pairs={{0,24},{2,26},{4,28},{6,30},{8,16},{10,18},{12,20},{14,22},{16,8},... | collective-permute-start | bytes 24584 | tf_op jit(solution)/shard_map/ppermute | solution.py:820
  26.8 0.0 collective-permute-start.10
  26.8 2.3 %collective-permute-start.9 = (f32[16,128]{1,0:T(8,128)S(1)}, f32[16,128]{1,0:T(8,128)S(1)}, u32[]{:S(2)}, u32[]{:S(2)}) collective-permute-start(f32[16,128]{1,0:T(8,128)S(1)} %add.16), channel_id=1, source_target_pairs={{0,8},{2,10},{4,12},{6,14},{8,0},{10,2},{12,4},{14,6},{16,24},{18,... | collective-permute-start | bytes 24584 | tf_op jit(solution)/shard_map/ppermute | solution.py:820
  29.1 0.0 collective-permute-done.5.near_ref
  29.1 0.0 collective-permute-done.6.far_ref
  29.1 0.9 %shard_map.77 = f32[19,4,8,128]{3,2,1,0:T(8,128)} custom-call(f32[19,4,8,128]{3,2,1,0:T(8,128)S(1)} %get-tuple-element.29.lam_ref, f32[40,128]{1,0:T(8,128)S(1)} %slice.16.rows_ref, f32[5,8,128]{2,1,0:T(8,128)S(1)} %collective-permute-done.5.near_ref, f32[6,8,128]{2,1,0:T(8,128)S(1)} %collective-permute-done.6.far_ref, ...), custom_call_target="tpu_custom_call" | custom-call | flops 500000 | bytes 1000000 | tf_op jit(solution)/shard_map/pallas_call | solution.py:776
  30.1 0.1 collective-permute-done.11
  30.2 1.1 %collective-permute-done.10 = f32[16,128]{1,0:T(8,128)S(1)} collective-permute-done((f32[16,128]{1,0:T(8,128)S(1)}, f32[16,128]{1,0:T(8,128)S(1)}, u32[]{:S(2)}, u32[]{:S(2)}) %collective-permute-start.10) | collective-permute-done | bytes 8224 | tf_op jit(solution)/shard_map/ppermute | solution.py:820
  31.3 0.0 collective-permute-done.9
  31.3 0.6 %fusion = f32[10]{0:T(128)} fusion(f32[16,128]{1,0:T(8,128)S(1)} %get-tuple-element.34, f32[16,128]{1,0:T(8,128)S(1)} %collective-permute-done.11, f32[16,128]{1,0:T(8,128)S(1)} %collective-permute-done.10, f32[16,128]{1,0:T(8,128)S(1)} %collective-permute-done.9, f32[16,128]{1,0:T(8,128)S(1)} %add.16), kind=kLoop, calls=%fused_computation.1 | loop fusion | flops 6390 | bytes 25640 | tf_op jit(solution)/shard_map/reduce_sum | solution.py:969
  (7 shorter events, 0.0 us)
Async XLA Ops:
  0.6 1.0 %copy-start = (f32[19,4,8,128]{3,2,1,0:T(8,128)S(1)}, f32[19,4,8,128]{3,2,1,0:T(8,128)}, u32[]{:S(2)}) copy-start(f32[19,4,8,128]{3,2,1,0:T(8,128)} %refs_1_.1) | copy-start | bytes 933892
  0.6 1.0 %copy-start.3 = (s32[4,8,128]{2,1,0:T(8,128)S(1)}, s32[4,8,128]{2,1,0:T(8,128)}, u32[]{:S(2)}) copy-start(s32[4,8,128]{2,1,0:T(8,128)} %map_ref.3) | copy-start | bytes 49156
  0.7 1.0 %copy-start.2 = (f32[3,4,8,128]{3,2,1,0:T(8,128)S(1)}, f32[3,4,8,128]{3,2,1,0:T(8,128)}, u32[]{:S(2)}) copy-start(f32[3,4,8,128]{3,2,1,0:T(8,128)} %scale_ref.3) | copy-start | bytes 147460
  0.7 1.1 %copy-start.1 = (bf16[3,19,4,8,128]{4,3,2,1,0:T(8,128)(2,1)S(1)}, bf16[3,19,4,8,128]{4,3,2,1,0:T(8,128)(2,1)}, u32[]{:S(2)}) copy-start(bf16[3,19,4,8,128]{4,3,2,1,0:T(8,128)(2,1)} %pops_ref.3) | copy-start | bytes 1400836
  0.7 1.1 %copy-start.4 = (f32[10]{0:T(128)S(1)}, f32[10]{0:T(128)}, u32[]{:S(2)}) copy-start(f32[10]{0:T(128)} %param.9) | copy-start | bytes 124
  2.0 5.1 %collective-permute-start.2 = (f32[2,48,128]{2,1,0:T(8,128)S(1)}, f32[2,48,128]{2,1,0:T(8,128)S(1)}, u32[]{:S(2)}, u32[]{:S(2)}) collective-permute-start(f32[2,48,128]{2,1,0:T(8,128)S(1)} %get-tuple-element.23), channel_id=1, source_target_pairs={{0,1},{1,0},{2,3},{3,2},{4,5},{5,4},{6,7},{7,6},{8,9},{9,8},{10,11... | collective-permute-start | bytes 147464 | tf_op jit(solution)/shard_map/ppermute | solution.py:796
  5.8 5.9 %collective-permute-start = (f32[2,168,128]{2,1,0:T(8,128)S(1)}, f32[2,168,128]{2,1,0:T(8,128)S(1)}, u32[]{:S(2)}, u32[]{:S(2)}) collective-permute-start(f32[2,168,128]{2,1,0:T(8,128)S(1)} %shard_map.71), channel_id=1, source_target_pairs={{0,1},{1,0},{2,3},{3,2},{4,5},{5,4},{6,7},{7,6},{8,9},{9,8},{10,11... | collective-permute-start | bytes 516104 | tf_op jit(solution)/shard_map/ppermute | solution.py:796
  7.3 7.4 %collective-permute-start.3 = (f32[38,8,128]{2,1,0:T(8,128)S(1)}, f32[38,8,128]{2,1,0:T(8,128)S(1)}, u32[]{:S(2)}, u32[]{:S(2)}) collective-permute-start(f32[38,8,128]{2,1,0:T(8,128)S(1)} %shard_map.73), channel_id=1, source_target_pairs={{0,30},{2,4},{4,2},{6,8},{8,6},{10,12},{12,10},{14,16},{16,14},{18... | collective-permute-start | bytes 466952 | tf_op jit(solution)/shard_map/ppermute | solution.py:813
  12.0 2.6 %collective-permute-start.1 = (f32[38,8,128]{2,1,0:T(8,128)S(1)}, f32[38,8,128]{2,1,0:T(8,128)S(1)}, u32[]{:S(2)}, u32[]{:S(2)}) collective-permute-start(f32[38,8,128]{2,1,0:T(8,128)S(1)} %get-tuple-element.22), channel_id=1, source_target_pairs={{0,2},{2,0},{4,6},{6,4},{8,10},{10,8},{12,14},{14,12},{16,18},{18,... | collective-permute-start | bytes 466952 | tf_op jit(solution)/shard_map/ppermute | solution.py:808
  15.4 4.4 %collective-permute-start.4 = (f32[56,128]{1,0:T(8,128)S(1)}, f32[56,128]{1,0:T(8,128)S(1)}, u32[]{:S(2)}, u32[]{:S(2)}) collective-permute-start(f32[56,128]{1,0:T(8,128)S(1)} %get-tuple-element.30), channel_id=1, source_target_pairs={{0,1},{1,0},{2,3},{3,2},{4,5},{5,4},{6,7},{7,6},{8,9},{9,8},{10,11... | collective-permute-start | bytes 86024 | tf_op jit(solution)/shard_map/ppermute | solution.py:838
  19.8 3.7 %collective-permute-start.7 = (f32[16,128]{1,0:T(8,128)S(1)}, f32[16,128]{1,0:T(8,128)S(1)}, u32[]{:S(2)}, u32[]{:S(2)}) collective-permute-start(f32[16,128]{1,0:T(8,128)S(1)} %get-tuple-element.35), channel_id=1, source_target_pairs={{0,4},{2,6},{4,0},{6,2},{8,12},{10,14},{12,8},{14,10},{16,20},{18,... | collective-permute-start | bytes 24584 | tf_op jit(solution)/shard_map/ppermute | solution.py:820
  20.4 8.7 %collective-permute-start.6 = (f32[6,8,128]{2,1,0:T(8,128)S(1)}, f32[6,8,128]{2,1,0:T(8,128)S(1)}, u32[]{:S(2)}, u32[]{:S(2)}) collective-permute-start(f32[6,8,128]{2,1,0:T(8,128)S(1)} %get-tuple-element.32), channel_id=1, source_target_pairs={{0,30},{2,4},{4,2},{6,8},{8,6},{10,12},{12,10},{14,16},{16,14},{18... | collective-permute-start | bytes 73736 | tf_op jit(solution)/shard_map/ppermute | solution.py:813
  22.6 6.5 %collective-permute-start.5 = (f32[5,8,128]{2,1,0:T(8,128)S(1)}, f32[5,8,128]{2,1,0:T(8,128)S(1)}, u32[]{:S(2)}, u32[]{:S(2)}) collective-permute-start(f32[5,8,128]{2,1,0:T(8,128)S(1)} %get-tuple-element.31), channel_id=1, source_target_pairs={{0,2},{2,0},{4,6},{6,4},{8,10},{10,8},{12,14},{14,12},{16,18},{18,... | collective-permute-start | bytes 61448 | tf_op jit(solution)/shard_map/ppermute | solution.py:808
  23.5 1.2 %collective-permute-start.8 = (f32[16,128]{1,0:T(8,128)S(1)}, f32[16,128]{1,0:T(8,128)S(1)}, u32[]{:S(2)}, u32[]{:S(2)}) collective-permute-start(f32[16,128]{1,0:T(8,128)S(1)} %add.15), channel_id=1, source_target_pairs={{0,2},{2,0},{4,6},{6,4},{8,10},{10,8},{12,14},{14,12},{16,18},{18,... | collective-permute-start | bytes 24584 | tf_op jit(solution)/shard_map/ppermute | solution.py:820
  24.7 5.4 %collective-permute-start.11 = (f32[16,128]{1,0:T(8,128)S(1)}, f32[16,128]{1,0:T(8,128)S(1)}, u32[]{:S(2)}, u32[]{:S(2)}) collective-permute-start(f32[16,128]{1,0:T(8,128)S(1)} %add.16), channel_id=1, source_target_pairs={{0,24},{2,26},{4,28},{6,30},{8,16},{10,18},{12,20},{14,22},{16,8},... | collective-permute-start | bytes 24584 | tf_op jit(solution)/shard_map/ppermute | solution.py:820
  26.8 4.5 %collective-permute-start.10 = (f32[16,128]{1,0:T(8,128)S(1)}, f32[16,128]{1,0:T(8,128)S(1)}, u32[]{:S(2)}, u32[]{:S(2)}) collective-permute-start(f32[16,128]{1,0:T(8,128)S(1)} %add.16), channel_id=1, source_target_pairs={{0,16},{2,18},{4,20},{6,22},{8,24},{10,26},{12,28},{14,30},{16,0},... | collective-permute-start | bytes 24584 | tf_op jit(solution)/shard_map/ppermute | solution.py:820
  26.8 4.5 %collective-permute-start.9 = (f32[16,128]{1,0:T(8,128)S(1)}, f32[16,128]{1,0:T(8,128)S(1)}, u32[]{:S(2)}, u32[]{:S(2)}) collective-permute-start(f32[16,128]{1,0:T(8,128)S(1)} %add.16), channel_id=1, source_target_pairs={{0,8},{2,10},{4,12},{6,14},{8,0},{10,2},{12,4},{14,6},{16,24},{18,... | collective-permute-start | bytes 24584 | tf_op jit(solution)/shard_map/ppermute | solution.py:820

commit v6 on v5

--- a/solution.py
+++ b/solution.py
@@ -713,7 +713,7 @@
         next_ref[start + turbine : start + turbine + 1, :] = row
 
 
-def last_faces_kernel(lam_ref, rows_ref, sums_ref, got_ref, near_ref, far_ref, total_ref):
+def last_faces_kernel(lam_ref, rows_ref, near_ref, far_ref):
     width = lam_ref.shape[1]
 
     def row_of(side, plane, member):
@@ -730,9 +730,12 @@
 
         return tile
 
-    total_ref[...] = sums_ref[...] + got_ref[...]
     far_ref[5:] = jnp.zeros((far_ref.shape[0] - 5,) + far_ref.shape[1:], jnp.float32)
     hand_out(moved(X_UP, 0), moved(X_DOWN, width - 1), near_ref, far_ref.at[0:5])
+
+
+def pass_kernel(value_ref, _, out_ref):
+    out_ref[...] = value_ref[...]
 
 
 def last_kernel(lam_ref, rows_ref, near_ref, far_ref, coef_ref, out_ref):
@@ -834,29 +837,34 @@
     width, height = lam.shape[1], lam.shape[3]
     rows_count = 10 * width
     sums = packed[rows_count:]
-    if lax.axis_size("gy") == 2:
+    count = lax.axis_size("gx")
+    apart = count & (count - 1) == 0 and count > 2
+    joined = apart and lax.axis_size("gy") == 2
+    if joined:
         got = lax.ppermute(packed, "gy", ring("gy", 1))
         rows, got = got[:rows_count], got[rows_count:]
+        got = got + lax.ppermute(sums, "gx", [(i, i ^ 2) for i in range(count)])
+        got = got + lax.ppermute(
+            sums, ("gx", "gy"), [(i, i ^ 5) for i in range(2 * count)]
+        )
     else:
         rows = swap_rows(packed[:rows_count].reshape(2, rows_count // 2, -1))
         rows = rows.reshape(rows_count, -1)
-        count = lax.axis_size("gy")
-        got = (lax.psum(sums, "gy") if count & (count - 1) else sum_bits(sums, "gy", 1)) - sums
-    near, far, sums = call(
+        spans = lax.axis_size("gy")
+        got = (lax.psum(sums, "gy") if spans & (spans - 1) else sum_bits(sums, "gy", 1)) - sums
+    near, far = call(
         last_faces_kernel,
-        [(5, lam.shape[2], height), (6, lam.shape[2], height), sums.shape],
+        [(5, lam.shape[2], height), (6, lam.shape[2], height)],
         lam,
         rows,
-        sums,
-        got,
         micros=0.1,
     )
-    count = lax.axis_size("gx")
-    apart = count & (count - 1) == 0 and count > 2
-    if apart:
+    sums = sums + got
+    if apart and not joined:
         sums = flips(sums, "gx", [2])
     got_near, got_far = swap_near(near), swap_far(far)
     if apart:
+        (sums,) = call(pass_kernel, [sums.shape], sums, got_near, micros=0.1)
         sums = sum_bits(flips(sums, "gx", [1]), "gx", 4)
     else:
         sums = lax.psum(sums, "gx")

time: 32.1 us -> 31.8 us (level)
  waiting for transfers between devices: 9.81 us -> 6.98 us
  starting transfers between devices: 16.3 us -> 18.8 us
    ppermute x1, waiting for transfers between devices: 1.85 us -> 0.3 us  [last_exchange(): got = lax.ppermute(packed, 'gy', ring('gy', 1))]
    ppermute x0 -> x2, starting transfers between devices: none -> 1.55 us  [the longest x1 1.55 us: last_exchange(): got = got + lax.ppermute(sums, 'gx', [(i, i ^ 2) for i in range(count)])]
    ppermute x2, starting transfers between devices: 5.64 us -> 6.98 us  [swap_far(): lax.ppermute(far, 'gx', [(i, (i + 1 if i % 2 else i - 1) % count) for i i...]
    ppermute x5 -> x4, waiting for transfers between devices: 3.34 us -> 2.05 us  [flips(): lax.ppermute(value, axis, [(i, i ^ flip) for i in range(count)])]
    ppermute x5 -> x4, starting transfers between devices: 4.95 us -> 4.46 us  [flips(): lax.ppermute(value, axis, [(i, i ^ flip) for i in range(count)])]
    pallas_call x10 -> x11, Pallas kernels: 3.33 us -> 3.32 us  [call(): pl.pallas_call(kernel, out_shape=tuple((jax.ShapeDtypeStruct(shape, jnp.f...]
  transfers between devices with their start and end apart: 12 -> 13, of which waited for: 8 -> 7; matrix products, arithmetic and copies ran while one was open for 0% -> 0% of each run, Pallas kernels for 8% -> 8%
where the time goes in v6:
time: 31.8 us; the launch traced here: 31.6 us
  starting transfers between devices  18.8 us (59%)
  waiting for transfers between devices  6.98 us (22%)
  Pallas kernels  3.32 us (10%)
  local copies, waits for them, and re-layouts  1.13 us (4%)
  between operations  0.79 us (2%)
  other arithmetic  0.64 us (2%)
    ppermute x2, starting transfers between devices, swap_far(): lax.ppermute(far, 'gx', [(i, (i + 1 if i % 2 else i - 1) % count) for i i...  6.98 us
    ppermute x4, starting transfers between devices, flips(): lax.ppermute(value, axis, [(i, i ^ flip) for i in range(count)])  4.46 us
    pallas_call x11, Pallas kernels, call(): pl.pallas_call(kernel, out_shape=tuple((jax.ShapeDtypeStruct(shape, jnp.f...  3.32 us
    ppermute x2, starting transfers between devices, swap_rows(): return lax.ppermute(rows, 'gy', ring('gy', 1))  3.09 us
    ppermute x1, starting transfers between devices, last_exchange(): got = lax.ppermute(packed, 'gy', ring('gy', 1))  2.55 us
    ppermute x2, waiting for transfers between devices, swap_far(): lax.ppermute(far, 'gx', [(i, (i + 1 if i % 2 else i - 1) % count) for i i...  2.34 us
    ppermute x2, waiting for transfers between devices, swap_rows(): return lax.ppermute(rows, 'gy', ring('gy', 1))  2.28 us
    ppermute x4, waiting for transfers between devices, flips(): lax.ppermute(value, axis, [(i, i ^ flip) for i in range(count)])  2.05 us
  transfers between devices with their start and end apart: 13, of which 7 were waited for; matrix products, arithmetic and copies ran while one was open for 0% of the time, Pallas kernels for 8%

profile of v6, /device:TPU:0, one launch (start us, length us, event | category | flops | bytes accessed | tf_op | source)
XLA Modules:
  0.0 31.6 jit_solution(15413938258582402302)
XLA Ops:
  0.6 0.0 copy-start
  0.6 0.0 copy-start.3
  0.7 0.0 copy-start.2
  0.7 0.0 copy-start.1
  0.7 0.0 copy-start.4
  0.7 0.9 %copy-done = f32[19,4,8,128]{3,2,1,0:T(8,128)S(1)} copy-done((f32[19,4,8,128]{3,2,1,0:T(8,128)S(1)}, f32[19,4,8,128]{3,2,1,0:T(8,128)}, u32[]{:S(2)}) %copy-start) | copy-done | bytes 311320
  1.6 0.0 copy-done.3
  1.6 0.0 copy-done.2
  1.6 0.2 copy-done.1
  1.8 0.0 copy-done.4
  1.8 0.1 shard_map.69
  2.0 3.0 %collective-permute-start.2 = (f32[2,48,128]{2,1,0:T(8,128)S(1)}, f32[2,48,128]{2,1,0:T(8,128)S(1)}, u32[]{:S(2)}, u32[]{:S(2)}) collective-permute-start(f32[2,48,128]{2,1,0:T(8,128)S(1)} %get-tuple-element.22), channel_id=1, source_target_pairs={{0,1},{1,0},{2,3},{3,2},{4,5},{5,4},{6,7},{7,6},{8,9},{9,8},{10,11... | collective-permute-start | bytes 147464 | tf_op jit(solution)/shard_map/ppermute | solution.py:799
  5.0 0.7 %shard_map.70 = (f32[42,4,8,128]{3,2,1,0:T(8,128)S(1)}, f32[42,4,8,128]{3,2,1,0:T(8,128)S(1)}, f32[42,4,8,128]{3,2,1,0:T(8,128)S(1)}) custom-call(f32[16,128]{1,0:T(8,128)S(1)} %get-tuple-element.18.thrust_ref.refs_0_, s32[4,8,128]{2,1,0:T(8,128)S(1)} %copy-done.3, f32[3,4,8,128]{3,2,1,0:T(8,128)S(1)} %copy-done.2, bf16[3,19,4,8,128]{4,3,2,1,0:T(8,128)(2,1)S(1)} %copy-done.1), custom_call_target="tpu_custom_call" | custom-call | flops 800000 | bytes 1600000 | tf_op jit(solution)/shard_map/pallas_call | solution.py:779
  5.7 0.1 shard_map.71
  5.8 0.1 collective-permute-start
  5.9 1.2 %collective-permute-done.2.first_ref = f32[2,48,128]{2,1,0:T(8,128)S(1)} collective-permute-done((f32[2,48,128]{2,1,0:T(8,128)S(1)}, f32[2,48,128]{2,1,0:T(8,128)S(1)}, u32[]{:S(2)}, u32[]{:S(2)}) %collective-permute-start.2) | collective-permute-done | bytes 49184 | tf_op jit(solution)/shard_map/ppermute | solution.py:799
  7.1 0.2 shard_map.73
  7.3 3.4 %collective-permute-start.3 = (f32[38,8,128]{2,1,0:T(8,128)S(1)}, f32[38,8,128]{2,1,0:T(8,128)S(1)}, u32[]{:S(2)}, u32[]{:S(2)}) collective-permute-start(f32[38,8,128]{2,1,0:T(8,128)S(1)} %shard_map.73), channel_id=1, source_target_pairs={{0,30},{2,4},{4,2},{6,8},{8,6},{10,12},{12,10},{14,16},{16,14},{18... | collective-permute-start | bytes 466952 | tf_op jit(solution)/shard_map/ppermute | solution.py:816
  10.7 1.1 %collective-permute-done.rows_ref.refs_2_ = f32[2,168,128]{2,1,0:T(8,128)S(1)} collective-permute-done((f32[2,168,128]{2,1,0:T(8,128)S(1)}, f32[2,168,128]{2,1,0:T(8,128)S(1)}, u32[]{:S(2)}, u32[]{:S(2)}) %collective-permute-start) | collective-permute-done | bytes 172064 | tf_op jit(solution)/shard_map/ppermute | solution.py:799
  11.7 0.3 %shard_map.72 = (f32[38,8,128]{2,1,0:T(8,128)S(1)}, f32[2,21,8,128]{3,2,1,0:T(8,128)S(1)}, f32[2,5,8,128]{3,2,1,0:T(8,128)S(1)}) custom-call(f32[16,128]{1,0:T(8,128)S(1)} %get-tuple-element.18.thrust_ref.refs_0_, f32[19,4,8,128]{3,2,1,0:T(8,128)S(1)} %copy-done, f32[21,4,8,128]{3,2,1,0:T(8,128)S(1)} %get-tuple-element.19.fields_ref.refs_7_, ...), custom_call_target="tpu_custom_call" | custom-call | flops 400000 | bytes 800000 | tf_op jit(solution)/shard_map/pallas_call | solution.py:779
  12.0 0.1 collective-permute-start.1
  12.1 0.2 shard_map.74
  12.3 2.3 %collective-permute-done.3.refs_4_ = f32[38,8,128]{2,1,0:T(8,128)S(1)} collective-permute-done((f32[38,8,128]{2,1,0:T(8,128)S(1)}, f32[38,8,128]{2,1,0:T(8,128)S(1)}, u32[]{:S(2)}, u32[]{:S(2)}) %collective-permute-start.3) | collective-permute-done | bytes 155680 | tf_op jit(solution)/shard_map/ppermute | solution.py:816
  14.7 0.0 collective-permute-done.1.refs_3_
  14.7 0.7 %shard_map.75 = (f32[19,4,8,128]{3,2,1,0:T(8,128)S(1)}, f32[56,128]{1,0:T(8,128)S(1)}) custom-call(f32[16,128]{1,0:T(8,128)S(1)} %get-tuple-element.18.thrust_ref.refs_0_, f32[19,4,8,128]{3,2,1,0:T(8,128)S(1)} %copy-done, f32[2,168,128]{2,1,0:T(8,128)S(1)} %collective-permute-done.rows_ref.refs_2_, f32[38,8,128]{2,1,0:T(8,128)S(1)} %collective-permute-done.1.refs_3_, ...), custom_call_target="tpu_custom_call" | custom-call | flops 800000 | bytes 1600000 | tf_op jit(solution)/shard_map/pallas_call | solution.py:779
  15.4 2.5 %collective-permute-start.4 = (f32[56,128]{1,0:T(8,128)S(1)}, f32[56,128]{1,0:T(8,128)S(1)}, u32[]{:S(2)}, u32[]{:S(2)}) collective-permute-start(f32[56,128]{1,0:T(8,128)S(1)} %get-tuple-element.29), channel_id=1, source_target_pairs={{0,1},{1,0},{2,3},{3,2},{4,5},{5,4},{6,7},{7,6},{8,9},{9,8},{10,11... | collective-permute-start | bytes 86024 | tf_op jit(solution)/shard_map/ppermute | solution.py:844
  17.9 0.0 collective-permute-start.8
  18.0 1.5 %collective-permute-start.7 = (f32[16,128]{1,0:T(8,128)S(1)}, f32[16,128]{1,0:T(8,128)S(1)}, u32[]{:S(2)}, u32[]{:S(2)}) collective-permute-start(f32[16,128]{1,0:T(8,128)S(1)} %slice.13), channel_id=1, source_target_pairs={{0,4},{2,6},{4,0},{6,2},{8,12},{10,14},{12,8},{14,10},{16,20},{18,... | collective-permute-start | bytes 24584 | tf_op jit(solution)/shard_map/ppermute | solution.py:846
  19.5 0.3 collective-permute-done.4
  19.8 0.1 collective-permute-start.5
  19.9 3.6 %collective-permute-start.6 = (f32[6,8,128]{2,1,0:T(8,128)S(1)}, f32[6,8,128]{2,1,0:T(8,128)S(1)}, u32[]{:S(2)}, u32[]{:S(2)}) collective-permute-start(f32[6,8,128]{2,1,0:T(8,128)S(1)} %get-tuple-element.31), channel_id=1, source_target_pairs={{0,30},{2,4},{4,2},{6,8},{8,6},{10,12},{12,10},{14,16},{16,14},{18... | collective-permute-start | bytes 73736 | tf_op jit(solution)/shard_map/ppermute | solution.py:816
  23.5 0.0 collective-permute-done.8
  23.5 0.0 collective-permute-done.7
  23.5 0.0 collective-permute-done.5.near_ref._
  23.5 0.1 collective-permute-start.9
  23.6 1.2 %collective-permute-done.9 = f32[16,128]{1,0:T(8,128)S(1)} collective-permute-done((f32[16,128]{1,0:T(8,128)S(1)}, f32[16,128]{1,0:T(8,128)S(1)}, u32[]{:S(2)}, u32[]{:S(2)}) %collective-permute-start.9) | collective-permute-done | bytes 8224 | tf_op jit(solution)/shard_map/ppermute | solution.py:823
  24.8 1.7 %collective-permute-start.12 = (f32[16,128]{1,0:T(8,128)S(1)}, f32[16,128]{1,0:T(8,128)S(1)}, u32[]{:S(2)}, u32[]{:S(2)}) collective-permute-start(f32[16,128]{1,0:T(8,128)S(1)} %add.24), channel_id=1, source_target_pairs={{0,24},{2,26},{4,28},{6,30},{8,16},{10,18},{12,20},{14,22},{16,8},... | collective-permute-start | bytes 24584 | tf_op jit(solution)/shard_map/ppermute | solution.py:823
  26.4 0.0 collective-permute-start.11
  26.4 2.7 %collective-permute-start.10 = (f32[16,128]{1,0:T(8,128)S(1)}, f32[16,128]{1,0:T(8,128)S(1)}, u32[]{:S(2)}, u32[]{:S(2)}) collective-permute-start(f32[16,128]{1,0:T(8,128)S(1)} %add.24), channel_id=1, source_target_pairs={{0,8},{2,10},{4,12},{6,14},{8,0},{10,2},{12,4},{14,6},{16,24},{18,... | collective-permute-start | bytes 24584 | tf_op jit(solution)/shard_map/ppermute | solution.py:823
  29.2 0.0 collective-permute-done.6.far_ref
  29.2 0.9 %shard_map.77 = f32[19,4,8,128]{3,2,1,0:T(8,128)} custom-call(f32[19,4,8,128]{3,2,1,0:T(8,128)S(1)} %get-tuple-element.28.lam_ref, f32[40,128]{1,0:T(8,128)S(1)} %slice.16.rows_ref, f32[5,8,128]{2,1,0:T(8,128)S(1)} %collective-permute-done.5.near_ref._, f32[6,8,128]{2,1,0:T(8,128)S(1)} %collective-permute-done.6.far_ref, ...), custom_call_target="tpu_custom_call" | custom-call | flops 500000 | bytes 1000000 | tf_op jit(solution)/shard_map/pallas_call | solution.py:779
  30.1 0.1 collective-permute-done.12
  30.2 0.8 %collective-permute-done.11 = f32[16,128]{1,0:T(8,128)S(1)} collective-permute-done((f32[16,128]{1,0:T(8,128)S(1)}, f32[16,128]{1,0:T(8,128)S(1)}, u32[]{:S(2)}, u32[]{:S(2)}) %collective-permute-start.11) | collective-permute-done | bytes 8224 | tf_op jit(solution)/shard_map/ppermute | solution.py:823
  31.0 0.0 collective-permute-done.10
  31.0 0.6 %fusion = f32[10]{0:T(128)} fusion(f32[16,128]{1,0:T(8,128)S(1)} %get-tuple-element.33, f32[16,128]{1,0:T(8,128)S(1)} %collective-permute-done.12, f32[16,128]{1,0:T(8,128)S(1)} %collective-permute-done.11, f32[16,128]{1,0:T(8,128)S(1)} %collective-permute-done.10, f32[16,128]{1,0:T(8,128)S(1)} %add.24), kind=kLoop, calls=%fused_computation.1 | loop fusion | flops 6390 | bytes 25640 | tf_op jit(solution)/shard_map/reduce_sum | solution.py:977
  (7 shorter events, 0.0 us)
Async XLA Ops:
  0.6 1.0 %copy-start = (f32[19,4,8,128]{3,2,1,0:T(8,128)S(1)}, f32[19,4,8,128]{3,2,1,0:T(8,128)}, u32[]{:S(2)}) copy-start(f32[19,4,8,128]{3,2,1,0:T(8,128)} %refs_1_.1) | copy-start | bytes 933892
  0.6 1.0 %copy-start.3 = (s32[4,8,128]{2,1,0:T(8,128)S(1)}, s32[4,8,128]{2,1,0:T(8,128)}, u32[]{:S(2)}) copy-start(s32[4,8,128]{2,1,0:T(8,128)} %map_ref.3) | copy-start | bytes 49156
  0.7 1.0 %copy-start.2 = (f32[3,4,8,128]{3,2,1,0:T(8,128)S(1)}, f32[3,4,8,128]{3,2,1,0:T(8,128)}, u32[]{:S(2)}) copy-start(f32[3,4,8,128]{3,2,1,0:T(8,128)} %scale_ref.3) | copy-start | bytes 147460
  0.7 1.1 %copy-start.1 = (bf16[3,19,4,8,128]{4,3,2,1,0:T(8,128)(2,1)S(1)}, bf16[3,19,4,8,128]{4,3,2,1,0:T(8,128)(2,1)}, u32[]{:S(2)}) copy-start(bf16[3,19,4,8,128]{4,3,2,1,0:T(8,128)(2,1)} %pops_ref.3) | copy-start | bytes 1400836
  0.7 1.1 %copy-start.4 = (f32[10]{0:T(128)S(1)}, f32[10]{0:T(128)}, u32[]{:S(2)}) copy-start(f32[10]{0:T(128)} %param.9) | copy-start | bytes 124
  2.0 5.1 %collective-permute-start.2 = (f32[2,48,128]{2,1,0:T(8,128)S(1)}, f32[2,48,128]{2,1,0:T(8,128)S(1)}, u32[]{:S(2)}, u32[]{:S(2)}) collective-permute-start(f32[2,48,128]{2,1,0:T(8,128)S(1)} %get-tuple-element.22), channel_id=1, source_target_pairs={{0,1},{1,0},{2,3},{3,2},{4,5},{5,4},{6,7},{7,6},{8,9},{9,8},{10,11... | collective-permute-start | bytes 147464 | tf_op jit(solution)/shard_map/ppermute | solution.py:799
  5.8 5.9 %collective-permute-start = (f32[2,168,128]{2,1,0:T(8,128)S(1)}, f32[2,168,128]{2,1,0:T(8,128)S(1)}, u32[]{:S(2)}, u32[]{:S(2)}) collective-permute-start(f32[2,168,128]{2,1,0:T(8,128)S(1)} %shard_map.71), channel_id=1, source_target_pairs={{0,1},{1,0},{2,3},{3,2},{4,5},{5,4},{6,7},{7,6},{8,9},{9,8},{10,11... | collective-permute-start | bytes 516104 | tf_op jit(solution)/shard_map/ppermute | solution.py:799
  7.3 7.4 %collective-permute-start.3 = (f32[38,8,128]{2,1,0:T(8,128)S(1)}, f32[38,8,128]{2,1,0:T(8,128)S(1)}, u32[]{:S(2)}, u32[]{:S(2)}) collective-permute-start(f32[38,8,128]{2,1,0:T(8,128)S(1)} %shard_map.73), channel_id=1, source_target_pairs={{0,30},{2,4},{4,2},{6,8},{8,6},{10,12},{12,10},{14,16},{16,14},{18... | collective-permute-start | bytes 466952 | tf_op jit(solution)/shard_map/ppermute | solution.py:816
  12.0 2.6 %collective-permute-start.1 = (f32[38,8,128]{2,1,0:T(8,128)S(1)}, f32[38,8,128]{2,1,0:T(8,128)S(1)}, u32[]{:S(2)}, u32[]{:S(2)}) collective-permute-start(f32[38,8,128]{2,1,0:T(8,128)S(1)} %get-tuple-element.21), channel_id=1, source_target_pairs={{0,2},{2,0},{4,6},{6,4},{8,10},{10,8},{12,14},{14,12},{16,18},{18,... | collective-permute-start | bytes 466952 | tf_op jit(solution)/shard_map/ppermute | solution.py:811
  15.4 4.4 %collective-permute-start.4 = (f32[56,128]{1,0:T(8,128)S(1)}, f32[56,128]{1,0:T(8,128)S(1)}, u32[]{:S(2)}, u32[]{:S(2)}) collective-permute-start(f32[56,128]{1,0:T(8,128)S(1)} %get-tuple-element.29), channel_id=1, source_target_pairs={{0,1},{1,0},{2,3},{3,2},{4,5},{5,4},{6,7},{7,6},{8,9},{9,8},{10,11... | collective-permute-start | bytes 86024 | tf_op jit(solution)/shard_map/ppermute | solution.py:844
  17.9 5.5 %collective-permute-start.8 = (f32[16,128]{1,0:T(8,128)S(1)}, f32[16,128]{1,0:T(8,128)S(1)}, u32[]{:S(2)}, u32[]{:S(2)}) collective-permute-start(f32[16,128]{1,0:T(8,128)S(1)} %slice.13), channel_id=1, source_target_pairs={{0,5},{1,4},{2,7},{3,6},{4,1},{5,0},{6,3},{7,2},{8,13},{9,12},{10,... | collective-permute-start | bytes 24584 | tf_op jit(solution)/shard_map/ppermute | solution.py:847
  18.0 5.5 %collective-permute-start.7 = (f32[16,128]{1,0:T(8,128)S(1)}, f32[16,128]{1,0:T(8,128)S(1)}, u32[]{:S(2)}, u32[]{:S(2)}) collective-permute-start(f32[16,128]{1,0:T(8,128)S(1)} %slice.13), channel_id=1, source_target_pairs={{0,4},{2,6},{4,0},{6,2},{8,12},{10,14},{12,8},{14,10},{16,20},{18,... | collective-permute-start | bytes 24584 | tf_op jit(solution)/shard_map/ppermute | solution.py:846
  19.8 3.7 %collective-permute-start.5 = (f32[5,8,128]{2,1,0:T(8,128)S(1)}, f32[5,8,128]{2,1,0:T(8,128)S(1)}, u32[]{:S(2)}, u32[]{:S(2)}) collective-permute-start(f32[5,8,128]{2,1,0:T(8,128)S(1)} %get-tuple-element.30), channel_id=1, source_target_pairs={{0,2},{2,0},{4,6},{6,4},{8,10},{10,8},{12,14},{14,12},{16,18},{18,... | collective-permute-start | bytes 61448 | tf_op jit(solution)/shard_map/ppermute | solution.py:811
  19.9 9.3 %collective-permute-start.6 = (f32[6,8,128]{2,1,0:T(8,128)S(1)}, f32[6,8,128]{2,1,0:T(8,128)S(1)}, u32[]{:S(2)}, u32[]{:S(2)}) collective-permute-start(f32[6,8,128]{2,1,0:T(8,128)S(1)} %get-tuple-element.31), channel_id=1, source_target_pairs={{0,30},{2,4},{4,2},{6,8},{8,6},{10,12},{12,10},{14,16},{16,14},{18... | collective-permute-start | bytes 73736 | tf_op jit(solution)/shard_map/ppermute | solution.py:816
  23.5 1.2 %collective-permute-start.9 = (f32[16,128]{1,0:T(8,128)S(1)}, f32[16,128]{1,0:T(8,128)S(1)}, u32[]{:S(2)}, u32[]{:S(2)}) collective-permute-start(f32[16,128]{1,0:T(8,128)S(1)} %shard_map.78), channel_id=1, source_target_pairs={{0,2},{2,0},{4,6},{6,4},{8,10},{10,8},{12,14},{14,12},{16,18},{18,... | collective-permute-start | bytes 24584 | tf_op jit(solution)/shard_map/ppermute | solution.py:823
  24.8 5.4 %collective-permute-start.12 = (f32[16,128]{1,0:T(8,128)S(1)}, f32[16,128]{1,0:T(8,128)S(1)}, u32[]{:S(2)}, u32[]{:S(2)}) collective-permute-start(f32[16,128]{1,0:T(8,128)S(1)} %add.24), channel_id=1, source_target_pairs={{0,24},{2,26},{4,28},{6,30},{8,16},{10,18},{12,20},{14,22},{16,8},... | collective-permute-start | bytes 24584 | tf_op jit(solution)/shard_map/ppermute | solution.py:823
  26.4 4.5 %collective-permute-start.11 = (f32[16,128]{1,0:T(8,128)S(1)}, f32[16,128]{1,0:T(8,128)S(1)}, u32[]{:S(2)}, u32[]{:S(2)}) collective-permute-start(f32[16,128]{1,0:T(8,128)S(1)} %add.24), channel_id=1, source_target_pairs={{0,16},{2,18},{4,20},{6,22},{8,24},{10,26},{12,28},{14,30},{16,0},... | collective-permute-start | bytes 24584 | tf_op jit(solution)/shard_map/ppermute | solution.py:823
  26.4 4.5 %collective-permute-start.10 = (f32[16,128]{1,0:T(8,128)S(1)}, f32[16,128]{1,0:T(8,128)S(1)}, u32[]{:S(2)}, u32[]{:S(2)}) collective-permute-start(f32[16,128]{1,0:T(8,128)S(1)} %add.24), channel_id=1, source_target_pairs={{0,8},{2,10},{4,12},{6,14},{8,0},{10,2},{12,4},{14,6},{16,24},{18,... | collective-permute-start | bytes 24584 | tf_op jit(solution)/shard_map/ppermute | solution.py:823

commit v7 on v6

--- a/solution.py
+++ b/solution.py
@@ -828,7 +828,7 @@
     count = lax.axis_size(axis)
     while start < count:
         stop = min(4 * start, count)
-        value = flips(value, axis, range(start, stop, start))
+        value = flips(value, axis, [step * start for step in (1, 3, 2) if step * start < stop])
         start = stop
     return value
 

time: 31.8 us -> 31.7 us (level)
  starting transfers between devices: 18.8 us -> 17.9 us
  waiting for transfers between devices: 6.98 us -> 7.77 us
    ppermute x4, starting transfers between devices: 4.46 us -> 3.56 us  [flips(): lax.ppermute(value, axis, [(i, i ^ flip) for i in range(count)])]
    ppermute x4, waiting for transfers between devices: 2.05 us -> 2.83 us  [flips(): lax.ppermute(value, axis, [(i, i ^ flip) for i in range(count)])]
where the time goes in v7:
time: 31.7 us; the launch traced here: 31.5 us
  starting transfers between devices  17.9 us (56%)
  waiting for transfers between devices  7.77 us (25%)
  Pallas kernels  3.32 us (10%)
  local copies, waits for them, and re-layouts  1.13 us (4%)
  between operations  0.79 us (2%)
  other arithmetic  0.64 us (2%)
    ppermute x2, starting transfers between devices, swap_far(): lax.ppermute(far, 'gx', [(i, (i + 1 if i % 2 else i - 1) % count) for i i...  6.98 us
    ppermute x4, starting transfers between devices, flips(): lax.ppermute(value, axis, [(i, i ^ flip) for i in range(count)])  3.56 us
    pallas_call x11, Pallas kernels, call(): pl.pallas_call(kernel, out_shape=tuple((jax.ShapeDtypeStruct(shape, jnp.f...  3.32 us
    ppermute x2, starting transfers between devices, swap_rows(): return lax.ppermute(rows, 'gy', ring('gy', 1))  3.09 us
    ppermute x4, waiting for transfers between devices, flips(): lax.ppermute(value, axis, [(i, i ^ flip) for i in range(count)])  2.83 us
    ppermute x1, starting transfers between devices, last_exchange(): got = lax.ppermute(packed, 'gy', ring('gy', 1))  2.55 us
    ppermute x2, waiting for transfers between devices, swap_far(): lax.ppermute(far, 'gx', [(i, (i + 1 if i % 2 else i - 1) % count) for i i...  2.34 us
    ppermute x2, waiting for transfers between devices, swap_rows(): return lax.ppermute(rows, 'gy', ring('gy', 1))  2.28 us
  transfers between devices with their start and end apart: 13, of which 7 were waited for; matrix products, arithmetic and copies ran while one was open for 0% of the time, Pallas kernels for 8%

profile of v7, /device:TPU:0, one launch (start us, length us, event | category | flops | bytes accessed | tf_op | source)
XLA Modules:
  0.0 31.5 jit_solution(18031811067972454441)
XLA Ops:
  0.6 0.0 copy-start
  0.6 0.0 copy-start.3
  0.7 0.0 copy-start.2
  0.7 0.0 copy-start.1
  0.7 0.0 copy-start.4
  0.7 0.9 %copy-done = f32[19,4,8,128]{3,2,1,0:T(8,128)S(1)} copy-done((f32[19,4,8,128]{3,2,1,0:T(8,128)S(1)}, f32[19,4,8,128]{3,2,1,0:T(8,128)}, u32[]{:S(2)}) %copy-start) | copy-done | bytes 311320
  1.6 0.0 copy-done.3
  1.6 0.0 copy-done.2
  1.6 0.2 copy-done.1
  1.8 0.0 copy-done.4
  1.8 0.1 shard_map.69
  2.0 3.0 %collective-permute-start.2 = (f32[2,48,128]{2,1,0:T(8,128)S(1)}, f32[2,48,128]{2,1,0:T(8,128)S(1)}, u32[]{:S(2)}, u32[]{:S(2)}) collective-permute-start(f32[2,48,128]{2,1,0:T(8,128)S(1)} %get-tuple-element.22), channel_id=1, source_target_pairs={{0,1},{1,0},{2,3},{3,2},{4,5},{5,4},{6,7},{7,6},{8,9},{9,8},{10,11... | collective-permute-start | bytes 147464 | tf_op jit(solution)/shard_map/ppermute | solution.py:799
  5.0 0.7 %shard_map.70 = (f32[42,4,8,128]{3,2,1,0:T(8,128)S(1)}, f32[42,4,8,128]{3,2,1,0:T(8,128)S(1)}, f32[42,4,8,128]{3,2,1,0:T(8,128)S(1)}) custom-call(f32[16,128]{1,0:T(8,128)S(1)} %get-tuple-element.18.thrust_ref.refs_0_, s32[4,8,128]{2,1,0:T(8,128)S(1)} %copy-done.3, f32[3,4,8,128]{3,2,1,0:T(8,128)S(1)} %copy-done.2, bf16[3,19,4,8,128]{4,3,2,1,0:T(8,128)(2,1)S(1)} %copy-done.1), custom_call_target="tpu_custom_call" | custom-call | flops 800000 | bytes 1600000 | tf_op jit(solution)/shard_map/pallas_call | solution.py:779
  5.7 0.1 shard_map.71
  5.8 0.1 collective-permute-start
  5.9 1.2 %collective-permute-done.2.first_ref = f32[2,48,128]{2,1,0:T(8,128)S(1)} collective-permute-done((f32[2,48,128]{2,1,0:T(8,128)S(1)}, f32[2,48,128]{2,1,0:T(8,128)S(1)}, u32[]{:S(2)}, u32[]{:S(2)}) %collective-permute-start.2) | collective-permute-done | bytes 49184 | tf_op jit(solution)/shard_map/ppermute | solution.py:799
  7.1 0.2 shard_map.73
  7.3 3.4 %collective-permute-start.3 = (f32[38,8,128]{2,1,0:T(8,128)S(1)}, f32[38,8,128]{2,1,0:T(8,128)S(1)}, u32[]{:S(2)}, u32[]{:S(2)}) collective-permute-start(f32[38,8,128]{2,1,0:T(8,128)S(1)} %shard_map.73), channel_id=1, source_target_pairs={{0,30},{2,4},{4,2},{6,8},{8,6},{10,12},{12,10},{14,16},{16,14},{18... | collective-permute-start | bytes 466952 | tf_op jit(solution)/shard_map/ppermute | solution.py:816
  10.7 1.1 %collective-permute-done.rows_ref.refs_2_ = f32[2,168,128]{2,1,0:T(8,128)S(1)} collective-permute-done((f32[2,168,128]{2,1,0:T(8,128)S(1)}, f32[2,168,128]{2,1,0:T(8,128)S(1)}, u32[]{:S(2)}, u32[]{:S(2)}) %collective-permute-start) | collective-permute-done | bytes 172064 | tf_op jit(solution)/shard_map/ppermute | solution.py:799
  11.7 0.3 %shard_map.72 = (f32[38,8,128]{2,1,0:T(8,128)S(1)}, f32[2,21,8,128]{3,2,1,0:T(8,128)S(1)}, f32[2,5,8,128]{3,2,1,0:T(8,128)S(1)}) custom-call(f32[16,128]{1,0:T(8,128)S(1)} %get-tuple-element.18.thrust_ref.refs_0_, f32[19,4,8,128]{3,2,1,0:T(8,128)S(1)} %copy-done, f32[21,4,8,128]{3,2,1,0:T(8,128)S(1)} %get-tuple-element.19.fields_ref.refs_7_, ...), custom_call_target="tpu_custom_call" | custom-call | flops 400000 | bytes 800000 | tf_op jit(solution)/shard_map/pallas_call | solution.py:779
  12.0 0.1 collective-permute-start.1
  12.1 0.2 shard_map.74
  12.3 2.3 %collective-permute-done.3.refs_4_ = f32[38,8,128]{2,1,0:T(8,128)S(1)} collective-permute-done((f32[38,8,128]{2,1,0:T(8,128)S(1)}, f32[38,8,128]{2,1,0:T(8,128)S(1)}, u32[]{:S(2)}, u32[]{:S(2)}) %collective-permute-start.3) | collective-permute-done | bytes 155680 | tf_op jit(solution)/shard_map/ppermute | solution.py:816
  14.7 0.0 collective-permute-done.1.refs_3_
  14.7 0.7 %shard_map.75 = (f32[19,4,8,128]{3,2,1,0:T(8,128)S(1)}, f32[56,128]{1,0:T(8,128)S(1)}) custom-call(f32[16,128]{1,0:T(8,128)S(1)} %get-tuple-element.18.thrust_ref.refs_0_, f32[19,4,8,128]{3,2,1,0:T(8,128)S(1)} %copy-done, f32[2,168,128]{2,1,0:T(8,128)S(1)} %collective-permute-done.rows_ref.refs_2_, f32[38,8,128]{2,1,0:T(8,128)S(1)} %collective-permute-done.1.refs_3_, ...), custom_call_target="tpu_custom_call" | custom-call | flops 800000 | bytes 1600000 | tf_op jit(solution)/shard_map/pallas_call | solution.py:779
  15.4 2.5 %collective-permute-start.4 = (f32[56,128]{1,0:T(8,128)S(1)}, f32[56,128]{1,0:T(8,128)S(1)}, u32[]{:S(2)}, u32[]{:S(2)}) collective-permute-start(f32[56,128]{1,0:T(8,128)S(1)} %get-tuple-element.29), channel_id=1, source_target_pairs={{0,1},{1,0},{2,3},{3,2},{4,5},{5,4},{6,7},{7,6},{8,9},{9,8},{10,11... | collective-permute-start | bytes 86024 | tf_op jit(solution)/shard_map/ppermute | solution.py:844
  17.9 0.0 collective-permute-start.8
  18.0 1.5 %collective-permute-start.7 = (f32[16,128]{1,0:T(8,128)S(1)}, f32[16,128]{1,0:T(8,128)S(1)}, u32[]{:S(2)}, u32[]{:S(2)}) collective-permute-start(f32[16,128]{1,0:T(8,128)S(1)} %slice.13), channel_id=1, source_target_pairs={{0,4},{2,6},{4,0},{6,2},{8,12},{10,14},{12,8},{14,10},{16,20},{18,... | collective-permute-start | bytes 24584 | tf_op jit(solution)/shard_map/ppermute | solution.py:846
  19.5 0.3 collective-permute-done.4
  19.8 0.1 collective-permute-start.5
  19.9 3.6 %collective-permute-start.6 = (f32[6,8,128]{2,1,0:T(8,128)S(1)}, f32[6,8,128]{2,1,0:T(8,128)S(1)}, u32[]{:S(2)}, u32[]{:S(2)}) collective-permute-start(f32[6,8,128]{2,1,0:T(8,128)S(1)} %get-tuple-element.31), channel_id=1, source_target_pairs={{0,30},{2,4},{4,2},{6,8},{8,6},{10,12},{12,10},{14,16},{16,14},{18... | collective-permute-start | bytes 73736 | tf_op jit(solution)/shard_map/ppermute | solution.py:816
  23.5 0.0 collective-permute-done.8
  23.5 0.0 collective-permute-done.7
  23.5 0.0 collective-permute-done.5.near_ref._
  23.5 0.1 collective-permute-start.9
  23.6 1.2 %collective-permute-done.9 = f32[16,128]{1,0:T(8,128)S(1)} collective-permute-done((f32[16,128]{1,0:T(8,128)S(1)}, f32[16,128]{1,0:T(8,128)S(1)}, u32[]{:S(2)}, u32[]{:S(2)}) %collective-permute-start.9) | collective-permute-done | bytes 8224 | tf_op jit(solution)/shard_map/ppermute | solution.py:823
  24.8 0.7 %collective-permute-start.12 = (f32[16,128]{1,0:T(8,128)S(1)}, f32[16,128]{1,0:T(8,128)S(1)}, u32[]{:S(2)}, u32[]{:S(2)}) collective-permute-start(f32[16,128]{1,0:T(8,128)S(1)} %add.24), channel_id=1, source_target_pairs={{0,16},{2,18},{4,20},{6,22},{8,24},{10,26},{12,28},{14,30},{16,0},... | collective-permute-start | bytes 24584 | tf_op jit(solution)/shard_map/ppermute | solution.py:823
  25.4 1.3 %collective-permute-start.11 = (f32[16,128]{1,0:T(8,128)S(1)}, f32[16,128]{1,0:T(8,128)S(1)}, u32[]{:S(2)}, u32[]{:S(2)}) collective-permute-start(f32[16,128]{1,0:T(8,128)S(1)} %add.24), channel_id=1, source_target_pairs={{0,24},{2,26},{4,28},{6,30},{8,16},{10,18},{12,20},{14,22},{16,8},... | collective-permute-start | bytes 24584 | tf_op jit(solution)/shard_map/ppermute | solution.py:823
  26.8 1.5 %collective-permute-start.10 = (f32[16,128]{1,0:T(8,128)S(1)}, f32[16,128]{1,0:T(8,128)S(1)}, u32[]{:S(2)}, u32[]{:S(2)}) collective-permute-start(f32[16,128]{1,0:T(8,128)S(1)} %add.24), channel_id=1, source_target_pairs={{0,8},{2,10},{4,12},{6,14},{8,0},{10,2},{12,4},{14,6},{16,24},{18,... | collective-permute-start | bytes 24584 | tf_op jit(solution)/shard_map/ppermute | solution.py:823
  28.3 0.0 collective-permute-done.6.far_ref
  28.3 0.9 %shard_map.77 = f32[19,4,8,128]{3,2,1,0:T(8,128)} custom-call(f32[19,4,8,128]{3,2,1,0:T(8,128)S(1)} %get-tuple-element.28.lam_ref, f32[40,128]{1,0:T(8,128)S(1)} %slice.16.rows_ref, f32[5,8,128]{2,1,0:T(8,128)S(1)} %collective-permute-done.5.near_ref._, f32[6,8,128]{2,1,0:T(8,128)S(1)} %collective-permute-done.6.far_ref, ...), custom_call_target="tpu_custom_call" | custom-call | flops 500000 | bytes 1000000 | tf_op jit(solution)/shard_map/pallas_call | solution.py:779
  29.2 0.1 collective-permute-done.12
  29.3 1.6 %collective-permute-done.11 = f32[16,128]{1,0:T(8,128)S(1)} collective-permute-done((f32[16,128]{1,0:T(8,128)S(1)}, f32[16,128]{1,0:T(8,128)S(1)}, u32[]{:S(2)}, u32[]{:S(2)}) %collective-permute-start.11) | collective-permute-done | bytes 8224 | tf_op jit(solution)/shard_map/ppermute | solution.py:823
  30.9 0.0 collective-permute-done.10
  30.9 0.6 %fusion = f32[10]{0:T(128)} fusion(f32[16,128]{1,0:T(8,128)S(1)} %get-tuple-element.33, f32[16,128]{1,0:T(8,128)S(1)} %collective-permute-done.12, f32[16,128]{1,0:T(8,128)S(1)} %collective-permute-done.11, f32[16,128]{1,0:T(8,128)S(1)} %collective-permute-done.10, f32[16,128]{1,0:T(8,128)S(1)} %add.24), kind=kLoop, calls=%fused_computation.1 | loop fusion | flops 6390 | bytes 25640 | tf_op jit(solution)/shard_map/reduce_sum | solution.py:977
  (7 shorter events, 0.0 us)
Async XLA Ops:
  0.6 1.0 %copy-start = (f32[19,4,8,128]{3,2,1,0:T(8,128)S(1)}, f32[19,4,8,128]{3,2,1,0:T(8,128)}, u32[]{:S(2)}) copy-start(f32[19,4,8,128]{3,2,1,0:T(8,128)} %refs_1_.1) | copy-start | bytes 933892
  0.6 1.0 %copy-start.3 = (s32[4,8,128]{2,1,0:T(8,128)S(1)}, s32[4,8,128]{2,1,0:T(8,128)}, u32[]{:S(2)}) copy-start(s32[4,8,128]{2,1,0:T(8,128)} %map_ref.3) | copy-start | bytes 49156
  0.7 1.0 %copy-start.2 = (f32[3,4,8,128]{3,2,1,0:T(8,128)S(1)}, f32[3,4,8,128]{3,2,1,0:T(8,128)}, u32[]{:S(2)}) copy-start(f32[3,4,8,128]{3,2,1,0:T(8,128)} %scale_ref.3) | copy-start | bytes 147460
  0.7 1.1 %copy-start.1 = (bf16[3,19,4,8,128]{4,3,2,1,0:T(8,128)(2,1)S(1)}, bf16[3,19,4,8,128]{4,3,2,1,0:T(8,128)(2,1)}, u32[]{:S(2)}) copy-start(bf16[3,19,4,8,128]{4,3,2,1,0:T(8,128)(2,1)} %pops_ref.3) | copy-start | bytes 1400836
  0.7 1.1 %copy-start.4 = (f32[10]{0:T(128)S(1)}, f32[10]{0:T(128)}, u32[]{:S(2)}) copy-start(f32[10]{0:T(128)} %param.9) | copy-start | bytes 124
  2.0 5.1 %collective-permute-start.2 = (f32[2,48,128]{2,1,0:T(8,128)S(1)}, f32[2,48,128]{2,1,0:T(8,128)S(1)}, u32[]{:S(2)}, u32[]{:S(2)}) collective-permute-start(f32[2,48,128]{2,1,0:T(8,128)S(1)} %get-tuple-element.22), channel_id=1, source_target_pairs={{0,1},{1,0},{2,3},{3,2},{4,5},{5,4},{6,7},{7,6},{8,9},{9,8},{10,11... | collective-permute-start | bytes 147464 | tf_op jit(solution)/shard_map/ppermute | solution.py:799
  5.8 5.9 %collective-permute-start = (f32[2,168,128]{2,1,0:T(8,128)S(1)}, f32[2,168,128]{2,1,0:T(8,128)S(1)}, u32[]{:S(2)}, u32[]{:S(2)}) collective-permute-start(f32[2,168,128]{2,1,0:T(8,128)S(1)} %shard_map.71), channel_id=1, source_target_pairs={{0,1},{1,0},{2,3},{3,2},{4,5},{5,4},{6,7},{7,6},{8,9},{9,8},{10,11... | collective-permute-start | bytes 516104 | tf_op jit(solution)/shard_map/ppermute | solution.py:799
  7.3 7.4 %collective-permute-start.3 = (f32[38,8,128]{2,1,0:T(8,128)S(1)}, f32[38,8,128]{2,1,0:T(8,128)S(1)}, u32[]{:S(2)}, u32[]{:S(2)}) collective-permute-start(f32[38,8,128]{2,1,0:T(8,128)S(1)} %shard_map.73), channel_id=1, source_target_pairs={{0,30},{2,4},{4,2},{6,8},{8,6},{10,12},{12,10},{14,16},{16,14},{18... | collective-permute-start | bytes 466952 | tf_op jit(solution)/shard_map/ppermute | solution.py:816
  12.0 2.6 %collective-permute-start.1 = (f32[38,8,128]{2,1,0:T(8,128)S(1)}, f32[38,8,128]{2,1,0:T(8,128)S(1)}, u32[]{:S(2)}, u32[]{:S(2)}) collective-permute-start(f32[38,8,128]{2,1,0:T(8,128)S(1)} %get-tuple-element.21), channel_id=1, source_target_pairs={{0,2},{2,0},{4,6},{6,4},{8,10},{10,8},{12,14},{14,12},{16,18},{18,... | collective-permute-start | bytes 466952 | tf_op jit(solution)/shard_map/ppermute | solution.py:811
  15.4 4.4 %collective-permute-start.4 = (f32[56,128]{1,0:T(8,128)S(1)}, f32[56,128]{1,0:T(8,128)S(1)}, u32[]{:S(2)}, u32[]{:S(2)}) collective-permute-start(f32[56,128]{1,0:T(8,128)S(1)} %get-tuple-element.29), channel_id=1, source_target_pairs={{0,1},{1,0},{2,3},{3,2},{4,5},{5,4},{6,7},{7,6},{8,9},{9,8},{10,11... | collective-permute-start | bytes 86024 | tf_op jit(solution)/shard_map/ppermute | solution.py:844
  17.9 5.5 %collective-permute-start.8 = (f32[16,128]{1,0:T(8,128)S(1)}, f32[16,128]{1,0:T(8,128)S(1)}, u32[]{:S(2)}, u32[]{:S(2)}) collective-permute-start(f32[16,128]{1,0:T(8,128)S(1)} %slice.13), channel_id=1, source_target_pairs={{0,5},{1,4},{2,7},{3,6},{4,1},{5,0},{6,3},{7,2},{8,13},{9,12},{10,... | collective-permute-start | bytes 24584 | tf_op jit(solution)/shard_map/ppermute | solution.py:847
  18.0 5.5 %collective-permute-start.7 = (f32[16,128]{1,0:T(8,128)S(1)}, f32[16,128]{1,0:T(8,128)S(1)}, u32[]{:S(2)}, u32[]{:S(2)}) collective-permute-start(f32[16,128]{1,0:T(8,128)S(1)} %slice.13), channel_id=1, source_target_pairs={{0,4},{2,6},{4,0},{6,2},{8,12},{10,14},{12,8},{14,10},{16,20},{18,... | collective-permute-start | bytes 24584 | tf_op jit(solution)/shard_map/ppermute | solution.py:846
  19.8 3.7 %collective-permute-start.5 = (f32[5,8,128]{2,1,0:T(8,128)S(1)}, f32[5,8,128]{2,1,0:T(8,128)S(1)}, u32[]{:S(2)}, u32[]{:S(2)}) collective-permute-start(f32[5,8,128]{2,1,0:T(8,128)S(1)} %get-tuple-element.30), channel_id=1, source_target_pairs={{0,2},{2,0},{4,6},{6,4},{8,10},{10,8},{12,14},{14,12},{16,18},{18,... | collective-permute-start | bytes 61448 | tf_op jit(solution)/shard_map/ppermute | solution.py:811
  19.9 8.4 %collective-permute-start.6 = (f32[6,8,128]{2,1,0:T(8,128)S(1)}, f32[6,8,128]{2,1,0:T(8,128)S(1)}, u32[]{:S(2)}, u32[]{:S(2)}) collective-permute-start(f32[6,8,128]{2,1,0:T(8,128)S(1)} %get-tuple-element.31), channel_id=1, source_target_pairs={{0,30},{2,4},{4,2},{6,8},{8,6},{10,12},{12,10},{14,16},{16,14},{18... | collective-permute-start | bytes 73736 | tf_op jit(solution)/shard_map/ppermute | solution.py:816
  23.5 1.2 %collective-permute-start.9 = (f32[16,128]{1,0:T(8,128)S(1)}, f32[16,128]{1,0:T(8,128)S(1)}, u32[]{:S(2)}, u32[]{:S(2)}) collective-permute-start(f32[16,128]{1,0:T(8,128)S(1)} %shard_map.78), channel_id=1, source_target_pairs={{0,2},{2,0},{4,6},{6,4},{8,10},{10,8},{12,14},{14,12},{16,18},{18,... | collective-permute-start | bytes 24584 | tf_op jit(solution)/shard_map/ppermute | solution.py:823
  24.8 4.5 %collective-permute-start.12 = (f32[16,128]{1,0:T(8,128)S(1)}, f32[16,128]{1,0:T(8,128)S(1)}, u32[]{:S(2)}, u32[]{:S(2)}) collective-permute-start(f32[16,128]{1,0:T(8,128)S(1)} %add.24), channel_id=1, source_target_pairs={{0,16},{2,18},{4,20},{6,22},{8,24},{10,26},{12,28},{14,30},{16,0},... | collective-permute-start | bytes 24584 | tf_op jit(solution)/shard_map/ppermute | solution.py:823
  25.4 5.4 %collective-permute-start.11 = (f32[16,128]{1,0:T(8,128)S(1)}, f32[16,128]{1,0:T(8,128)S(1)}, u32[]{:S(2)}, u32[]{:S(2)}) collective-permute-start(f32[16,128]{1,0:T(8,128)S(1)} %add.24), channel_id=1, source_target_pairs={{0,24},{2,26},{4,28},{6,30},{8,16},{10,18},{12,20},{14,22},{16,8},... | collective-permute-start | bytes 24584 | tf_op jit(solution)/shard_map/ppermute | solution.py:823
  26.8 4.1 %collective-permute-start.10 = (f32[16,128]{1,0:T(8,128)S(1)}, f32[16,128]{1,0:T(8,128)S(1)}, u32[]{:S(2)}, u32[]{:S(2)}) collective-permute-start(f32[16,128]{1,0:T(8,128)S(1)} %add.24), channel_id=1, source_target_pairs={{0,8},{2,10},{4,12},{6,14},{8,0},{10,2},{12,4},{14,6},{16,24},{18,... | collective-permute-start | bytes 24584 | tf_op jit(solution)/shard_map/ppermute | solution.py:823
